TPU v7x, 512 devices: a whole 4x8x8 slice. The times are simulated.
512 devices in a mesh: dp: 64 (over z, y_lo, core), mp: 8 (over y_hi, x).
Axes of the slice: x: 4, y: 8 (y_hi: 2, y_lo: 4; y = y_hi * 4 + y_lo), z: 8, core: 2. Of those that a mesh axis runs over, the one named last changes fastest.
Arguments:
- acts: bfloat16 [32768, 12288], P('dp', 'mp'), may hold values from -8 to 8
- lengths: int32 [128], P('dp'), may hold values from 1 to 256, as said below
- ln_gain: float32 [12288], P('mp'), may hold values from 0.1 to 1.9
- ln_bias: float32 [12288], P('mp'), may hold values from -3 to 3
- w_fc1: bfloat16 [12288, 24576], P('dp', 'mp'), may hold values from -0.0546875 to 0.0546875
Outputs:
- w_served: bfloat16 [24576, 12288], P(('mp', 'dp'))
- scales: float32 [12288], P('mp')
- tok_scale: float32 [32768], P('dp')
Inputs may be any that keep to these rules, and one draw needn't show every extreme that they name: `lengths`: in every draw some sequence has all 256 positions valid and some has one.
All inputs are finite; a program needn't handle non-finite values. Where the computation divides by a largest or mean magnitude, that divisor is 1e-20 or more.
Results may differ from a plain program's by a relative error of at most 0.0004.
Values may be sent and summed in bfloat16 or wider, within the bound.
No kernel may reach another device: no remote copies, remote signals or barrier semaphores. Data moves between devices by JAX's collectives and lax.ppermute only.
A program may use at most 64 MiB of HBM per device.

v0:
```python
import jax
import jax.numpy as jnp
from jax import lax
from jax.sharding import PartitionSpec as P

D = 12288


def body(acts, lengths, ln_gain, ln_bias, w_fc1):
    x = acts.astype(jnp.float32)
    moments = lax.psum((jnp.sum(x, axis=1), jnp.sum(x * x, axis=1)), "mp")
    mean = moments[0] / D
    var = moments[1] / D - mean * mean
    normed = (x - mean[:, None]) * lax.rsqrt(var + 1e-05)[:, None] * ln_gain + ln_bias
    seq_count = lengths.shape[0]
    slot_len = acts.shape[0] // seq_count
    positions = lax.broadcasted_iota(jnp.int32, (seq_count, slot_len), 1)
    valid = (positions < lengths[:, None]).reshape(acts.shape[0])
    act_local = jnp.max(jnp.where(valid[:, None], jnp.abs(normed), 0.0), axis=0)
    w_local = jnp.max(jnp.abs(w_fc1.astype(jnp.float32)), axis=1)
    feat_block = acts.shape[1]
    row_block = w_fc1.shape[0]
    mp_place = lax.axis_index("mp")
    dp_place = lax.axis_index("dp")
    act_block = lax.pmax(act_local, "dp")
    act_full = lax.all_gather(act_block, "mp", axis=0, tiled=True)
    w_rows = lax.pmax(w_local, "mp")
    w_full = lax.all_gather(w_rows, "dp", axis=0, tiled=True)
    scale_full = jnp.sqrt(act_full + 1e-05) / jnp.sqrt(w_full + 1e-05)
    scale_block = lax.dynamic_slice_in_dim(scale_full, mp_place * feat_block, feat_block, 0)
    peaks = jnp.max(jnp.abs(normed / scale_block), axis=1)
    peaks = lax.pmax(peaks, "mp")
    tok_scale = jnp.where(valid, peaks, 0.0)
    row_scales = lax.dynamic_slice_in_dim(scale_full, dp_place * row_block, row_block, 0)
    smoothed = (w_fc1.astype(jnp.float32) * row_scales[:, None]).astype(jnp.bfloat16).T
    w_served = lax.all_to_all(smoothed, "dp", split_axis=0, concat_axis=1, tiled=True)
    return (w_served, scale_block, tok_scale)


def solution(mesh):
    return jax.shard_map(
        body,
        mesh=mesh,
        in_specs=(P("dp", "mp"), P("dp"), P("mp"), P("mp"), P("dp", "mp")),
        out_specs=(P(("mp", "dp"), None), P("mp"), P("dp")),
        check_vma=False,
    )
```

profile of v0, /device:TPU:1, one launch (start us, length us, event | category | flops | bytes accessed | tf_op | source)
XLA Modules:
  0.0 570.9 jit_solution(6404457706409665014)
XLA Ops:
  0.6 0.0 copy-start
  0.6 0.0 copy-start.1
  0.7 0.0 copy-start.2
  0.7 0.8 iota_compare_fusion
  1.5 2.0 convert_reduce_fusion
  3.5 28.9 %all-reduce.1 = (f32[512]{0:T(512)S(1)}, f32[512]{0:T(512)S(1)}) all-reduce(f32[512]{0:T(512)S(1)} %get-tuple-element.4, f32[512]{0:T(512)S(1)} %get-tuple-element.3), channel_id=1, replica_groups=mesh['dp'=64,'mp'=8] {'mp'}, use_global_device_ids=true, to_apply=%region_3.0 | all-reduce | flops 1024 | bytes 8192 | tf_op jit(solution)/shard_map/psum | solution.py:11
  32.4 0.0 copy-done
  32.4 0.0 copy-done.1
  32.4 0.0 copy-done.2
  32.4 0.9 fusion.9
  33.3 143.2 %pmax.21 = f32[1536]{0:T(1024)S(1)} all-reduce(f32[1536]{0:T(1024)S(1)} %fusion.9), channel_id=1, replica_groups=mesh['dp'=64,'mp'=8] {'dp'}, use_global_device_ids=true, to_apply=%region_5.6 | all-reduce | flops 1536 | bytes 12288 | tf_op jit(solution)/shard_map/pmax | solution.py:25
  176.6 37.6 %all-gather = f32[8,1,1536]{2,1,0:T(1,128)S(1)} all-gather(f32[1,1,1536]{2,1,0:T(1,128)S(1)} %reshape.36), channel_id=1, replica_groups=mesh['dp'=64,'mp'=8] {'mp'}, dimensions={0}, use_global_device_ids=true | all-gather | bytes 55296 | tf_op jit(solution)/shard_map/all_gather | solution.py:26
  214.2 0.1 add_sqrt_fusion
  214.3 1.6 copy.12
  215.9 0.5 fusion
  216.4 20.3 %pmax.22 = f32[192]{0:T(256)S(1)} all-reduce(f32[192]{0:T(256)S(1)} %fusion), channel_id=1, replica_groups=mesh['dp'=64,'mp'=8] {'mp'}, use_global_device_ids=true, to_apply=%region_7.8 | all-reduce | flops 192 | bytes 1536 | tf_op jit(solution)/shard_map/pmax | solution.py:27
  236.7 1.3 dynamic-slice
  238.6 0.3 dynamic-update-slice
  238.9 270.4 %all-reduce = f32[12288]{0:T(1024)S(1)} all-reduce(f32[12288]{0:T(1024)S(1)} %dynamic-update-slice), channel_id=1, replica_groups=mesh['dp'=64,'mp'=8] {'dp'}, use_global_device_ids=true, to_apply=%add | all-reduce | flops 12288 | bytes 98304
  509.3 0.1 dynamic_slice.6
  509.4 1.5 fusion.1
  510.9 12.1 %all-to-all-start = ((bf16[64,48,192]{2,1,0:T(8,128)(2,1)}), bf16[64,48,192]{2,1,0:T(8,128)(2,1)S(1)}, u32[]{:S(2)}, u32[]{:S(2)}) async-start(bf16[64,48,192]{2,1,0:T(8,128)(2,1)} %bitcast.7), calls=%async_computation | async-start | bytes 3145728 | tf_op jit(solution)/shard_map/all_to_all | solution.py:36
  523.0 0.1 dynamic_slice.7
  523.1 0.0 copy-start.3
  523.1 1.0 fusion.11
  524.2 43.1 %pmax.23 = f32[512]{0:T(512)S(1)} all-reduce(f32[512]{0:T(512)S(1)} %fusion.11), channel_id=1, replica_groups=mesh['dp'=64,'mp'=8] {'mp'}, use_global_device_ids=true, to_apply=%region_9.10 | all-reduce | flops 512 | bytes 4096 | tf_op jit(solution)/shard_map/pmax | solution.py:32
  567.3 0.6 broadcast_select_fusion
  567.8 0.0 all-to-all-done
  567.8 0.5 copy.13
  568.4 0.0 copy-done.3
  568.4 2.5 all_to_all.17
  (5 shorter events, 0.1 us)
Async XLA Ops:
  0.6 31.8 %copy-start = (bf16[512,1536]{1,0:T(8,128)(2,1)S(1)}, bf16[512,1536]{1,0:T(8,128)(2,1)}, u32[]{:S(2)}) copy-start(bf16[512,1536]{1,0:T(8,128)(2,1)} %param.5) | copy-start | bytes 4718596
  0.6 31.7 %copy-start.1 = (f32[1536]{0:T(1024)S(1)}, f32[1536]{0:T(1024)}, u32[]{:S(2)}) copy-start(f32[1536]{0:T(1024)} %param.8) | copy-start | bytes 18436
  0.7 31.7 %copy-start.2 = (f32[1536]{0:T(1024)S(1)}, f32[1536]{0:T(1024)}, u32[]{:S(2)}) copy-start(f32[1536]{0:T(1024)} %param.7) | copy-start | bytes 18436
  510.9 56.9 %all-to-all-start = ((bf16[64,48,192]{2,1,0:T(8,128)(2,1)}), bf16[64,48,192]{2,1,0:T(8,128)(2,1)S(1)}, u32[]{:S(2)}, u32[]{:S(2)}) async-start(bf16[64,48,192]{2,1,0:T(8,128)(2,1)} %bitcast.7), calls=%async_computation | async-start | bytes 3145728 | tf_op jit(solution)/shard_map/all_to_all | solution.py:36
  523.1 45.3 %copy-start.3 = (f32[1536]{0:T(1024)}, f32[1536]{0:T(1024)S(1)}, u32[]{:S(2)}) copy-start(f32[1536]{0:T(1024)S(1)} %dynamic_slice.7) | copy-start | bytes 18436
where the time goes:
time: 573 us; the launch traced here: 571 us
  blocking collectives  543 us (95%)
  starting transfers between devices  12.1 us (2%)
  other arithmetic  7.48 us (1%)
  local copies, waits for them, and re-layouts  6.45 us (1%)
    unnamed x1, blocking collectives  270 us
    pmax x1, blocking collectives, body(): act_block = lax.pmax(act_local, 'dp')  143 us
    pmax x1, blocking collectives, body(): peaks = lax.pmax(peaks, 'mp')  43.1 us
    all_gather x1, blocking collectives, body(): act_full = lax.all_gather(act_block, 'mp', axis=0, tiled=True)  37.6 us
    psum x1, blocking collectives, body(): moments = lax.psum((jnp.sum(x, axis=1), jnp.sum(x * x, axis=1)), 'mp')  28.9 us
    pmax x1, blocking collectives, body(): w_rows = lax.pmax(w_local, 'mp')  20.3 us
    all_to_all x1, starting transfers between devices, body(): lax.all_to_all(smoothed, 'dp', split_axis=0, concat_axis=1, tiled=True)  12.1 us
  transfers between devices with their start and end apart: 1, of which 0 were waited for; matrix products, arithmetic and copies ran while one was open for 0% of the time, Pallas kernels for 0%

commit v1 on v0

v1 whole, which is shorter than its diff:
```python
import jax
import jax.numpy as jnp
from jax import lax
from jax.experimental import pallas as pl
from jax.experimental.pallas import tpu as pltpu
from jax.sharding import PartitionSpec as P

D = 12288
SLOT = 256
EPS = 1e-05
VMEM_SPEC = pl.BlockSpec(memory_space=pltpu.VMEM)
SMEM_SPEC = pl.BlockSpec(memory_space=pltpu.SMEM)


def params():
    return pltpu.CompilerParams(vmem_limit_bytes=40 * 1024 * 1024)


def stats_kernel(place_ref, acts_ref, w_ref, page_ref, rows_ref):
    parity = place_ref[0] % 2
    for block in range(4):
        total = jnp.zeros((128, 128), jnp.float32)
        square = jnp.zeros((128, 128), jnp.float32)
        for tile in range(12):
            x = acts_ref[pl.ds(128 * block, 128), pl.ds(128 * tile, 128)].astype(jnp.float32)
            total = total + x
            square = square + x * x
        page_ref[0, block : block + 1, :] = jnp.sum(total.T, axis=0, keepdims=True)
        page_ref[0, 4 + block : 5 + block, :] = jnp.sum(square.T, axis=0, keepdims=True)
    rows_ref[...] = jnp.zeros_like(rows_ref)
    for part in range(2):
        peak = jnp.zeros((96, 128), jnp.float32)
        for tile in range(24):
            peak = jnp.maximum(peak, jnp.abs(w_ref[pl.ds(96 * part, 96), pl.ds(128 * tile, 128)].astype(jnp.float32)))
        rows_ref[pl.ds(pl.multiple_of(192 * parity + 96 * part, 32), 96), :] = peak
    for block in range(3):
        page_ref[0, 8 + block : 9 + block, :] = jnp.max(rows_ref[pl.ds(128 * block, 128), :].T, axis=0, keepdims=True)
    page_ref[0, 11:16, :] = jnp.zeros((5, 128), jnp.float32)
    page = page_ref[0]
    for peer in range(1, page_ref.shape[0]):
        page_ref[peer] = page


def pack_kernel(place_ref, w_ref, page_ref):
    parity = place_ref[0] % 2
    low = lax.broadcasted_iota(jnp.int32, (24, 128), 1) < 64
    first = low == (parity == 0)

    def step(index, carry):
        columns = pl.ds(pl.multiple_of(384 * index, 128), 384)
        full = w_ref[pl.ds(pl.multiple_of(64 * parity, 64), 128), columns].astype(jnp.float32).T
        half = w_ref[pl.ds(pl.multiple_of(128 * (1 - parity), 64), 64), columns].astype(jnp.float32)
        twice = jnp.concatenate([half, half], axis=0).T
        for peer in range(8):
            upper = twice[48 * peer : 48 * peer + 24]
            lower = twice[48 * peer + 24 : 48 * peer + 48]
            page = jnp.concatenate([full[48 * peer : 48 * peer + 48], jnp.where(first, upper, lower)], axis=0)
            page_ref[8 * index + peer] = page.astype(jnp.bfloat16)
        return carry

    lax.fori_loop(0, 8, step, 0)


def moments(sums):
    total = jnp.sum(sums[:, 0:8], axis=0)
    mean = total[0:4] / D
    var = total[4:8] / D - mean * mean
    rstd = lax.rsqrt(var + EPS)
    return jnp.concatenate([mean, rstd], axis=0).T


def act_kernel(lengths_ref, sums_ref, acts_ref, gain_ref, bias_ref, page_ref):
    columns = moments(sums_ref[...])
    place = lax.broadcasted_iota(jnp.int32, (128, 1), 0)
    for tile in range(12):
        gain = gain_ref[tile : tile + 1, :]
        bias = bias_ref[tile : tile + 1, :]
        peak = jnp.zeros((128, 128), jnp.float32)
        for block in range(4):
            x = acts_ref[pl.ds(128 * block, 128), pl.ds(128 * tile, 128)].astype(jnp.float32)
            normed = (x - columns[:, block : block + 1]) * columns[:, 4 + block : 5 + block] * gain + bias
            valid = place + 128 * (block % 2) < lengths_ref[block // 2]
            peak = jnp.maximum(peak, jnp.where(valid, jnp.abs(normed), 0.0))
        page_ref[0, tile : tile + 1, :] = jnp.max(peak, axis=0, keepdims=True)
    page_ref[0, 12:15, :] = jnp.max(sums_ref[:, 8:11, :], axis=0)
    page_ref[0, 15:16, :] = jnp.zeros((1, 128), jnp.float32)
    page = page_ref[0]
    for peer in range(1, page_ref.shape[0]):
        page_ref[peer] = page


def peak_kernel(place_ref, maxima_ref, sums_ref, acts_ref, gain_ref, bias_ref, page_ref):
    columns = moments(sums_ref[...])
    act = jnp.max(maxima_ref[:, 0:12, :], axis=0)
    start = 8 * place_ref[1]
    for pair in range(4):
        both = jnp.maximum(maxima_ref[start + 2 * pair, 12:15, :], maxima_ref[start + 2 * pair + 1, 12:15, :])
        page_ref[0, 3 * pair : 3 * pair + 3, :] = both
    scale = jnp.sqrt(act + EPS) / jnp.sqrt(page_ref[0, 0:12, :] + EPS)
    page_ref[0, 0:12, :] = scale
    inverse = 1.0 / scale
    for block in range(4):
        peak = jnp.zeros((128, 128), jnp.float32)
        for tile in range(12):
            x = acts_ref[pl.ds(128 * block, 128), pl.ds(128 * tile, 128)].astype(jnp.float32)
            gain = gain_ref[tile : tile + 1, :]
            bias = bias_ref[tile : tile + 1, :]
            normed = (x - columns[:, block : block + 1]) * columns[:, 4 + block : 5 + block] * gain + bias
            peak = jnp.maximum(peak, jnp.abs(normed) * inverse[tile : tile + 1])
        page_ref[0, 12 + block : 13 + block, :] = jnp.max(peak.T, axis=0, keepdims=True)
    page = page_ref[0]
    for peer in range(1, page_ref.shape[0]):
        page_ref[peer] = page


def serve_kernel(place_ref, lengths_ref, blocks_ref, pages_ref, served_ref, scale_ref, tok_ref):
    scale_ref[...] = blocks_ref[place_ref[1], 0:12, :]
    peaks = jnp.max(blocks_ref[:, 12:16, :], axis=0)
    lane = lax.broadcasted_iota(jnp.int32, (1, 128), 1)
    for block in range(4):
        valid = lane + 128 * (block % 2) < lengths_ref[block // 2]
        tok_ref[block : block + 1, :] = jnp.where(valid, peaks[block : block + 1], 0.0)
    low = lax.broadcasted_iota(jnp.int32, (24, 128), 1) < 64
    for pair in range(32):
        even = pages_ref[2 * pair].astype(jnp.float32)
        odd = pages_ref[2 * pair + 1].astype(jnp.float32)
        upper = jnp.where(low, even[48:72], odd[48:72])
        lower = pltpu.roll(jnp.where(low, odd[48:72], even[48:72]), 64, 1)
        middle = jnp.concatenate([upper, lower], axis=0)
        for part, tile in enumerate((even[0:48], middle, odd[0:48])):
            row = 3 * pair + part
            scale = blocks_ref[row // 12, row % 12 : row % 12 + 1, :]
            served_ref[:, pl.ds(128 * row, 128)] = (tile * scale).astype(jnp.bfloat16)


def body(acts, lengths, ln_gain, ln_bias, w_fc1):
    place = jnp.stack([lax.axis_index("dp"), lax.axis_index("mp")]).astype(jnp.int32)
    gain = ln_gain.reshape(12, 128)
    bias = ln_bias.reshape(12, 128)
    with jax.named_scope("token_moments"):
        page = pl.pallas_call(
            stats_kernel,
            out_shape=jax.ShapeDtypeStruct((8, 16, 128), jnp.float32),
            in_specs=[SMEM_SPEC, VMEM_SPEC, VMEM_SPEC],
            out_specs=VMEM_SPEC,
            scratch_shapes=[pltpu.VMEM((384, 128), jnp.float32)],
            compiler_params=params(),
        )(place, acts, w_fc1)
        sums = lax.all_to_all(page, "mp", 0, 0, tiled=True)
    with jax.named_scope("weight_exchange"):
        packed = pl.pallas_call(
            pack_kernel,
            out_shape=jax.ShapeDtypeStruct((64, 72, 128), jnp.bfloat16),
            in_specs=[SMEM_SPEC, VMEM_SPEC],
            out_specs=VMEM_SPEC,
            compiler_params=params(),
        )(place, w_fc1)
        pages = lax.all_to_all(packed, "dp", 0, 0, tiled=True)
    with jax.named_scope("channel_maxima"):
        page = pl.pallas_call(
            act_kernel,
            out_shape=jax.ShapeDtypeStruct((64, 16, 128), jnp.float32),
            in_specs=[SMEM_SPEC] + [VMEM_SPEC] * 4,
            out_specs=VMEM_SPEC,
            compiler_params=params(),
        )(lengths, sums, acts, gain, bias)
        maxima = lax.all_to_all(page, "dp", 0, 0, tiled=True)
    with jax.named_scope("token_peaks"):
        page = pl.pallas_call(
            peak_kernel,
            out_shape=jax.ShapeDtypeStruct((8, 16, 128), jnp.float32),
            in_specs=[SMEM_SPEC] + [VMEM_SPEC] * 5,
            out_specs=VMEM_SPEC,
            compiler_params=params(),
        )(place, maxima, sums, acts, gain, bias)
        blocks = lax.all_to_all(page, "mp", 0, 0, tiled=True)
    with jax.named_scope("smoothed_weight"):
        served, scale, tok = pl.pallas_call(
            serve_kernel,
            out_shape=(
                jax.ShapeDtypeStruct((48, D), jnp.bfloat16),
                jax.ShapeDtypeStruct((12, 128), jnp.float32),
                jax.ShapeDtypeStruct((4, 128), jnp.float32),
            ),
            in_specs=[SMEM_SPEC, SMEM_SPEC, VMEM_SPEC, VMEM_SPEC],
            out_specs=(VMEM_SPEC,) * 3,
            compiler_params=params(),
        )(place, lengths, blocks, pages)
    return served, scale.reshape(1536), tok.reshape(512)


def solution(mesh):
    return jax.shard_map(
        body,
        mesh=mesh,
        in_specs=(P("dp", "mp"), P("dp"), P("mp"), P("mp"), P("dp", "mp")),
        out_specs=(P(("mp", "dp"), None), P("mp"), P("dp")),
        check_vma=False,
    )
```

time: 573 us -> 111 us (0.19)
  blocking collectives: 543 us -> 87.5 us
  starting transfers between devices: 12.1 us -> 3.35 us
  Pallas kernels: 0 us -> 8.71 us
  waiting for transfers between devices: 0.01 us -> 7.55 us
  other arithmetic: 7.48 us -> 0.08 us
    unnamed x1 -> x0, blocking collectives: 270 us -> none
    pmax x3 -> x0, blocking collectives: 207 us -> none  [the longest x1 143 us: body(): act_block = lax.pmax(act_local, 'dp')]
    all_to_all x0 -> x3, blocking collectives: none -> 87.5 us  [the longest x1 36.7 us: body(): pages = lax.all_to_all(packed, 'dp', 0, 0, tiled=True)]
    all_gather x1 -> x0, blocking collectives: 37.6 us -> none  [body(): act_full = lax.all_gather(act_block, 'mp', axis=0, tiled=True)]
    psum x1 -> x0, blocking collectives: 28.9 us -> none  [body(): moments = lax.psum((jnp.sum(x, axis=1), jnp.sum(x * x, axis=1)), 'mp')]
    all_to_all x1, starting transfers between devices: 12.1 us -> 3.35 us  [body(): blocks = lax.all_to_all(page, 'mp', 0, 0, tiled=True)]
    pallas_call x0 -> x5, Pallas kernels: none -> 8.71 us  [the longest x1 2.27 us: body(): pl.pallas_call(peak_kernel, out_shape=jax.ShapeDtypeStruct((8, 16, 128),...]
    all_to_all x1, waiting for transfers between devices: 0.01 us -> 7.55 us  [body(): blocks = lax.all_to_all(page, 'mp', 0, 0, tiled=True)]
  transfers between devices with their start and end apart: 1 -> 1, of which waited for: 0 -> 1; matrix products, arithmetic and copies ran while one was open for 0% -> 0% of each run, Pallas kernels for 0% -> 2%
where the time goes in v1:
time: 111 us
  blocking collectives  87.5 us (79%)
  Pallas kernels  8.71 us (8%)
  waiting for transfers between devices  7.55 us (7%)
  starting transfers between devices  3.35 us (3%)
  local copies, waits for them, and re-layouts  2.7 us (2%)
    all_to_all x1, blocking collectives, body(): pages = lax.all_to_all(packed, 'dp', 0, 0, tiled=True)  36.7 us
    all_to_all x1, blocking collectives, body(): maxima = lax.all_to_all(page, 'dp', 0, 0, tiled=True)  31.6 us
    all_to_all x1, blocking collectives, body(): sums = lax.all_to_all(page, 'mp', 0, 0, tiled=True)  19.1 us
    all_to_all x1, waiting for transfers between devices, body(): blocks = lax.all_to_all(page, 'mp', 0, 0, tiled=True)  7.55 us
    all_to_all x1, starting transfers between devices, body(): blocks = lax.all_to_all(page, 'mp', 0, 0, tiled=True)  3.35 us
    unnamed x14, local copies, waits for them, and re-layouts  2.7 us
    pallas_call x1, Pallas kernels, body(): pl.pallas_call(peak_kernel, out_shape=jax.ShapeDtypeStruct((8, 16, 128),...  2.27 us
  transfers between devices with their start and end apart: 1, of which 1 were waited for; matrix products, arithmetic and copies ran while one was open for 0% of the time, Pallas kernels for 2%

profile of v1, /device:TPU:1, one launch (start us, length us, event | category | flops | bytes accessed | tf_op | source)
XLA Modules:
  0.0 110.6 jit_solution(18087920442602106587)
XLA Ops:
  0.6 0.1 pad_add_fusion.place_ref
  0.7 0.0 copy-start
  0.7 1.4 %copy-done = bf16[512,1536]{1,0:T(8,128)(2,1)S(1)} copy-done((bf16[512,1536]{1,0:T(8,128)(2,1)S(1)}, bf16[512,1536]{1,0:T(8,128)(2,1)}, u32[]{:S(2)}) %copy-start) | copy-done | bytes 1572888
  2.1 0.0 copy-start.2
  2.1 1.3 %copy-done.2 = bf16[192,3072]{1,0:T(8,128)(2,1)S(1)} copy-done((bf16[192,3072]{1,0:T(8,128)(2,1)S(1)}, bf16[192,3072]{1,0:T(8,128)(2,1)}, u32[]{:S(2)}) %copy-start.2) | copy-done | bytes 1179672
  3.4 0.0 copy-start.1
  3.4 0.0 copy-start.4
  3.4 0.0 copy-start.5
  3.4 0.0 copy-start.6
  3.4 1.3 %token_moments.1 = f32[8,16,128]{2,1,0:T(8,128)S(1)} custom-call(s32[2]{0:T(128)S(1)} %pad_add_fusion.place_ref, bf16[512,1536]{1,0:T(8,128)(2,1)S(1)} %copy-done, bf16[192,3072]{1,0:T(8,128)(2,1)S(1)} %copy-done.2), custom_call_target="tpu_custom_call" | custom-call | tf_op jit(solution)/shard_map/token_moments/pallas_call | solution.py:141
  4.7 19.1 %all_to_all.20.sums_ref = f32[8,16,128]{2,1,0:T(8,128)S(1)} all-to-all(f32[8,16,128]{2,1,0:T(8,128)S(1)} %token_moments.1), channel_id=1, replica_groups=mesh['dp'=64,'mp'=8] {'mp'}, dimensions={0} | all-to-all | bytes 131072 | tf_op jit(solution)/shard_map/token_moments/all_to_all | solution.py:149
  23.8 0.0 copy-done.1
  23.8 0.0 copy-done.4
  23.8 0.0 copy-done.5
  23.8 0.0 copy-done.6
  23.8 1.6 %channel_maxima.1 = f32[64,16,128]{2,1,0:T(8,128)S(1)} custom-call(s32[2]{0:T(128)S(1)} %copy-done.6, f32[8,16,128]{2,1,0:T(8,128)S(1)} %all_to_all.20.sums_ref, bf16[512,1536]{1,0:T(8,128)(2,1)S(1)} %copy-done.1, f32[12,128]{1,0:T(8,128)S(1)} %bitcast.6, f32[12,128]{1,0:T(8,128)S(1)} %bitcast.8), custom_call_target="tpu_custom_call" | custom-call | tf_op jit(solution)/shard_map/channel_maxima/pallas_call | solution.py:160
  25.5 31.6 %all_to_all.21.maxima_ref = f32[64,16,128]{2,1,0:T(8,128)S(1)} all-to-all(f32[64,16,128]{2,1,0:T(8,128)S(1)} %channel_maxima.1), channel_id=1, replica_groups=mesh['dp'=64,'mp'=8] {'dp'}, dimensions={0} | all-to-all | bytes 1048576 | tf_op jit(solution)/shard_map/channel_maxima/all_to_all | solution.py:167
  57.1 0.0 copy-start.3
  57.1 2.3 %token_peaks.1 = f32[8,16,128]{2,1,0:T(8,128)} custom-call(s32[2]{0:T(128)S(1)} %pad_add_fusion.place_ref, f32[64,16,128]{2,1,0:T(8,128)S(1)} %all_to_all.21.maxima_ref, f32[8,16,128]{2,1,0:T(8,128)S(1)} %all_to_all.20.sums_ref, bf16[512,1536]{1,0:T(8,128)(2,1)S(1)} %copy-done.1, f32[12,128]{1,0:T(8,128)S(1)} %bitcast.7, f32[12,128]{1,0:T(8,128)S(1)} %bitcast.9), custom_call_target="tpu_custom_call" | custom-call | tf_op jit(solution)/shard_map/token_peaks/pallas_call | solution.py:169
  59.4 3.4 %all-to-all-start.2 = ((f32[8,16,128]{2,1,0:T(8,128)}), f32[8,16,128]{2,1,0:T(8,128)S(1)}, u32[]{:S(2)}, u32[]{:S(2)}) async-start(f32[8,16,128]{2,1,0:T(8,128)} %token_peaks.1), calls=%async_computation.2 | async-start | bytes 131072 | tf_op jit(solution)/shard_map/token_peaks/all_to_all | solution.py:176
  62.8 0.0 copy-done.3
  62.8 1.7 %weight_exchange.1 = bf16[64,72,128]{2,1,0:T(8,128)(2,1)S(1)} custom-call(s32[2]{0:T(128)S(1)} %pad_add_fusion.place_ref, bf16[192,3072]{1,0:T(8,128)(2,1)S(1)} %copy-done.3), custom_call_target="tpu_custom_call" | custom-call | tf_op jit(solution)/shard_map/weight_exchange/pallas_call | solution.py:151
  64.4 7.5 %all-to-all-done.2.blocks_ref = f32[8,16,128]{2,1,0:T(8,128)S(1)} async-done(((f32[8,16,128]{2,1,0:T(8,128)}), f32[8,16,128]{2,1,0:T(8,128)S(1)}, u32[]{:S(2)}, u32[]{:S(2)}) %all-to-all-start.2) | async-done | bytes 65568 | tf_op jit(solution)/shard_map/token_peaks/all_to_all | solution.py:176
  72.0 36.7 %all_to_all.22.pages_ref = bf16[64,72,128]{2,1,0:T(8,128)(2,1)S(1)} all-to-all(bf16[64,72,128]{2,1,0:T(8,128)(2,1)S(1)} %weight_exchange.1), channel_id=1, replica_groups=mesh['dp'=64,'mp'=8] {'dp'}, dimensions={0} | all-to-all | bytes 2359296 | tf_op jit(solution)/shard_map/weight_exchange/all_to_all | solution.py:158
  108.7 1.8 %smoothed_weight.1 = (bf16[48,12288]{1,0:T(8,128)(2,1)}, f32[12,128]{1,0:T(8,128)}, f32[4,128]{1,0:T(4,128)}) custom-call(s32[2]{0:T(128)S(1)} %pad_add_fusion.place_ref, s32[2]{0:T(128)S(1)} %copy-done.6, f32[8,16,128]{2,1,0:T(8,128)S(1)} %all-to-all-done.2.blocks_ref, bf16[64,72,128]{2,1,0:T(8,128)(2,1)S(1)} %all_to_all.22.pages_ref), custom_call_target="tpu_custom_call" | custom-call | tf_op jit(solution)/shard_map/smoothed_weight/pallas_call | solution.py:178
Async XLA Ops:
  0.7 1.4 %copy-start = (bf16[512,1536]{1,0:T(8,128)(2,1)S(1)}, bf16[512,1536]{1,0:T(8,128)(2,1)}, u32[]{:S(2)}) copy-start(bf16[512,1536]{1,0:T(8,128)(2,1)} %acts_ref.5) | copy-start | bytes 4718596
  2.1 1.3 %copy-start.2 = (bf16[192,3072]{1,0:T(8,128)(2,1)S(1)}, bf16[192,3072]{1,0:T(8,128)(2,1)}, u32[]{:S(2)}) copy-start(bf16[192,3072]{1,0:T(8,128)(2,1)} %w_ref.3) | copy-start | bytes 3538948
  3.4 20.4 %copy-start.1 = (bf16[512,1536]{1,0:T(8,128)(2,1)S(1)}, bf16[512,1536]{1,0:T(8,128)(2,1)}, u32[]{:S(2)}) copy-start(bf16[512,1536]{1,0:T(8,128)(2,1)} %acts_ref.5) | copy-start | bytes 4718596
  3.4 20.4 %copy-start.4 = (f32[1536]{0:T(1024)S(1)}, f32[1536]{0:T(1024)}, u32[]{:S(2)}) copy-start(f32[1536]{0:T(1024)} %param.7) | copy-start | bytes 18436
  3.4 20.4 %copy-start.5 = (f32[1536]{0:T(1024)S(1)}, f32[1536]{0:T(1024)}, u32[]{:S(2)}) copy-start(f32[1536]{0:T(1024)} %param.8) | copy-start | bytes 18436
  3.4 20.4 %copy-start.6 = (s32[2]{0:T(128)S(1)}, s32[2]{0:T(128)}, u32[]{:S(2)}) copy-start(s32[2]{0:T(128)} %lengths_ref.3) | copy-start | bytes 28
  57.1 5.6 %copy-start.3 = (bf16[192,3072]{1,0:T(8,128)(2,1)S(1)}, bf16[192,3072]{1,0:T(8,128)(2,1)}, u32[]{:S(2)}) copy-start(bf16[192,3072]{1,0:T(8,128)(2,1)} %w_ref.3) | copy-start | bytes 3538948
  59.4 12.6 %all-to-all-start.2 = ((f32[8,16,128]{2,1,0:T(8,128)}), f32[8,16,128]{2,1,0:T(8,128)S(1)}, u32[]{:S(2)}, u32[]{:S(2)}) async-start(f32[8,16,128]{2,1,0:T(8,128)} %token_peaks.1), calls=%async_computation.2 | async-start | bytes 131072 | tf_op jit(solution)/shard_map/token_peaks/all_to_all | solution.py:176

commit v2 on v1

--- a/solution.py
+++ b/solution.py
@@ -25,8 +25,8 @@
             x = acts_ref[pl.ds(128 * block, 128), pl.ds(128 * tile, 128)].astype(jnp.float32)
             total = total + x
             square = square + x * x
-        page_ref[0, block : block + 1, :] = jnp.sum(total.T, axis=0, keepdims=True)
-        page_ref[0, 4 + block : 5 + block, :] = jnp.sum(square.T, axis=0, keepdims=True)
+        page_ref[block : block + 1, :] = jnp.sum(total.T, axis=0, keepdims=True)
+        page_ref[4 + block : 5 + block, :] = jnp.sum(square.T, axis=0, keepdims=True)
     rows_ref[...] = jnp.zeros_like(rows_ref)
     for part in range(2):
         peak = jnp.zeros((96, 128), jnp.float32)
@@ -34,11 +34,8 @@
             peak = jnp.maximum(peak, jnp.abs(w_ref[pl.ds(96 * part, 96), pl.ds(128 * tile, 128)].astype(jnp.float32)))
         rows_ref[pl.ds(pl.multiple_of(192 * parity + 96 * part, 32), 96), :] = peak
     for block in range(3):
-        page_ref[0, 8 + block : 9 + block, :] = jnp.max(rows_ref[pl.ds(128 * block, 128), :].T, axis=0, keepdims=True)
-    page_ref[0, 11:16, :] = jnp.zeros((5, 128), jnp.float32)
-    page = page_ref[0]
-    for peer in range(1, page_ref.shape[0]):
-        page_ref[peer] = page
+        page_ref[8 + block : 9 + block, :] = jnp.max(rows_ref[pl.ds(128 * block, 128), :].T, axis=0, keepdims=True)
+    page_ref[11:16, :] = jnp.zeros((5, 128), jnp.float32)
 
 
 def pack_kernel(place_ref, w_ref, page_ref):
@@ -62,14 +59,13 @@
 
 
 def moments(sums):
-    total = jnp.sum(sums[:, 0:8], axis=0)
-    mean = total[0:4] / D
-    var = total[4:8] / D - mean * mean
+    mean = sums[0:4] / D
+    var = sums[4:8] / D - mean * mean
     rstd = lax.rsqrt(var + EPS)
     return jnp.concatenate([mean, rstd], axis=0).T
 
 
-def act_kernel(lengths_ref, sums_ref, acts_ref, gain_ref, bias_ref, page_ref):
+def act_kernel(place_ref, lengths_ref, sums_ref, acts_ref, gain_ref, bias_ref, page_ref):
     columns = moments(sums_ref[...])
     place = lax.broadcasted_iota(jnp.int32, (128, 1), 0)
     for tile in range(12):
@@ -81,22 +77,16 @@
             normed = (x - columns[:, block : block + 1]) * columns[:, 4 + block : 5 + block] * gain + bias
             valid = place + 128 * (block % 2) < lengths_ref[block // 2]
             peak = jnp.maximum(peak, jnp.where(valid, jnp.abs(normed), 0.0))
-        page_ref[0, tile : tile + 1, :] = jnp.max(peak, axis=0, keepdims=True)
-    page_ref[0, 12:15, :] = jnp.max(sums_ref[:, 8:11, :], axis=0)
-    page_ref[0, 15:16, :] = jnp.zeros((1, 128), jnp.float32)
-    page = page_ref[0]
-    for peer in range(1, page_ref.shape[0]):
-        page_ref[peer] = page
-
-
-def peak_kernel(place_ref, maxima_ref, sums_ref, acts_ref, gain_ref, bias_ref, page_ref):
+        page_ref[tile : tile + 1, :] = jnp.max(peak, axis=0, keepdims=True)
+    pair = (place_ref[0] // 2) % 4
+    for slot in range(4):
+        page_ref[12 + 3 * slot : 15 + 3 * slot, :] = jnp.where(pair == slot, sums_ref[8:11, :], 0.0)
+
+
+def peak_kernel(pages_ref, maxima_ref, sums_ref, acts_ref, gain_ref, bias_ref, page_ref):
+    del pages_ref
     columns = moments(sums_ref[...])
-    act = jnp.max(maxima_ref[:, 0:12, :], axis=0)
-    start = 8 * place_ref[1]
-    for pair in range(4):
-        both = jnp.maximum(maxima_ref[start + 2 * pair, 12:15, :], maxima_ref[start + 2 * pair + 1, 12:15, :])
-        page_ref[0, 3 * pair : 3 * pair + 3, :] = both
-    scale = jnp.sqrt(act + EPS) / jnp.sqrt(page_ref[0, 0:12, :] + EPS)
+    scale = jnp.sqrt(maxima_ref[0:12, :] + EPS) / jnp.sqrt(maxima_ref[12:24, :] + EPS)
     page_ref[0, 0:12, :] = scale
     inverse = 1.0 / scale
     for block in range(4):
@@ -133,20 +123,17 @@
             served_ref[:, pl.ds(128 * row, 128)] = (tile * scale).astype(jnp.bfloat16)
 
 
+def swap(x, axis, bit):
+    size = lax.axis_size(axis)
+    return lax.ppermute(x, axis, [(i, i ^ bit) for i in range(size)])
+
+
 def body(acts, lengths, ln_gain, ln_bias, w_fc1):
-    place = jnp.stack([lax.axis_index("dp"), lax.axis_index("mp")]).astype(jnp.int32)
+    dp_place = lax.axis_index("dp")
+    mp_place = lax.axis_index("mp")
+    place = jnp.stack([dp_place, mp_place]).astype(jnp.int32)
     gain = ln_gain.reshape(12, 128)
     bias = ln_bias.reshape(12, 128)
-    with jax.named_scope("token_moments"):
-        page = pl.pallas_call(
-            stats_kernel,
-            out_shape=jax.ShapeDtypeStruct((8, 16, 128), jnp.float32),
-            in_specs=[SMEM_SPEC, VMEM_SPEC, VMEM_SPEC],
-            out_specs=VMEM_SPEC,
-            scratch_shapes=[pltpu.VMEM((384, 128), jnp.float32)],
-            compiler_params=params(),
-        )(place, acts, w_fc1)
-        sums = lax.all_to_all(page, "mp", 0, 0, tiled=True)
     with jax.named_scope("weight_exchange"):
         packed = pl.pallas_call(
             pack_kernel,
@@ -156,23 +143,41 @@
             compiler_params=params(),
         )(place, w_fc1)
         pages = lax.all_to_all(packed, "dp", 0, 0, tiled=True)
+    with jax.named_scope("token_moments"):
+        sums = pl.pallas_call(
+            stats_kernel,
+            out_shape=jax.ShapeDtypeStruct((16, 128), jnp.float32),
+            in_specs=[SMEM_SPEC, VMEM_SPEC, VMEM_SPEC],
+            out_specs=VMEM_SPEC,
+            scratch_shapes=[pltpu.VMEM((384, 128), jnp.float32)],
+            compiler_params=params(),
+        )(place, acts, w_fc1)
+        added = lax.broadcasted_iota(jnp.int32, (16, 128), 0) < 8
+        for bit in (1, 2, 4):
+            other = swap(sums, "mp", bit)
+            sums = jnp.where(added, sums + other, jnp.maximum(sums, other))
     with jax.named_scope("channel_maxima"):
-        page = pl.pallas_call(
+        maxima = pl.pallas_call(
             act_kernel,
-            out_shape=jax.ShapeDtypeStruct((64, 16, 128), jnp.float32),
-            in_specs=[SMEM_SPEC] + [VMEM_SPEC] * 4,
-            out_specs=VMEM_SPEC,
-            compiler_params=params(),
-        )(lengths, sums, acts, gain, bias)
-        maxima = lax.all_to_all(page, "dp", 0, 0, tiled=True)
+            out_shape=jax.ShapeDtypeStruct((24, 128), jnp.float32),
+            in_specs=[SMEM_SPEC] * 2 + [VMEM_SPEC] * 4,
+            out_specs=VMEM_SPEC,
+            compiler_params=params(),
+        )(place, lengths, sums, acts, gain, bias)
+        for bit in (1, 2, 4):
+            maxima = jnp.maximum(maxima, swap(maxima, "dp", bit))
+        kept = (lax.broadcasted_iota(jnp.int32, (24, 128), 0) < 12) | (dp_place // 8 == mp_place)
+        maxima = jnp.where(kept, maxima, 0.0)
+        for bit in (8, 16, 32):
+            maxima = jnp.maximum(maxima, swap(maxima, "dp", bit))
     with jax.named_scope("token_peaks"):
         page = pl.pallas_call(
             peak_kernel,
             out_shape=jax.ShapeDtypeStruct((8, 16, 128), jnp.float32),
-            in_specs=[SMEM_SPEC] + [VMEM_SPEC] * 5,
-            out_specs=VMEM_SPEC,
-            compiler_params=params(),
-        )(place, maxima, sums, acts, gain, bias)
+            in_specs=[pl.BlockSpec(memory_space=pl.ANY)] + [VMEM_SPEC] * 5,
+            out_specs=VMEM_SPEC,
+            compiler_params=params(),
+        )(pages, maxima, sums, acts, gain, bias)
         blocks = lax.all_to_all(page, "mp", 0, 0, tiled=True)
     with jax.named_scope("smoothed_weight"):
         served, scale, tok = pl.pallas_call(

time: 111 us -> 103 us (0.928)
  the two profiles are of different devices: /device:TPU:1 before, /device:TPU:16 now
where the time goes in v2:
time: 103 us
  starting transfers between devices  50 us (49%)
  waiting for transfers between devices  23.2 us (23%)
  blocking collectives  17.2 us (17%)
  Pallas kernels  7.46 us (7%)
  local copies, waits for them, and re-layouts  3.56 us (3%)
    ppermute x9, starting transfers between devices, swap(): return lax.ppermute(x, axis, [(i, i ^ bit) for i in range(size)])  35.6 us
    ppermute x9, waiting for transfers between devices, swap(): return lax.ppermute(x, axis, [(i, i ^ bit) for i in range(size)])  23.2 us
    all_to_all x1, blocking collectives, body(): blocks = lax.all_to_all(page, 'mp', 0, 0, tiled=True)  17.2 us
    all_to_all x1, starting transfers between devices, body(): pages = lax.all_to_all(packed, 'dp', 0, 0, tiled=True)  14.4 us
    unnamed x14, local copies, waits for them, and re-layouts  3.56 us
  transfers between devices with their start and end apart: 10, of which 9 were waited for; matrix products, arithmetic and copies ran while one was open for 0% of the time, Pallas kernels for 3%

profile of v2, /device:TPU:16, one launch (start us, length us, event | category | flops | bytes accessed | tf_op | source)
XLA Modules:
  0.0 102.6 jit_solution(17494844620791546183)
XLA Ops:
  0.6 0.1 pad_add_fusion.place_ref
  0.7 0.0 copy-start.1
  0.7 1.3 %copy-done.1 = bf16[192,3072]{1,0:T(8,128)(2,1)S(1)} copy-done((bf16[192,3072]{1,0:T(8,128)(2,1)S(1)}, bf16[192,3072]{1,0:T(8,128)(2,1)}, u32[]{:S(2)}) %copy-start.1) | copy-done | bytes 1179672
  2.0 1.7 %weight_exchange.1 = bf16[64,72,128]{2,1,0:T(8,128)(2,1)S(1)} custom-call(s32[2]{0:T(128)S(1)} %pad_add_fusion.place_ref, bf16[192,3072]{1,0:T(8,128)(2,1)S(1)} %copy-done.1), custom_call_target="tpu_custom_call" | custom-call | tf_op jit(solution)/shard_map/weight_exchange/pallas_call | solution.py:138
  3.6 0.0 copy-start.3
  3.7 1.0 copy-done.3
  4.7 0.0 copy-start
  4.7 14.4 %all-to-all-start = ((bf16[64,72,128]{2,1,0:T(8,128)(2,1)}), bf16[64,72,128]{2,1,0:T(8,128)(2,1)S(1)}, u32[]{:S(2)}, u32[]{:S(2)}) async-start(bf16[64,72,128]{2,1,0:T(8,128)(2,1)} %copy-done.3), calls=%async_computation | async-start | bytes 2359296 | tf_op jit(solution)/shard_map/weight_exchange/all_to_all | solution.py:145
  19.0 0.0 copy-done
  19.1 0.0 copy-start.2
  19.1 1.3 %copy-done.2 = bf16[192,3072]{1,0:T(8,128)(2,1)S(1)} copy-done((bf16[192,3072]{1,0:T(8,128)(2,1)S(1)}, bf16[192,3072]{1,0:T(8,128)(2,1)}, u32[]{:S(2)}) %copy-start.2) | copy-done | bytes 1179672
  20.3 0.0 copy-start.4
  20.3 0.0 copy-start.5
  20.3 0.0 copy-start.6
  20.3 1.3 %token_moments.1 = f32[16,128]{1,0:T(8,128)S(1)} custom-call(s32[2]{0:T(128)S(1)} %pad_add_fusion.place_ref, bf16[512,1536]{1,0:T(8,128)(2,1)S(1)} %copy-done, bf16[192,3072]{1,0:T(8,128)(2,1)S(1)} %copy-done.2), custom_call_target="tpu_custom_call" | custom-call | tf_op jit(solution)/shard_map/token_moments/pallas_call | solution.py:147
  21.7 3.4 %collective-permute-start = (f32[16,128]{1,0:T(8,128)S(1)}, f32[16,128]{1,0:T(8,128)S(1)}, u32[]{:S(2)}, u32[]{:S(2)}) collective-permute-start(f32[16,128]{1,0:T(8,128)S(1)} %token_moments.1), channel_id=1, source_target_pairs={{0,1},{1,0},{2,3},{3,2},{4,5},{5,4},{6,7},{7,6},{8,9},{9,8},{10,11... | collective-permute-start | bytes 24584 | tf_op jit(solution)/shard_map/token_moments/ppermute | solution.py:128
  25.1 2.1 %collective-permute-done = f32[16,128]{1,0:T(8,128)S(1)} collective-permute-done((f32[16,128]{1,0:T(8,128)S(1)}, f32[16,128]{1,0:T(8,128)S(1)}, u32[]{:S(2)}, u32[]{:S(2)}) %collective-permute-start) | collective-permute-done | bytes 8224 | tf_op jit(solution)/shard_map/token_moments/ppermute | solution.py:128
  27.2 0.1 maximum_select_fusion.3
  27.3 4.9 %collective-permute-start.1 = (f32[16,128]{1,0:T(8,128)S(1)}, f32[16,128]{1,0:T(8,128)S(1)}, u32[]{:S(2)}, u32[]{:S(2)}) collective-permute-start(f32[16,128]{1,0:T(8,128)S(1)} %maximum_select_fusion.3), channel_id=1, source_target_pairs={{0,2},{1,3},{2,0},{3,1},{4,6},{5,7},{6,4},{7,5},{8,10},{9,11},{10,... | collective-permute-start | bytes 24584 | tf_op jit(solution)/shard_map/token_moments/ppermute | solution.py:128
  32.2 2.1 %collective-permute-done.1 = f32[16,128]{1,0:T(8,128)S(1)} collective-permute-done((f32[16,128]{1,0:T(8,128)S(1)}, f32[16,128]{1,0:T(8,128)S(1)}, u32[]{:S(2)}, u32[]{:S(2)}) %collective-permute-start.1) | collective-permute-done | bytes 8224 | tf_op jit(solution)/shard_map/token_moments/ppermute | solution.py:128
  34.3 0.1 maximum_select_fusion.2
  34.4 5.0 %collective-permute-start.2 = (f32[16,128]{1,0:T(8,128)S(1)}, f32[16,128]{1,0:T(8,128)S(1)}, u32[]{:S(2)}, u32[]{:S(2)}) collective-permute-start(f32[16,128]{1,0:T(8,128)S(1)} %maximum_select_fusion.2), channel_id=1, source_target_pairs={{0,4},{1,5},{2,6},{3,7},{4,0},{5,1},{6,2},{7,3},{8,12},{9,13},{10,... | collective-permute-start | bytes 24584 | tf_op jit(solution)/shard_map/token_moments/ppermute | solution.py:128
  39.4 4.6 %collective-permute-done.2 = f32[16,128]{1,0:T(8,128)S(1)} collective-permute-done((f32[16,128]{1,0:T(8,128)S(1)}, f32[16,128]{1,0:T(8,128)S(1)}, u32[]{:S(2)}, u32[]{:S(2)}) %collective-permute-start.2) | collective-permute-done | bytes 8224 | tf_op jit(solution)/shard_map/token_moments/ppermute | solution.py:128
  44.0 0.1 maximum_select_fusion.1.sums_ref
  44.1 0.0 copy-done.4
  44.1 0.0 copy-done.5
  44.1 0.0 copy-done.6
  44.1 1.6 %channel_maxima.1 = f32[24,128]{1,0:T(8,128)S(1)} custom-call(s32[2]{0:T(128)S(1)} %pad_add_fusion.place_ref, s32[2]{0:T(128)S(1)} %copy-done.6, f32[16,128]{1,0:T(8,128)S(1)} %maximum_select_fusion.1.sums_ref, bf16[512,1536]{1,0:T(8,128)(2,1)S(1)} %copy-done, f32[12,128]{1,0:T(8,128)S(1)} %bitcast.6, f32[12,128]{1,0:T(8,128)S(1)} %bitcast.8), custom_call_target="tpu_custom_call" | custom-call | tf_op jit(solution)/shard_map/channel_maxima/pallas_call | solution.py:160
  45.7 1.9 %collective-permute-start.3 = (f32[24,128]{1,0:T(8,128)S(1)}, f32[24,128]{1,0:T(8,128)S(1)}, u32[]{:S(2)}, u32[]{:S(2)}) collective-permute-start(f32[24,128]{1,0:T(8,128)S(1)} %channel_maxima.1), channel_id=1, source_target_pairs={{0,8},{8,0},{16,24},{24,16},{32,40},{40,32},{48,56},{56,48},{64,72... | collective-permute-start | bytes 36872 | tf_op jit(solution)/shard_map/channel_maxima/ppermute | solution.py:128
  47.6 1.1 %collective-permute-done.3 = f32[24,128]{1,0:T(8,128)S(1)} collective-permute-done((f32[24,128]{1,0:T(8,128)S(1)}, f32[24,128]{1,0:T(8,128)S(1)}, u32[]{:S(2)}, u32[]{:S(2)}) %collective-permute-start.3) | collective-permute-done | bytes 12320 | tf_op jit(solution)/shard_map/channel_maxima/ppermute | solution.py:128
  48.8 3.3 %collective-permute-start.4 = (f32[24,128]{1,0:T(8,128)S(1)}, f32[24,128]{1,0:T(8,128)S(1)}, u32[]{:S(2)}, u32[]{:S(2)}) collective-permute-start(f32[24,128]{1,0:T(8,128)S(1)} %max.30), channel_id=1, source_target_pairs={{0,16},{8,24},{16,0},{24,8},{32,48},{40,56},{48,32},{56,40},{64,80... | collective-permute-start | bytes 36872 | tf_op jit(solution)/shard_map/channel_maxima/ppermute | solution.py:128
  52.1 2.3 %collective-permute-done.4 = f32[24,128]{1,0:T(8,128)S(1)} collective-permute-done((f32[24,128]{1,0:T(8,128)S(1)}, f32[24,128]{1,0:T(8,128)S(1)}, u32[]{:S(2)}, u32[]{:S(2)}) %collective-permute-start.4) | collective-permute-done | bytes 12320 | tf_op jit(solution)/shard_map/channel_maxima/ppermute | solution.py:128
  54.4 2.3 %collective-permute-start.5 = (f32[24,128]{1,0:T(8,128)S(1)}, f32[24,128]{1,0:T(8,128)S(1)}, u32[]{:S(2)}, u32[]{:S(2)}) collective-permute-start(f32[24,128]{1,0:T(8,128)S(1)} %max.31), channel_id=1, source_target_pairs={{0,32},{8,40},{16,48},{24,56},{32,0},{40,8},{48,16},{56,24},{64,96... | collective-permute-start | bytes 36872 | tf_op jit(solution)/shard_map/channel_maxima/ppermute | solution.py:128
  56.7 4.2 %collective-permute-done.5 = f32[24,128]{1,0:T(8,128)S(1)} collective-permute-done((f32[24,128]{1,0:T(8,128)S(1)}, f32[24,128]{1,0:T(8,128)S(1)}, u32[]{:S(2)}, u32[]{:S(2)}) %collective-permute-start.5) | collective-permute-done | bytes 12320 | tf_op jit(solution)/shard_map/channel_maxima/ppermute | solution.py:128
  60.9 0.1 maximum_select_fusion
  61.0 3.3 %collective-permute-start.6 = (f32[24,128]{1,0:T(8,128)S(1)}, f32[24,128]{1,0:T(8,128)S(1)}, u32[]{:S(2)}, u32[]{:S(2)}) collective-permute-start(f32[24,128]{1,0:T(8,128)S(1)} %maximum_select_fusion), channel_id=1, source_target_pairs={{0,64},{8,72},{16,80},{24,88},{32,96},{40,104},{48,112},{56,120},{... | collective-permute-start | bytes 36872 | tf_op jit(solution)/shard_map/channel_maxima/ppermute | solution.py:128
  64.3 2.2 %collective-permute-done.6 = f32[24,128]{1,0:T(8,128)S(1)} collective-permute-done((f32[24,128]{1,0:T(8,128)S(1)}, f32[24,128]{1,0:T(8,128)S(1)}, u32[]{:S(2)}, u32[]{:S(2)}) %collective-permute-start.6) | collective-permute-done | bytes 12320 | tf_op jit(solution)/shard_map/channel_maxima/ppermute | solution.py:128
  66.5 4.2 %collective-permute-start.7 = (f32[24,128]{1,0:T(8,128)S(1)}, f32[24,128]{1,0:T(8,128)S(1)}, u32[]{:S(2)}, u32[]{:S(2)}) collective-permute-start(f32[24,128]{1,0:T(8,128)S(1)} %max.33), channel_id=1, source_target_pairs={{0,128},{8,136},{16,144},{24,152},{32,160},{40,168},{48,176},{56,1... | collective-permute-start | bytes 36872 | tf_op jit(solution)/shard_map/channel_maxima/ppermute | solution.py:128
  70.7 2.3 %collective-permute-done.7 = f32[24,128]{1,0:T(8,128)S(1)} collective-permute-done((f32[24,128]{1,0:T(8,128)S(1)}, f32[24,128]{1,0:T(8,128)S(1)}, u32[]{:S(2)}, u32[]{:S(2)}) %collective-permute-start.7) | collective-permute-done | bytes 12320 | tf_op jit(solution)/shard_map/channel_maxima/ppermute | solution.py:128
  73.0 7.3 %collective-permute-start.8 = (f32[24,128]{1,0:T(8,128)S(1)}, f32[24,128]{1,0:T(8,128)S(1)}, u32[]{:S(2)}, u32[]{:S(2)}) collective-permute-start(f32[24,128]{1,0:T(8,128)S(1)} %max.34), channel_id=1, source_target_pairs={{0,256},{8,264},{16,272},{24,280},{32,288},{40,296},{48,304},{56,3... | collective-permute-start | bytes 36872 | tf_op jit(solution)/shard_map/channel_maxima/ppermute | solution.py:128
  80.3 2.2 %collective-permute-done.8 = f32[24,128]{1,0:T(8,128)S(1)} collective-permute-done((f32[24,128]{1,0:T(8,128)S(1)}, f32[24,128]{1,0:T(8,128)S(1)}, u32[]{:S(2)}, u32[]{:S(2)}) %collective-permute-start.8) | collective-permute-done | bytes 12320 | tf_op jit(solution)/shard_map/channel_maxima/ppermute | solution.py:128
  82.6 0.0 all-to-all-done.pages_ref
  82.6 1.1 %token_peaks.1 = f32[8,16,128]{2,1,0:T(8,128)S(1)} custom-call(bf16[64,72,128]{2,1,0:T(8,128)(2,1)S(1)} %all-to-all-done.pages_ref, f32[24,128]{1,0:T(8,128)S(1)} %max.35.maxima_ref, f32[16,128]{1,0:T(8,128)S(1)} %maximum_select_fusion.1.sums_ref, bf16[512,1536]{1,0:T(8,128)(2,1)S(1)} %copy-done, f32[12,128]{1,0:T(8,128)S(1)} %bitcast.7, f32[12,128]{1,0:T(8,128)S(1)} %bitcast.9), custom_call_target="tpu_custom_call" | custom-call | tf_op jit(solution)/shard_map/token_peaks/pallas_call | solution.py:174
  83.6 17.2 %all_to_all.10.blocks_ref = f32[8,16,128]{2,1,0:T(8,128)S(1)} all-to-all(f32[8,16,128]{2,1,0:T(8,128)S(1)} %token_peaks.1), channel_id=1, replica_groups=mesh['dp'=64,'mp'=8] {'mp'}, dimensions={0} | all-to-all | bytes 131072 | tf_op jit(solution)/shard_map/token_peaks/all_to_all | solution.py:181
  100.8 1.8 %smoothed_weight.1 = (bf16[48,12288]{1,0:T(8,128)(2,1)}, f32[12,128]{1,0:T(8,128)}, f32[4,128]{1,0:T(4,128)}) custom-call(s32[2]{0:T(128)S(1)} %pad_add_fusion.place_ref, s32[2]{0:T(128)S(1)} %copy-done.6, f32[8,16,128]{2,1,0:T(8,128)S(1)} %all_to_all.10.blocks_ref, bf16[64,72,128]{2,1,0:T(8,128)(2,1)S(1)} %all-to-all-done.pages_ref), custom_call_target="tpu_custom_call" | custom-call | tf_op jit(solution)/shard_map/smoothed_weight/pallas_call | solution.py:183
  (7 shorter events, 0.0 us)
Async XLA Ops:
  0.7 1.3 %copy-start.1 = (bf16[192,3072]{1,0:T(8,128)(2,1)S(1)}, bf16[192,3072]{1,0:T(8,128)(2,1)}, u32[]{:S(2)}) copy-start(bf16[192,3072]{1,0:T(8,128)(2,1)} %w_ref.3) | copy-start | bytes 3538948
  3.6 1.0 copy-start.3
  4.7 14.4 %copy-start = (bf16[512,1536]{1,0:T(8,128)(2,1)S(1)}, bf16[512,1536]{1,0:T(8,128)(2,1)}, u32[]{:S(2)}) copy-start(bf16[512,1536]{1,0:T(8,128)(2,1)} %acts_ref.5) | copy-start | bytes 4718596
  4.7 77.9 %all-to-all-start = ((bf16[64,72,128]{2,1,0:T(8,128)(2,1)}), bf16[64,72,128]{2,1,0:T(8,128)(2,1)S(1)}, u32[]{:S(2)}, u32[]{:S(2)}) async-start(bf16[64,72,128]{2,1,0:T(8,128)(2,1)} %copy-done.3), calls=%async_computation | async-start | bytes 2359296 | tf_op jit(solution)/shard_map/weight_exchange/all_to_all | solution.py:145
  19.1 1.3 %copy-start.2 = (bf16[192,3072]{1,0:T(8,128)(2,1)S(1)}, bf16[192,3072]{1,0:T(8,128)(2,1)}, u32[]{:S(2)}) copy-start(bf16[192,3072]{1,0:T(8,128)(2,1)} %w_ref.3) | copy-start | bytes 3538948
  20.3 23.8 %copy-start.4 = (f32[1536]{0:T(1024)S(1)}, f32[1536]{0:T(1024)}, u32[]{:S(2)}) copy-start(f32[1536]{0:T(1024)} %param.7) | copy-start | bytes 18436
  20.3 23.8 %copy-start.5 = (f32[1536]{0:T(1024)S(1)}, f32[1536]{0:T(1024)}, u32[]{:S(2)}) copy-start(f32[1536]{0:T(1024)} %param.8) | copy-start | bytes 18436
  20.3 23.8 %copy-start.6 = (s32[2]{0:T(128)S(1)}, s32[2]{0:T(128)}, u32[]{:S(2)}) copy-start(s32[2]{0:T(128)} %lengths_ref.3) | copy-start | bytes 28
  21.7 5.5 %collective-permute-start = (f32[16,128]{1,0:T(8,128)S(1)}, f32[16,128]{1,0:T(8,128)S(1)}, u32[]{:S(2)}, u32[]{:S(2)}) collective-permute-start(f32[16,128]{1,0:T(8,128)S(1)} %token_moments.1), channel_id=1, source_target_pairs={{0,1},{1,0},{2,3},{3,2},{4,5},{5,4},{6,7},{7,6},{8,9},{9,8},{10,11... | collective-permute-start | bytes 24584 | tf_op jit(solution)/shard_map/token_moments/ppermute | solution.py:128
  27.3 7.0 %collective-permute-start.1 = (f32[16,128]{1,0:T(8,128)S(1)}, f32[16,128]{1,0:T(8,128)S(1)}, u32[]{:S(2)}, u32[]{:S(2)}) collective-permute-start(f32[16,128]{1,0:T(8,128)S(1)} %maximum_select_fusion.3), channel_id=1, source_target_pairs={{0,2},{1,3},{2,0},{3,1},{4,6},{5,7},{6,4},{7,5},{8,10},{9,11},{10,... | collective-permute-start | bytes 24584 | tf_op jit(solution)/shard_map/token_moments/ppermute | solution.py:128
  34.4 9.6 %collective-permute-start.2 = (f32[16,128]{1,0:T(8,128)S(1)}, f32[16,128]{1,0:T(8,128)S(1)}, u32[]{:S(2)}, u32[]{:S(2)}) collective-permute-start(f32[16,128]{1,0:T(8,128)S(1)} %maximum_select_fusion.2), channel_id=1, source_target_pairs={{0,4},{1,5},{2,6},{3,7},{4,0},{5,1},{6,2},{7,3},{8,12},{9,13},{10,... | collective-permute-start | bytes 24584 | tf_op jit(solution)/shard_map/token_moments/ppermute | solution.py:128
  45.7 3.1 %collective-permute-start.3 = (f32[24,128]{1,0:T(8,128)S(1)}, f32[24,128]{1,0:T(8,128)S(1)}, u32[]{:S(2)}, u32[]{:S(2)}) collective-permute-start(f32[24,128]{1,0:T(8,128)S(1)} %channel_maxima.1), channel_id=1, source_target_pairs={{0,8},{8,0},{16,24},{24,16},{32,40},{40,32},{48,56},{56,48},{64,72... | collective-permute-start | bytes 36872 | tf_op jit(solution)/shard_map/channel_maxima/ppermute | solution.py:128
  48.8 5.6 %collective-permute-start.4 = (f32[24,128]{1,0:T(8,128)S(1)}, f32[24,128]{1,0:T(8,128)S(1)}, u32[]{:S(2)}, u32[]{:S(2)}) collective-permute-start(f32[24,128]{1,0:T(8,128)S(1)} %max.30), channel_id=1, source_target_pairs={{0,16},{8,24},{16,0},{24,8},{32,48},{40,56},{48,32},{56,40},{64,80... | collective-permute-start | bytes 36872 | tf_op jit(solution)/shard_map/channel_maxima/ppermute | solution.py:128
  54.4 6.5 %collective-permute-start.5 = (f32[24,128]{1,0:T(8,128)S(1)}, f32[24,128]{1,0:T(8,128)S(1)}, u32[]{:S(2)}, u32[]{:S(2)}) collective-permute-start(f32[24,128]{1,0:T(8,128)S(1)} %max.31), channel_id=1, source_target_pairs={{0,32},{8,40},{16,48},{24,56},{32,0},{40,8},{48,16},{56,24},{64,96... | collective-permute-start | bytes 36872 | tf_op jit(solution)/shard_map/channel_maxima/ppermute | solution.py:128
  61.0 5.6 %collective-permute-start.6 = (f32[24,128]{1,0:T(8,128)S(1)}, f32[24,128]{1,0:T(8,128)S(1)}, u32[]{:S(2)}, u32[]{:S(2)}) collective-permute-start(f32[24,128]{1,0:T(8,128)S(1)} %maximum_select_fusion), channel_id=1, source_target_pairs={{0,64},{8,72},{16,80},{24,88},{32,96},{40,104},{48,112},{56,120},{... | collective-permute-start | bytes 36872 | tf_op jit(solution)/shard_map/channel_maxima/ppermute | solution.py:128
  66.5 6.5 %collective-permute-start.7 = (f32[24,128]{1,0:T(8,128)S(1)}, f32[24,128]{1,0:T(8,128)S(1)}, u32[]{:S(2)}, u32[]{:S(2)}) collective-permute-start(f32[24,128]{1,0:T(8,128)S(1)} %max.33), channel_id=1, source_target_pairs={{0,128},{8,136},{16,144},{24,152},{32,160},{40,168},{48,176},{56,1... | collective-permute-start | bytes 36872 | tf_op jit(solution)/shard_map/channel_maxima/ppermute | solution.py:128
  73.0 9.5 %collective-permute-start.8 = (f32[24,128]{1,0:T(8,128)S(1)}, f32[24,128]{1,0:T(8,128)S(1)}, u32[]{:S(2)}, u32[]{:S(2)}) collective-permute-start(f32[24,128]{1,0:T(8,128)S(1)} %max.34), channel_id=1, source_target_pairs={{0,256},{8,264},{16,272},{24,280},{32,288},{40,296},{48,304},{56,3... | collective-permute-start | bytes 36872 | tf_op jit(solution)/shard_map/channel_maxima/ppermute | solution.py:128

commit v3 on v2

v3 whole, which is shorter than its diff:
```python
import jax
import jax.numpy as jnp
from jax import lax
from jax.experimental import pallas as pl
from jax.experimental.pallas import tpu as pltpu
from jax.sharding import PartitionSpec as P

D = 12288
SLOT = 256
EPS = 1e-05
VMEM_SPEC = pl.BlockSpec(memory_space=pltpu.VMEM)
SMEM_SPEC = pl.BlockSpec(memory_space=pltpu.SMEM)


def params(mebibytes=40):
    return pltpu.CompilerParams(vmem_limit_bytes=mebibytes * 1024 * 1024)


def pack_kernel(place_ref, w_ref, page_ref, peak_ref, rows_ref):
    step = pl.program_id(0)
    parity = place_ref[0] % 2
    low = lax.broadcasted_iota(jnp.int32, (24, 128), 1) < 64
    first = low == (parity == 0)

    @pl.when(step == 0)
    def _():
        rows_ref[...] = jnp.zeros_like(rows_ref)

    own = pl.ds(pl.multiple_of(192 * parity, 64), 192)
    w = jnp.abs(w_ref[...].astype(jnp.float32))
    peak = jnp.maximum(jnp.maximum(w[:, 0:128], w[:, 128:256]), w[:, 256:384])
    rows_ref[own, :] = jnp.maximum(rows_ref[own, :], peak)
    full = w_ref[pl.ds(pl.multiple_of(64 * parity, 64), 128), :].astype(jnp.float32).T
    half = w_ref[pl.ds(pl.multiple_of(128 * (1 - parity), 64), 64), :].astype(jnp.float32)
    twice = jnp.concatenate([half, half], axis=0).T
    for peer in range(8):
        upper = twice[48 * peer : 48 * peer + 24]
        lower = twice[48 * peer + 24 : 48 * peer + 48]
        page = jnp.concatenate([full[48 * peer : 48 * peer + 48], jnp.where(first, upper, lower)], axis=0)
        page_ref[peer] = page.astype(jnp.bfloat16)

    @pl.when(step == pl.num_programs(0) - 1)
    def _():
        for block in range(3):
            peak_ref[block : block + 1, :] = jnp.max(rows_ref[pl.ds(128 * block, 128), :].T, axis=0, keepdims=True)
        peak_ref[3:8, :] = jnp.zeros((5, 128), jnp.float32)


def stats_kernel(peak_ref, acts_ref, page_ref):
    page_ref[8:16, :] = peak_ref[...]
    for block in range(4):
        total = jnp.zeros((128, 128), jnp.float32)
        square = jnp.zeros((128, 128), jnp.float32)
        for tile in range(12):
            x = acts_ref[pl.ds(128 * block, 128), pl.ds(128 * tile, 128)].astype(jnp.float32)
            total = total + x
            square = square + x * x
        page_ref[block : block + 1, :] = jnp.sum(total.T, axis=0, keepdims=True)
        page_ref[4 + block : 5 + block, :] = jnp.sum(square.T, axis=0, keepdims=True)


def moments(sums):
    mean = sums[0:4] / D
    var = sums[4:8] / D - mean * mean
    rstd = lax.rsqrt(var + EPS)
    return jnp.concatenate([mean, rstd], axis=0).T


def act_kernel(lengths_ref, sums_ref, acts_ref, gain_ref, bias_ref, page_ref):
    columns = moments(sums_ref[...])
    place = lax.broadcasted_iota(jnp.int32, (128, 1), 0)
    for tile in range(12):
        gain = gain_ref[tile : tile + 1, :]
        bias = bias_ref[tile : tile + 1, :]
        peak = jnp.zeros((128, 128), jnp.float32)
        for block in range(4):
            x = acts_ref[pl.ds(128 * block, 128), pl.ds(128 * tile, 128)].astype(jnp.float32)
            normed = (x - columns[:, block : block + 1]) * columns[:, 4 + block : 5 + block] * gain + bias
            valid = place + 128 * (block % 2) < lengths_ref[block // 2]
            peak = jnp.maximum(peak, jnp.where(valid, jnp.abs(normed), 0.0))
        page_ref[tile : tile + 1, :] = jnp.max(peak, axis=0, keepdims=True)
    page_ref[12:15, :] = sums_ref[8:11, :]
    page_ref[15:16, :] = jnp.zeros((1, 128), jnp.float32)


def peak_kernel(place_ref, maxima_ref, sums_ref, acts_ref, gain_ref, bias_ref, page_ref):
    columns = moments(sums_ref[...])
    act = jnp.max(maxima_ref[:, 0:12, :], axis=0)
    for slot in range(4):
        page_ref[0, 3 * slot : 3 * slot + 3, :] = maxima_ref[4 * place_ref[1] + slot, 12:15, :]
    scale = jnp.sqrt(act + EPS) / jnp.sqrt(page_ref[0, 0:12, :] + EPS)
    page_ref[0, 0:12, :] = scale
    inverse = 1.0 / scale
    for block in range(4):
        peak = jnp.zeros((128, 128), jnp.float32)
        for tile in range(12):
            x = acts_ref[pl.ds(128 * block, 128), pl.ds(128 * tile, 128)].astype(jnp.float32)
            gain = gain_ref[tile : tile + 1, :]
            bias = bias_ref[tile : tile + 1, :]
            normed = (x - columns[:, block : block + 1]) * columns[:, 4 + block : 5 + block] * gain + bias
            peak = jnp.maximum(peak, jnp.abs(normed) * inverse[tile : tile + 1])
        page_ref[0, 12 + block : 13 + block, :] = jnp.max(peak.T, axis=0, keepdims=True)
    page = page_ref[0]
    for peer in range(1, page_ref.shape[0]):
        page_ref[peer] = page


def serve_kernel(place_ref, lengths_ref, blocks_ref, pages_ref, served_ref, scale_ref, tok_ref):
    step = pl.program_id(0)

    @pl.when(step == 0)
    def _():
        scale_ref[...] = blocks_ref[place_ref[1], 0:12, :]
        peaks = jnp.max(blocks_ref[:, 12:16, :], axis=0)
        lane = lax.broadcasted_iota(jnp.int32, (1, 128), 1)
        for block in range(4):
            valid = lane + 128 * (block % 2) < lengths_ref[block // 2]
            tok_ref[block : block + 1, :] = jnp.where(valid, peaks[block : block + 1], 0.0)

    low = lax.broadcasted_iota(jnp.int32, (24, 128), 1) < 64
    for pair in range(8):
        even = pages_ref[2 * pair].astype(jnp.float32)
        odd = pages_ref[2 * pair + 1].astype(jnp.float32)
        upper = jnp.where(low, even[48:72], odd[48:72])
        lower = pltpu.roll(jnp.where(low, odd[48:72], even[48:72]), 64, 1)
        middle = jnp.concatenate([upper, lower], axis=0)
        for part, tile in enumerate((even[0:48], middle, odd[0:48])):
            row = 3 * pair + part
            scale = blocks_ref[2 * step + row // 12, row % 12 : row % 12 + 1, :]
            served_ref[:, pl.ds(128 * row, 128)] = (tile * scale).astype(jnp.bfloat16)


def swap(x, axis, bit):
    size = lax.axis_size(axis)
    return lax.ppermute(x, axis, [(i, i ^ bit) for i in range(size)])


def body(acts, lengths, ln_gain, ln_bias, w_fc1):
    dp_place = lax.axis_index("dp")
    mp_place = lax.axis_index("mp")
    place = jnp.stack([dp_place, mp_place]).astype(jnp.int32)
    gain = ln_gain.reshape(12, 128)
    bias = ln_bias.reshape(12, 128)
    whole = lambda *shape: pl.BlockSpec(shape, lambda step: (0,) * len(shape))
    with jax.named_scope("weight_exchange"):
        packed, w_peak = pl.pallas_call(
            pack_kernel,
            grid=(8,),
            out_shape=(
                jax.ShapeDtypeStruct((64, 72, 128), jnp.bfloat16),
                jax.ShapeDtypeStruct((8, 128), jnp.float32),
            ),
            in_specs=[SMEM_SPEC, pl.BlockSpec((192, 384), lambda step: (0, step))],
            out_specs=(pl.BlockSpec((8, 72, 128), lambda step: (step, 0, 0)), whole(8, 128)),
            scratch_shapes=[pltpu.VMEM((384, 128), jnp.float32)],
            compiler_params=params(60),
        )(place, w_fc1)
        pages = lax.all_to_all(packed, "dp", 0, 0, tiled=True)
    with jax.named_scope("token_moments"):
        sums = pl.pallas_call(
            stats_kernel,
            out_shape=jax.ShapeDtypeStruct((16, 128), jnp.float32),
            in_specs=[VMEM_SPEC, VMEM_SPEC],
            out_specs=VMEM_SPEC,
            compiler_params=params(),
        )(w_peak, acts)
        added = lax.broadcasted_iota(jnp.int32, (16, 128), 0) < 8
        for bit in (1, 2, 4):
            other = swap(sums, "mp", bit)
            sums = jnp.where(added, sums + other, jnp.maximum(sums, other))
    with jax.named_scope("channel_maxima"):
        maxima = pl.pallas_call(
            act_kernel,
            out_shape=jax.ShapeDtypeStruct((16, 128), jnp.float32),
            in_specs=[SMEM_SPEC] + [VMEM_SPEC] * 4,
            out_specs=VMEM_SPEC,
            compiler_params=params(),
        )(lengths, sums, acts, gain, bias)
        maxima = jnp.maximum(maxima, swap(maxima, "dp", 1))
        maxima, pages = lax.optimization_barrier((maxima, pages))
        copies = jnp.broadcast_to(maxima[None], (32, 16, 128))
        kinds = [[2 * chip + core for chip in range(32)] for core in range(2)]
        maxima = lax.all_to_all(copies, "dp", 0, 0, axis_index_groups=kinds, tiled=True)
    with jax.named_scope("token_peaks"):
        page = pl.pallas_call(
            peak_kernel,
            out_shape=jax.ShapeDtypeStruct((8, 16, 128), jnp.float32),
            in_specs=[SMEM_SPEC] + [VMEM_SPEC] * 5,
            out_specs=VMEM_SPEC,
            compiler_params=params(),
        )(place, maxima, sums, acts, gain, bias)
        blocks = lax.all_to_all(page, "mp", 0, 0, tiled=True)
    with jax.named_scope("smoothed_weight"):
        served, scale, tok = pl.pallas_call(
            serve_kernel,
            grid=(4,),
            out_shape=(
                jax.ShapeDtypeStruct((48, D), jnp.bfloat16),
                jax.ShapeDtypeStruct((12, 128), jnp.float32),
                jax.ShapeDtypeStruct((4, 128), jnp.float32),
            ),
            in_specs=[SMEM_SPEC, SMEM_SPEC, whole(8, 16, 128), pl.BlockSpec((16, 72, 128), lambda step: (step, 0, 0))],
            out_specs=(pl.BlockSpec((48, 3072), lambda step: (0, step)), whole(12, 128), whole(4, 128)),
            compiler_params=params(),
        )(place, lengths, blocks, pages)
    return served, scale.reshape(1536), tok.reshape(512)


def solution(mesh):
    return jax.shard_map(
        body,
        mesh=mesh,
        in_specs=(P("dp", "mp"), P("dp"), P("mp"), P("mp"), P("dp", "mp")),
        out_specs=(P(("mp", "dp"), None), P("mp"), P("dp")),
        check_vma=False,
    )
```

time: 103 us -> 92.6 us (0.90)
  the two profiles are of different devices: /device:TPU:16 before, /device:TPU:1 now
where the time goes in v3:
time: 92.6 us; the launch traced here: 91 us
  blocking collectives  32.9 us (36%)
  starting transfers between devices  30.9 us (33%)
  waiting for transfers between devices  13.7 us (15%)
  Pallas kernels  11.9 us (13%)
    all_to_all x1, blocking collectives, body(): lax.all_to_all(copies, 'dp', 0, 0, axis_index_groups=kinds, tiled=True)  17.8 us
    all_to_all x1, starting transfers between devices, body(): pages = lax.all_to_all(packed, 'dp', 0, 0, tiled=True)  15.5 us
    ppermute x4, starting transfers between devices, swap(): return lax.ppermute(x, axis, [(i, i ^ bit) for i in range(size)])  15.3 us
    all_to_all x1, blocking collectives, body(): blocks = lax.all_to_all(page, 'mp', 0, 0, tiled=True)  15.2 us
    ppermute x4, waiting for transfers between devices, swap(): return lax.ppermute(x, axis, [(i, i ^ bit) for i in range(size)])  10.2 us
    pallas_call x1, Pallas kernels, body(): pl.pallas_call(pack_kernel, grid=(8,), out_shape=(jax.ShapeDtypeStruct((6...  5.93 us
    all_to_all x1, waiting for transfers between devices, body(): pages = lax.all_to_all(packed, 'dp', 0, 0, tiled=True)  3.47 us
    pallas_call x1, Pallas kernels, body(): pl.pallas_call(serve_kernel, grid=(4,), out_shape=(jax.ShapeDtypeStruct((...  2.35 us
  transfers between devices with their start and end apart: 5, of which 5 were waited for; matrix products, arithmetic and copies ran while one was open for 0% of the time, Pallas kernels for 2%

profile of v3, /device:TPU:1, one launch (start us, length us, event | category | flops | bytes accessed | tf_op | source)
XLA Modules:
  0.0 91.0 jit_solution(5339612839346140913)
XLA Ops:
  0.6 0.6 pad_add_fusion.place_ref
  1.2 5.9 %weight_exchange.1 = (bf16[64,72,128]{2,1,0:T(8,128)(2,1)}, f32[8,128]{1,0:T(8,128)}) custom-call(s32[2]{0:T(128)} %pad_add_fusion.place_ref, bf16[192,3072]{1,0:T(8,128)(2,1)} %w_ref.1), custom_call_target="tpu_custom_call" | custom-call | tf_op jit(solution)/shard_map/weight_exchange/pallas_call | solution.py:146
  7.2 0.0 copy-start
  7.2 0.0 copy-start.4
  7.2 15.5 %all-to-all-start = ((bf16[64,72,128]{2,1,0:T(8,128)(2,1)}), bf16[64,72,128]{2,1,0:T(8,128)(2,1)S(1)}, u32[]{:S(2)}, u32[]{:S(2)}) async-start(bf16[64,72,128]{2,1,0:T(8,128)(2,1)} %get-tuple-element.11), calls=%async_computation | async-start | bytes 2359296 | tf_op jit(solution)/shard_map/weight_exchange/all_to_all | solution.py:158
  22.7 0.0 copy-start.1
  22.7 0.0 copy-start.2
  22.7 0.0 copy-start.5
  22.7 0.0 copy-done
  22.8 0.0 copy-done.4
  22.8 0.5 token_moments.1
  23.2 3.1 %collective-permute-start = (f32[16,128]{1,0:T(8,128)S(1)}, f32[16,128]{1,0:T(8,128)S(1)}, u32[]{:S(2)}, u32[]{:S(2)}) collective-permute-start(f32[16,128]{1,0:T(8,128)S(1)} %token_moments.1), channel_id=1, source_target_pairs={{0,1},{1,0},{2,3},{3,2},{4,5},{5,4},{6,7},{7,6},{8,9},{9,8},{10,11... | collective-permute-start | bytes 24584 | tf_op jit(solution)/shard_map/token_moments/ppermute | solution.py:135
  26.4 1.6 %collective-permute-done = f32[16,128]{1,0:T(8,128)S(1)} collective-permute-done((f32[16,128]{1,0:T(8,128)S(1)}, f32[16,128]{1,0:T(8,128)S(1)}, u32[]{:S(2)}, u32[]{:S(2)}) %collective-permute-start) | collective-permute-done | bytes 8224 | tf_op jit(solution)/shard_map/token_moments/ppermute | solution.py:135
  27.9 0.1 maximum_select_fusion.2
  28.0 4.6 %collective-permute-start.1 = (f32[16,128]{1,0:T(8,128)S(1)}, f32[16,128]{1,0:T(8,128)S(1)}, u32[]{:S(2)}, u32[]{:S(2)}) collective-permute-start(f32[16,128]{1,0:T(8,128)S(1)} %maximum_select_fusion.2), channel_id=1, source_target_pairs={{0,2},{1,3},{2,0},{3,1},{4,6},{5,7},{6,4},{7,5},{8,10},{9,11},{10,... | collective-permute-start | bytes 24584 | tf_op jit(solution)/shard_map/token_moments/ppermute | solution.py:135
  32.7 1.5 %collective-permute-done.1 = f32[16,128]{1,0:T(8,128)S(1)} collective-permute-done((f32[16,128]{1,0:T(8,128)S(1)}, f32[16,128]{1,0:T(8,128)S(1)}, u32[]{:S(2)}, u32[]{:S(2)}) %collective-permute-start.1) | collective-permute-done | bytes 8224 | tf_op jit(solution)/shard_map/token_moments/ppermute | solution.py:135
  34.2 0.1 maximum_select_fusion.1
  34.3 4.7 %collective-permute-start.2 = (f32[16,128]{1,0:T(8,128)S(1)}, f32[16,128]{1,0:T(8,128)S(1)}, u32[]{:S(2)}, u32[]{:S(2)}) collective-permute-start(f32[16,128]{1,0:T(8,128)S(1)} %maximum_select_fusion.1), channel_id=1, source_target_pairs={{0,4},{1,5},{2,6},{3,7},{4,0},{5,1},{6,2},{7,3},{8,12},{9,13},{10,... | collective-permute-start | bytes 24584 | tf_op jit(solution)/shard_map/token_moments/ppermute | solution.py:135
  39.0 6.3 %collective-permute-done.2 = f32[16,128]{1,0:T(8,128)S(1)} collective-permute-done((f32[16,128]{1,0:T(8,128)S(1)}, f32[16,128]{1,0:T(8,128)S(1)}, u32[]{:S(2)}, u32[]{:S(2)}) %collective-permute-start.2) | collective-permute-done | bytes 8224 | tf_op jit(solution)/shard_map/token_moments/ppermute | solution.py:135
  45.3 0.1 maximum_select_fusion.sums_ref
  45.4 0.0 copy-done.1
  45.4 0.0 copy-done.2
  45.4 0.0 copy-done.5
  45.4 0.0 copy-start.3
  45.4 1.6 %channel_maxima.1 = f32[16,128]{1,0:T(8,128)S(1)} custom-call(s32[2]{0:T(128)S(1)} %copy-done.5, f32[16,128]{1,0:T(8,128)S(1)} %maximum_select_fusion.sums_ref, bf16[512,1536]{1,0:T(8,128)(2,1)S(1)} %copy-done, f32[12,128]{1,0:T(8,128)S(1)} %bitcast.6, f32[12,128]{1,0:T(8,128)S(1)} %bitcast.8), custom_call_target="tpu_custom_call" | custom-call | tf_op jit(solution)/shard_map/channel_maxima/pallas_call | solution.py:172
  47.0 2.8 %collective-permute-start.3 = (f32[16,128]{1,0:T(8,128)S(1)}, f32[16,128]{1,0:T(8,128)S(1)}, u32[]{:S(2)}, u32[]{:S(2)}) collective-permute-start(f32[16,128]{1,0:T(8,128)S(1)} %channel_maxima.1), channel_id=1, source_target_pairs={{0,8},{8,0},{16,24},{24,16},{32,40},{40,32},{48,56},{56,48},{64,72... | collective-permute-start | bytes 24584 | tf_op jit(solution)/shard_map/channel_maxima/ppermute | solution.py:135
  49.9 0.8 collective-permute-done.3
  50.7 3.5 %all-to-all-done.pages_ref = bf16[64,72,128]{2,1,0:T(8,128)(2,1)S(1)} async-done(((bf16[64,72,128]{2,1,0:T(8,128)(2,1)}), bf16[64,72,128]{2,1,0:T(8,128)(2,1)S(1)}, u32[]{:S(2)}, u32[]{:S(2)}) %all-to-all-start) | async-done | bytes 1179680 | tf_op jit(solution)/shard_map/weight_exchange/all_to_all | solution.py:158
  54.2 17.8 %all_to_all.15.maxima_ref = f32[32,16,128]{2,1,0:T(8,128)S(1)} all-to-all(f32[32,16,128]{2,1,0:T(8,128)S(1)} %broadcast_in_dim.2), channel_id=1, replica_groups={{0,16,32,48,64,80,96,112,128,144,160,176,192,208,224,240,256,272,288,30..., dimensions={0} | all-to-all | bytes 524288 | tf_op jit(solution)/shard_map/channel_maxima/all_to_all | solution.py:183
  71.9 0.0 copy-done.3
  71.9 1.6 %token_peaks.1 = f32[8,16,128]{2,1,0:T(8,128)S(1)} custom-call(s32[2]{0:T(128)S(1)} %copy-done.3, f32[32,16,128]{2,1,0:T(8,128)S(1)} %all_to_all.15.maxima_ref, f32[16,128]{1,0:T(8,128)S(1)} %maximum_select_fusion.sums_ref, bf16[512,1536]{1,0:T(8,128)(2,1)S(1)} %copy-done, f32[12,128]{1,0:T(8,128)S(1)} %bitcast.7, f32[12,128]{1,0:T(8,128)S(1)} %bitcast.9), custom_call_target="tpu_custom_call" | custom-call | tf_op jit(solution)/shard_map/token_peaks/pallas_call | solution.py:185
  73.5 15.2 %all_to_all.16.blocks_ref = f32[8,16,128]{2,1,0:T(8,128)S(1)} all-to-all(f32[8,16,128]{2,1,0:T(8,128)S(1)} %token_peaks.1), channel_id=1, replica_groups=mesh['dp'=64,'mp'=8] {'mp'}, dimensions={0} | all-to-all | bytes 131072 | tf_op jit(solution)/shard_map/token_peaks/all_to_all | solution.py:192
  88.7 2.3 %smoothed_weight.1 = (bf16[48,12288]{1,0:T(8,128)(2,1)}, f32[12,128]{1,0:T(8,128)}, f32[4,128]{1,0:T(4,128)}) custom-call(s32[2]{0:T(128)S(1)} %copy-done.3, s32[2]{0:T(128)S(1)} %copy-done.5, f32[8,16,128]{2,1,0:T(8,128)S(1)} %all_to_all.16.blocks_ref, bf16[64,72,128]{2,1,0:T(8,128)(2,1)S(1)} %all-to-all-done.pages_ref), custom_call_target="tpu_custom_call" | custom-call | tf_op jit(solution)/shard_map/smoothed_weight/pallas_call | solution.py:194
  (3 shorter events, 0.0 us)
Async XLA Ops:
  7.2 15.6 %copy-start = (bf16[512,1536]{1,0:T(8,128)(2,1)S(1)}, bf16[512,1536]{1,0:T(8,128)(2,1)}, u32[]{:S(2)}) copy-start(bf16[512,1536]{1,0:T(8,128)(2,1)} %acts_ref.5) | copy-start | bytes 4718596
  7.2 15.6 %copy-start.4 = (f32[8,128]{1,0:T(8,128)S(1)}, f32[8,128]{1,0:T(8,128)}, u32[]{:S(2)}) copy-start(f32[8,128]{1,0:T(8,128)} %get-tuple-element.10.peak_ref) | copy-start | bytes 12292
  7.2 47.0 %all-to-all-start = ((bf16[64,72,128]{2,1,0:T(8,128)(2,1)}), bf16[64,72,128]{2,1,0:T(8,128)(2,1)S(1)}, u32[]{:S(2)}, u32[]{:S(2)}) async-start(bf16[64,72,128]{2,1,0:T(8,128)(2,1)} %get-tuple-element.11), calls=%async_computation | async-start | bytes 2359296 | tf_op jit(solution)/shard_map/weight_exchange/all_to_all | solution.py:158
  22.7 22.7 %copy-start.1 = (f32[1536]{0:T(1024)S(1)}, f32[1536]{0:T(1024)}, u32[]{:S(2)}) copy-start(f32[1536]{0:T(1024)} %param.7) | copy-start | bytes 18436
  22.7 22.7 %copy-start.2 = (f32[1536]{0:T(1024)S(1)}, f32[1536]{0:T(1024)}, u32[]{:S(2)}) copy-start(f32[1536]{0:T(1024)} %param.8) | copy-start | bytes 18436
  22.7 22.7 %copy-start.5 = (s32[2]{0:T(128)S(1)}, s32[2]{0:T(128)}, u32[]{:S(2)}) copy-start(s32[2]{0:T(128)} %lengths_ref.3) | copy-start | bytes 28
  23.2 4.7 %collective-permute-start = (f32[16,128]{1,0:T(8,128)S(1)}, f32[16,128]{1,0:T(8,128)S(1)}, u32[]{:S(2)}, u32[]{:S(2)}) collective-permute-start(f32[16,128]{1,0:T(8,128)S(1)} %token_moments.1), channel_id=1, source_target_pairs={{0,1},{1,0},{2,3},{3,2},{4,5},{5,4},{6,7},{7,6},{8,9},{9,8},{10,11... | collective-permute-start | bytes 24584 | tf_op jit(solution)/shard_map/token_moments/ppermute | solution.py:135
  28.0 6.2 %collective-permute-start.1 = (f32[16,128]{1,0:T(8,128)S(1)}, f32[16,128]{1,0:T(8,128)S(1)}, u32[]{:S(2)}, u32[]{:S(2)}) collective-permute-start(f32[16,128]{1,0:T(8,128)S(1)} %maximum_select_fusion.2), channel_id=1, source_target_pairs={{0,2},{1,3},{2,0},{3,1},{4,6},{5,7},{6,4},{7,5},{8,10},{9,11},{10,... | collective-permute-start | bytes 24584 | tf_op jit(solution)/shard_map/token_moments/ppermute | solution.py:135
  34.3 11.1 %collective-permute-start.2 = (f32[16,128]{1,0:T(8,128)S(1)}, f32[16,128]{1,0:T(8,128)S(1)}, u32[]{:S(2)}, u32[]{:S(2)}) collective-permute-start(f32[16,128]{1,0:T(8,128)S(1)} %maximum_select_fusion.1), channel_id=1, source_target_pairs={{0,4},{1,5},{2,6},{3,7},{4,0},{5,1},{6,2},{7,3},{8,12},{9,13},{10,... | collective-permute-start | bytes 24584 | tf_op jit(solution)/shard_map/token_moments/ppermute | solution.py:135
  45.4 26.5 %copy-start.3 = (s32[2]{0:T(128)S(1)}, s32[2]{0:T(128)}, u32[]{:S(2)}) copy-start(s32[2]{0:T(128)} %pad_add_fusion.place_ref) | copy-start | bytes 28
  47.0 3.6 %collective-permute-start.3 = (f32[16,128]{1,0:T(8,128)S(1)}, f32[16,128]{1,0:T(8,128)S(1)}, u32[]{:S(2)}, u32[]{:S(2)}) collective-permute-start(f32[16,128]{1,0:T(8,128)S(1)} %channel_maxima.1), channel_id=1, source_target_pairs={{0,8},{8,0},{16,24},{24,16},{32,40},{40,32},{48,56},{56,48},{64,72... | collective-permute-start | bytes 24584 | tf_op jit(solution)/shard_map/channel_maxima/ppermute | solution.py:135

commit v4 on v3

v4 whole, which is shorter than its diff:
```python
import jax
import jax.numpy as jnp
from jax import lax
from jax.experimental import pallas as pl
from jax.experimental.pallas import tpu as pltpu
from jax.sharding import PartitionSpec as P

D = 12288
SLOT = 256
EPS = 1e-05
VMEM_SPEC = pl.BlockSpec(memory_space=pltpu.VMEM)
SMEM_SPEC = pl.BlockSpec(memory_space=pltpu.SMEM)
ANY_SPEC = pl.BlockSpec(memory_space=pl.ANY)


def params(mebibytes=40):
    return pltpu.CompilerParams(vmem_limit_bytes=mebibytes * 1024 * 1024)


def pack_kernel(w_hbm, page_hbm, peak_ref, w_ref, page_ref, rows_ref, in_sems, out_sems):
    parity = lax.axis_index("dp") % 2
    low = lax.broadcasted_iota(jnp.int32, (24, 128), 1) < 64
    first = low == (parity == 0)
    own = pl.ds(pl.multiple_of(192 * parity, 64), 192)

    def columns(step):
        return pl.ds(pl.multiple_of(384 * step, 128), 384)

    def fetch(step):
        return pltpu.make_async_copy(w_hbm.at[:, columns(step)], w_ref.at[:, columns(step)], in_sems.at[step])

    def store(step):
        peers = pl.ds(8 * step, 8)
        return pltpu.make_async_copy(page_ref.at[peers], page_hbm.at[peers], out_sems.at[step])

    for step in range(8):
        fetch(step).start()
    rows_ref[...] = jnp.zeros_like(rows_ref)

    def pack(step, carry):
        fetch(step).wait()
        w = jnp.abs(w_ref[:, columns(step)].astype(jnp.float32))
        peak = jnp.maximum(jnp.maximum(w[:, 0:128], w[:, 128:256]), w[:, 256:384])
        rows_ref[own, :] = jnp.maximum(rows_ref[own, :], peak)
        full = w_ref[pl.ds(pl.multiple_of(64 * parity, 64), 128), columns(step)].astype(jnp.float32).T
        half = w_ref[pl.ds(pl.multiple_of(128 * (1 - parity), 64), 64), columns(step)].astype(jnp.float32)
        twice = jnp.concatenate([half, half], axis=0).T
        for peer in range(8):
            upper = twice[48 * peer : 48 * peer + 24]
            lower = twice[48 * peer + 24 : 48 * peer + 48]
            page = jnp.concatenate([full[48 * peer : 48 * peer + 48], jnp.where(first, upper, lower)], axis=0)
            page_ref[8 * step + peer] = page.astype(jnp.bfloat16)
        store(step).start()
        return carry

    lax.fori_loop(0, 8, pack, 0)
    for block in range(3):
        peak_ref[block : block + 1, :] = jnp.max(rows_ref[pl.ds(128 * block, 128), :].T, axis=0, keepdims=True)
    peak_ref[3:8, :] = jnp.zeros((5, 128), jnp.float32)
    for step in range(8):
        store(step).wait()


def stats_kernel(peak_ref, acts_ref, page_ref):
    page_ref[8:16, :] = peak_ref[...]
    for block in range(4):
        total = jnp.zeros((128, 128), jnp.float32)
        square = jnp.zeros((128, 128), jnp.float32)
        for tile in range(12):
            x = acts_ref[pl.ds(128 * block, 128), pl.ds(128 * tile, 128)].astype(jnp.float32)
            total = total + x
            square = square + x * x
        page_ref[block : block + 1, :] = jnp.sum(total.T, axis=0, keepdims=True)
        page_ref[4 + block : 5 + block, :] = jnp.sum(square.T, axis=0, keepdims=True)


def moments(sums):
    mean = sums[0:4] / D
    var = sums[4:8] / D - mean * mean
    rstd = lax.rsqrt(var + EPS)
    return jnp.concatenate([mean, rstd], axis=0).T


def act_kernel(lengths_ref, sums_ref, acts_ref, gain_ref, bias_ref, page_ref):
    columns = moments(sums_ref[...])
    place = lax.broadcasted_iota(jnp.int32, (128, 128), 0)
    peaks = [jnp.zeros((8, 128), jnp.float32)] * 12
    for block in range(4):
        mean = jnp.broadcast_to(columns[:, block : block + 1], (128, 128))
        rstd = jnp.broadcast_to(columns[:, 4 + block : 5 + block], (128, 128))
        valid = place + 128 * (block % 2) < lengths_ref[block // 2]
        for tile in range(12):
            x = acts_ref[pl.ds(128 * block, 128), pl.ds(128 * tile, 128)].astype(jnp.float32)
            normed = (x - mean) * rstd * gain_ref[tile : tile + 1, :] + bias_ref[tile : tile + 1, :]
            peak = jnp.where(valid, jnp.abs(normed), 0.0)
            peaks[tile] = jnp.maximum(peaks[tile], jnp.max(peak.reshape(16, 8, 128), axis=0))
    for tile in range(12):
        page_ref[tile : tile + 1, :] = jnp.max(peaks[tile], axis=0, keepdims=True)
    kept = lax.axis_index("dp") // 8 == lax.axis_index("mp")
    page_ref[12:15, :] = jnp.where(kept, sums_ref[8:11, :], 0.0)
    page_ref[15:16, :] = jnp.zeros((1, 128), jnp.float32)


def peak_kernel(maxima_ref, sums_ref, acts_ref, gain_ref, bias_ref, page_ref):
    columns = moments(sums_ref[...])
    start = 4 * (lax.axis_index("mp") // 2)
    act = jnp.max(maxima_ref[:, 0:12, :], axis=0)
    for slot in range(4):
        page_ref[0, 3 * slot : 3 * slot + 3, :] = maxima_ref[start + slot, 12:15, :]
    scale = jnp.sqrt(act + EPS) / jnp.sqrt(page_ref[0, 0:12, :] + EPS)
    page_ref[0, 0:12, :] = scale
    inverse = 1.0 / scale
    gain = gain_ref[...] * inverse
    bias = bias_ref[...] * inverse
    for block in range(4):
        mean = jnp.broadcast_to(columns[:, block : block + 1], (128, 128))
        rstd = jnp.broadcast_to(columns[:, 4 + block : 5 + block], (128, 128))
        peak = jnp.zeros((128, 128), jnp.float32)
        for tile in range(12):
            x = acts_ref[pl.ds(128 * block, 128), pl.ds(128 * tile, 128)].astype(jnp.float32)
            smoothed = (x - mean) * rstd * gain[tile : tile + 1] + bias[tile : tile + 1]
            peak = jnp.maximum(peak, jnp.abs(smoothed))
        page_ref[0, 12 + block : 13 + block, :] = jnp.max(peak.T, axis=0, keepdims=True)
    page = page_ref[0]
    for peer in range(1, page_ref.shape[0]):
        page_ref[peer] = page


def serve_kernel(lengths_ref, blocks_ref, pages_ref, served_hbm, scale_ref, tok_ref, served_ref, sems):
    low = lax.broadcasted_iota(jnp.int32, (24, 128), 1) < 64

    def store(step):
        columns = pl.ds(pl.multiple_of(3072 * step, 128), 3072)
        return pltpu.make_async_copy(served_ref.at[:, columns], served_hbm.at[:, columns], sems.at[step])

    for step in range(4):
        for pair in range(8 * step, 8 * step + 8):
            even = pages_ref[2 * pair].astype(jnp.float32)
            odd = pages_ref[2 * pair + 1].astype(jnp.float32)
            upper = jnp.where(low, even[48:72], odd[48:72])
            lower = pltpu.roll(jnp.where(low, odd[48:72], even[48:72]), 64, 1)
            middle = jnp.concatenate([upper, lower], axis=0)
            for part, tile in enumerate((even[0:48], middle, odd[0:48])):
                row = 3 * pair + part
                scale = blocks_ref[row // 12, row % 12 : row % 12 + 1, :]
                served_ref[:, pl.ds(128 * row, 128)] = (tile * scale).astype(jnp.bfloat16)
        store(step).start()
    scale_ref[...] = blocks_ref[lax.axis_index("mp"), 0:12, :]
    peaks = jnp.max(blocks_ref[:, 12:16, :], axis=0)
    lane = lax.broadcasted_iota(jnp.int32, (1, 128), 1)
    for block in range(4):
        valid = lane + 128 * (block % 2) < lengths_ref[block // 2]
        tok_ref[block : block + 1, :] = jnp.where(valid, peaks[block : block + 1], 0.0)
    for step in range(4):
        store(step).wait()


def swap(x, axis, bit):
    size = lax.axis_size(axis)
    return lax.ppermute(x, axis, [(i, i ^ bit) for i in range(size)])


def body(acts, lengths, ln_gain, ln_bias, w_fc1):
    gain = ln_gain.reshape(12, 128)
    bias = ln_bias.reshape(12, 128)
    with jax.named_scope("weight_exchange"):
        packed, w_peak = pl.pallas_call(
            pack_kernel,
            out_shape=(
                jax.ShapeDtypeStruct((64, 72, 128), jnp.bfloat16),
                jax.ShapeDtypeStruct((8, 128), jnp.float32),
            ),
            in_specs=[ANY_SPEC],
            out_specs=(ANY_SPEC, VMEM_SPEC),
            scratch_shapes=[
                pltpu.VMEM((192, 3072), jnp.bfloat16),
                pltpu.VMEM((64, 72, 128), jnp.bfloat16),
                pltpu.VMEM((384, 128), jnp.float32),
                pltpu.SemaphoreType.DMA((8,)),
                pltpu.SemaphoreType.DMA((8,)),
            ],
            compiler_params=params(60),
        )(w_fc1)
        pages = lax.all_to_all(packed, "dp", 0, 0, tiled=True)
    with jax.named_scope("token_moments"):
        sums = pl.pallas_call(
            stats_kernel,
            out_shape=jax.ShapeDtypeStruct((16, 128), jnp.float32),
            in_specs=[VMEM_SPEC, VMEM_SPEC],
            out_specs=VMEM_SPEC,
            compiler_params=params(),
        )(w_peak, acts)
        added = lax.broadcasted_iota(jnp.int32, (16, 128), 0) < 8
        for bit in (1, 2, 4):
            other = swap(sums, "mp", bit)
            sums = jnp.where(added, sums + other, jnp.maximum(sums, other))
    with jax.named_scope("channel_maxima"):
        maxima = pl.pallas_call(
            act_kernel,
            out_shape=jax.ShapeDtypeStruct((16, 128), jnp.float32),
            in_specs=[SMEM_SPEC] + [VMEM_SPEC] * 4,
            out_specs=VMEM_SPEC,
            compiler_params=params(),
        )(lengths, sums, acts, gain, bias)
        for bit in (1, 8):
            maxima = jnp.maximum(maxima, swap(maxima, "dp", bit))
        maxima, pages = lax.optimization_barrier((maxima, pages))
        copies = jnp.broadcast_to(maxima[None], (16, 16, 128))
        kinds = [[16 * pair + 8 * plane + 2 * y + core for pair in range(4) for y in range(4)] for plane in (0, 1) for core in (0, 1)]
        maxima = lax.all_to_all(copies, "dp", 0, 0, axis_index_groups=kinds, tiled=True)
    with jax.named_scope("token_peaks"):
        page = pl.pallas_call(
            peak_kernel,
            out_shape=jax.ShapeDtypeStruct((8, 16, 128), jnp.float32),
            in_specs=[VMEM_SPEC] * 5,
            out_specs=VMEM_SPEC,
            compiler_params=params(),
        )(maxima, sums, acts, gain, bias)
        blocks = lax.all_to_all(page, "mp", 0, 0, tiled=True)
    with jax.named_scope("smoothed_weight"):
        served, scale, tok = pl.pallas_call(
            serve_kernel,
            out_shape=(
                jax.ShapeDtypeStruct((48, D), jnp.bfloat16),
                jax.ShapeDtypeStruct((12, 128), jnp.float32),
                jax.ShapeDtypeStruct((4, 128), jnp.float32),
            ),
            in_specs=[SMEM_SPEC, VMEM_SPEC, VMEM_SPEC],
            out_specs=(ANY_SPEC, VMEM_SPEC, VMEM_SPEC),
            scratch_shapes=[pltpu.VMEM((48, D), jnp.bfloat16), pltpu.SemaphoreType.DMA((4,))],
            compiler_params=params(),
        )(lengths, blocks, pages)
    return served, scale.reshape(1536), tok.reshape(512)


def solution(mesh):
    return jax.shard_map(
        body,
        mesh=mesh,
        in_specs=(P("dp", "mp"), P("dp"), P("mp"), P("mp"), P("dp", "mp")),
        out_specs=(P(("mp", "dp"), None), P("mp"), P("dp")),
        check_vma=False,
    )
```

time: 92.6 us -> 91.9 us (level)
  the two profiles are of different devices: /device:TPU:1 before, /device:TPU:2 now
where the time goes in v4:
time: 91.9 us; the launch traced here: 91.5 us
  blocking collectives  36.1 us (39%)
  starting transfers between devices  31.5 us (34%)
  waiting for transfers between devices  14 us (15%)
  Pallas kernels  8.81 us (10%)
    all_to_all x1, blocking collectives, body(): lax.all_to_all(copies, 'dp', 0, 0, axis_index_groups=kinds, tiled=True)  20.5 us
    ppermute x5, starting transfers between devices, swap(): return lax.ppermute(x, axis, [(i, i ^ bit) for i in range(size)])  17 us
    all_to_all x1, blocking collectives, body(): blocks = lax.all_to_all(page, 'mp', 0, 0, tiled=True)  15.7 us
    all_to_all x1, starting transfers between devices, body(): pages = lax.all_to_all(packed, 'dp', 0, 0, tiled=True)  14.5 us
    ppermute x5, waiting for transfers between devices, swap(): return lax.ppermute(x, axis, [(i, i ^ bit) for i in range(size)])  14 us
    pallas_call x1, Pallas kernels, body(): pl.pallas_call(pack_kernel, out_shape=(jax.ShapeDtypeStruct((64, 72, 128)...  3.48 us
    pallas_call x1, Pallas kernels, body(): pl.pallas_call(serve_kernel, out_shape=(jax.ShapeDtypeStruct((48, D), jnp...  2.35 us
  transfers between devices with their start and end apart: 6, of which 5 were waited for; matrix products, arithmetic and copies ran while one was open for 0% of the time, Pallas kernels for 2%

profile of v4, /device:TPU:2, one launch (start us, length us, event | category | flops | bytes accessed | tf_op | source)
XLA Modules:
  0.0 91.5 jit_solution(7782897312182219782)
XLA Ops:
  0.6 3.5 %weight_exchange.1 = (bf16[64,72,128]{2,1,0:T(8,128)(2,1)}, f32[8,128]{1,0:T(8,128)}) custom-call(bf16[192,3072]{1,0:T(8,128)(2,1)} %w_hbm.1), custom_call_target="tpu_custom_call" | custom-call | tf_op jit(solution)/shard_map/weight_exchange/pallas_call | solution.py:167
  4.1 0.0 copy-start
  4.1 0.0 copy-start.3
  4.1 14.5 %all-to-all-start = ((bf16[64,72,128]{2,1,0:T(8,128)(2,1)}), bf16[64,72,128]{2,1,0:T(8,128)(2,1)S(1)}, u32[]{:S(2)}, u32[]{:S(2)}) async-start(bf16[64,72,128]{2,1,0:T(8,128)(2,1)} %get-tuple-element.11), calls=%async_computation | async-start | bytes 2359296 | tf_op jit(solution)/shard_map/weight_exchange/all_to_all | solution.py:184
  18.7 0.0 copy-start.1
  18.7 0.0 copy-start.2
  18.7 0.0 copy-start.4
  18.7 0.0 copy-done
  18.7 0.0 copy-done.3
  18.7 0.5 token_moments.1
  19.2 2.4 %collective-permute-start = (f32[16,128]{1,0:T(8,128)S(1)}, f32[16,128]{1,0:T(8,128)S(1)}, u32[]{:S(2)}, u32[]{:S(2)}) collective-permute-start(f32[16,128]{1,0:T(8,128)S(1)} %token_moments.1), channel_id=1, source_target_pairs={{0,1},{1,0},{2,3},{3,2},{4,5},{5,4},{6,7},{7,6},{8,9},{9,8},{10,11... | collective-permute-start | bytes 24584 | tf_op jit(solution)/shard_map/token_moments/ppermute | solution.py:160
  21.7 3.1 %collective-permute-done = f32[16,128]{1,0:T(8,128)S(1)} collective-permute-done((f32[16,128]{1,0:T(8,128)S(1)}, f32[16,128]{1,0:T(8,128)S(1)}, u32[]{:S(2)}, u32[]{:S(2)}) %collective-permute-start) | collective-permute-done | bytes 8224 | tf_op jit(solution)/shard_map/token_moments/ppermute | solution.py:160
  24.7 0.1 maximum_select_fusion.2
  24.8 4.0 %collective-permute-start.1 = (f32[16,128]{1,0:T(8,128)S(1)}, f32[16,128]{1,0:T(8,128)S(1)}, u32[]{:S(2)}, u32[]{:S(2)}) collective-permute-start(f32[16,128]{1,0:T(8,128)S(1)} %maximum_select_fusion.2), channel_id=1, source_target_pairs={{0,2},{1,3},{2,0},{3,1},{4,6},{5,7},{6,4},{7,5},{8,10},{9,11},{10,... | collective-permute-start | bytes 24584 | tf_op jit(solution)/shard_map/token_moments/ppermute | solution.py:160
  28.8 3.0 %collective-permute-done.1 = f32[16,128]{1,0:T(8,128)S(1)} collective-permute-done((f32[16,128]{1,0:T(8,128)S(1)}, f32[16,128]{1,0:T(8,128)S(1)}, u32[]{:S(2)}, u32[]{:S(2)}) %collective-permute-start.1) | collective-permute-done | bytes 8224 | tf_op jit(solution)/shard_map/token_moments/ppermute | solution.py:160
  31.8 0.1 maximum_select_fusion.1
  31.9 5.0 %collective-permute-start.2 = (f32[16,128]{1,0:T(8,128)S(1)}, f32[16,128]{1,0:T(8,128)S(1)}, u32[]{:S(2)}, u32[]{:S(2)}) collective-permute-start(f32[16,128]{1,0:T(8,128)S(1)} %maximum_select_fusion.1), channel_id=1, source_target_pairs={{0,4},{1,5},{2,6},{3,7},{4,0},{5,1},{6,2},{7,3},{8,12},{9,13},{10,... | collective-permute-start | bytes 24584 | tf_op jit(solution)/shard_map/token_moments/ppermute | solution.py:160
  37.0 4.8 %collective-permute-done.2 = f32[16,128]{1,0:T(8,128)S(1)} collective-permute-done((f32[16,128]{1,0:T(8,128)S(1)}, f32[16,128]{1,0:T(8,128)S(1)}, u32[]{:S(2)}, u32[]{:S(2)}) %collective-permute-start.2) | collective-permute-done | bytes 8224 | tf_op jit(solution)/shard_map/token_moments/ppermute | solution.py:160
  41.8 0.1 maximum_select_fusion.sums_ref
  41.8 0.0 copy-done.1
  41.8 0.0 copy-done.2
  41.8 0.0 copy-done.4
  41.8 1.6 %channel_maxima.1 = f32[16,128]{1,0:T(8,128)S(1)} custom-call(s32[2]{0:T(128)S(1)} %copy-done.4, f32[16,128]{1,0:T(8,128)S(1)} %maximum_select_fusion.sums_ref, bf16[512,1536]{1,0:T(8,128)(2,1)S(1)} %copy-done, f32[12,128]{1,0:T(8,128)S(1)} %bitcast.4, f32[12,128]{1,0:T(8,128)S(1)} %bitcast.6), custom_call_target="tpu_custom_call" | custom-call | tf_op jit(solution)/shard_map/channel_maxima/pallas_call | solution.py:198
  43.4 1.9 %collective-permute-start.3 = (f32[16,128]{1,0:T(8,128)S(1)}, f32[16,128]{1,0:T(8,128)S(1)}, u32[]{:S(2)}, u32[]{:S(2)}) collective-permute-start(f32[16,128]{1,0:T(8,128)S(1)} %channel_maxima.1), channel_id=1, source_target_pairs={{0,8},{8,0},{16,24},{24,16},{32,40},{40,32},{48,56},{56,48},{64,72... | collective-permute-start | bytes 24584 | tf_op jit(solution)/shard_map/channel_maxima/ppermute | solution.py:160
  45.3 1.1 %collective-permute-done.3 = f32[16,128]{1,0:T(8,128)S(1)} collective-permute-done((f32[16,128]{1,0:T(8,128)S(1)}, f32[16,128]{1,0:T(8,128)S(1)}, u32[]{:S(2)}, u32[]{:S(2)}) %collective-permute-start.3) | collective-permute-done | bytes 8224 | tf_op jit(solution)/shard_map/channel_maxima/ppermute | solution.py:160
  46.5 3.6 %collective-permute-start.4 = (f32[16,128]{1,0:T(8,128)S(1)}, f32[16,128]{1,0:T(8,128)S(1)}, u32[]{:S(2)}, u32[]{:S(2)}) collective-permute-start(f32[16,128]{1,0:T(8,128)S(1)} %max.18), channel_id=1, source_target_pairs={{0,64},{8,72},{16,80},{24,88},{32,96},{40,104},{48,112},{56,120},{... | collective-permute-start | bytes 24584 | tf_op jit(solution)/shard_map/channel_maxima/ppermute | solution.py:160
  50.1 2.0 %collective-permute-done.4 = f32[16,128]{1,0:T(8,128)S(1)} collective-permute-done((f32[16,128]{1,0:T(8,128)S(1)}, f32[16,128]{1,0:T(8,128)S(1)}, u32[]{:S(2)}, u32[]{:S(2)}) %collective-permute-start.4) | collective-permute-done | bytes 8224 | tf_op jit(solution)/shard_map/channel_maxima/ppermute | solution.py:160
  52.0 0.0 all-to-all-done.pages_ref
  52.0 20.5 %all_to_all.15.maxima_ref = f32[16,16,128]{2,1,0:T(8,128)S(1)} all-to-all(f32[16,16,128]{2,1,0:T(8,128)S(1)} %broadcast_in_dim.2), channel_id=1, replica_groups={{0,16,32,48,128,144,160,176,256,272,288,304,384,400,416,432},{8,24,40,5..., dimensions={0} | all-to-all | bytes 262144 | tf_op jit(solution)/shard_map/channel_maxima/all_to_all | solution.py:210
  72.5 0.9 %token_peaks.1 = f32[8,16,128]{2,1,0:T(8,128)S(1)} custom-call(f32[16,16,128]{2,1,0:T(8,128)S(1)} %all_to_all.15.maxima_ref, f32[16,128]{1,0:T(8,128)S(1)} %maximum_select_fusion.sums_ref, bf16[512,1536]{1,0:T(8,128)(2,1)S(1)} %copy-done, f32[12,128]{1,0:T(8,128)S(1)} %bitcast.5, f32[12,128]{1,0:T(8,128)S(1)} %bitcast.7), custom_call_target="tpu_custom_call" | custom-call | tf_op jit(solution)/shard_map/token_peaks/pallas_call | solution.py:212
  73.4 15.7 %all_to_all.16.blocks_ref = f32[8,16,128]{2,1,0:T(8,128)S(1)} all-to-all(f32[8,16,128]{2,1,0:T(8,128)S(1)} %token_peaks.1), channel_id=1, replica_groups=mesh['dp'=64,'mp'=8] {'mp'}, dimensions={0} | all-to-all | bytes 131072 | tf_op jit(solution)/shard_map/token_peaks/all_to_all | solution.py:219
  89.1 2.4 %smoothed_weight.1 = (bf16[48,12288]{1,0:T(8,128)(2,1)}, f32[12,128]{1,0:T(8,128)}, f32[4,128]{1,0:T(4,128)}) custom-call(s32[2]{0:T(128)S(1)} %copy-done.4, f32[8,16,128]{2,1,0:T(8,128)S(1)} %all_to_all.16.blocks_ref, bf16[64,72,128]{2,1,0:T(8,128)(2,1)S(1)} %all-to-all-done.pages_ref), custom_call_target="tpu_custom_call" | custom-call | tf_op jit(solution)/shard_map/smoothed_weight/pallas_call | solution.py:221
  (4 shorter events, 0.0 us)
Async XLA Ops:
  4.1 14.6 %copy-start = (bf16[512,1536]{1,0:T(8,128)(2,1)S(1)}, bf16[512,1536]{1,0:T(8,128)(2,1)}, u32[]{:S(2)}) copy-start(bf16[512,1536]{1,0:T(8,128)(2,1)} %acts_ref.5) | copy-start | bytes 4718596
  4.1 14.6 %copy-start.3 = (f32[8,128]{1,0:T(8,128)S(1)}, f32[8,128]{1,0:T(8,128)}, u32[]{:S(2)}) copy-start(f32[8,128]{1,0:T(8,128)} %get-tuple-element.10.peak_ref) | copy-start | bytes 12292
  4.1 47.9 %all-to-all-start = ((bf16[64,72,128]{2,1,0:T(8,128)(2,1)}), bf16[64,72,128]{2,1,0:T(8,128)(2,1)S(1)}, u32[]{:S(2)}, u32[]{:S(2)}) async-start(bf16[64,72,128]{2,1,0:T(8,128)(2,1)} %get-tuple-element.11), calls=%async_computation | async-start | bytes 2359296 | tf_op jit(solution)/shard_map/weight_exchange/all_to_all | solution.py:184
  18.7 23.2 %copy-start.1 = (f32[1536]{0:T(1024)S(1)}, f32[1536]{0:T(1024)}, u32[]{:S(2)}) copy-start(f32[1536]{0:T(1024)} %param.7) | copy-start | bytes 18436
  18.7 23.2 %copy-start.2 = (f32[1536]{0:T(1024)S(1)}, f32[1536]{0:T(1024)}, u32[]{:S(2)}) copy-start(f32[1536]{0:T(1024)} %param.8) | copy-start | bytes 18436
  18.7 23.2 %copy-start.4 = (s32[2]{0:T(128)S(1)}, s32[2]{0:T(128)}, u32[]{:S(2)}) copy-start(s32[2]{0:T(128)} %lengths_ref.3) | copy-start | bytes 28
  19.2 5.5 %collective-permute-start = (f32[16,128]{1,0:T(8,128)S(1)}, f32[16,128]{1,0:T(8,128)S(1)}, u32[]{:S(2)}, u32[]{:S(2)}) collective-permute-start(f32[16,128]{1,0:T(8,128)S(1)} %token_moments.1), channel_id=1, source_target_pairs={{0,1},{1,0},{2,3},{3,2},{4,5},{5,4},{6,7},{7,6},{8,9},{9,8},{10,11... | collective-permute-start | bytes 24584 | tf_op jit(solution)/shard_map/token_moments/ppermute | solution.py:160
  24.8 7.0 %collective-permute-start.1 = (f32[16,128]{1,0:T(8,128)S(1)}, f32[16,128]{1,0:T(8,128)S(1)}, u32[]{:S(2)}, u32[]{:S(2)}) collective-permute-start(f32[16,128]{1,0:T(8,128)S(1)} %maximum_select_fusion.2), channel_id=1, source_target_pairs={{0,2},{1,3},{2,0},{3,1},{4,6},{5,7},{6,4},{7,5},{8,10},{9,11},{10,... | collective-permute-start | bytes 24584 | tf_op jit(solution)/shard_map/token_moments/ppermute | solution.py:160
  31.9 9.8 %collective-permute-start.2 = (f32[16,128]{1,0:T(8,128)S(1)}, f32[16,128]{1,0:T(8,128)S(1)}, u32[]{:S(2)}, u32[]{:S(2)}) collective-permute-start(f32[16,128]{1,0:T(8,128)S(1)} %maximum_select_fusion.1), channel_id=1, source_target_pairs={{0,4},{1,5},{2,6},{3,7},{4,0},{5,1},{6,2},{7,3},{8,12},{9,13},{10,... | collective-permute-start | bytes 24584 | tf_op jit(solution)/shard_map/token_moments/ppermute | solution.py:160
  43.4 3.1 %collective-permute-start.3 = (f32[16,128]{1,0:T(8,128)S(1)}, f32[16,128]{1,0:T(8,128)S(1)}, u32[]{:S(2)}, u32[]{:S(2)}) collective-permute-start(f32[16,128]{1,0:T(8,128)S(1)} %channel_maxima.1), channel_id=1, source_target_pairs={{0,8},{8,0},{16,24},{24,16},{32,40},{40,32},{48,56},{56,48},{64,72... | collective-permute-start | bytes 24584 | tf_op jit(solution)/shard_map/channel_maxima/ppermute | solution.py:160
  46.5 5.5 %collective-permute-start.4 = (f32[16,128]{1,0:T(8,128)S(1)}, f32[16,128]{1,0:T(8,128)S(1)}, u32[]{:S(2)}, u32[]{:S(2)}) collective-permute-start(f32[16,128]{1,0:T(8,128)S(1)} %max.18), channel_id=1, source_target_pairs={{0,64},{8,72},{16,80},{24,88},{32,96},{40,104},{48,112},{56,120},{... | collective-permute-start | bytes 24584 | tf_op jit(solution)/shard_map/channel_maxima/ppermute | solution.py:160

commit v5 on v4

--- a/solution.py
+++ b/solution.py
@@ -96,14 +96,13 @@
             peaks[tile] = jnp.maximum(peaks[tile], jnp.max(peak.reshape(16, 8, 128), axis=0))
     for tile in range(12):
         page_ref[tile : tile + 1, :] = jnp.max(peaks[tile], axis=0, keepdims=True)
-    kept = lax.axis_index("dp") // 8 == lax.axis_index("mp")
-    page_ref[12:15, :] = jnp.where(kept, sums_ref[8:11, :], 0.0)
+    page_ref[12:15, :] = sums_ref[8:11, :]
     page_ref[15:16, :] = jnp.zeros((1, 128), jnp.float32)
 
 
 def peak_kernel(maxima_ref, sums_ref, acts_ref, gain_ref, bias_ref, page_ref):
     columns = moments(sums_ref[...])
-    start = 4 * (lax.axis_index("mp") // 2)
+    start = 4 * lax.axis_index("mp")
     act = jnp.max(maxima_ref[:, 0:12, :], axis=0)
     for slot in range(4):
         page_ref[0, 3 * slot : 3 * slot + 3, :] = maxima_ref[start + slot, 12:15, :]
@@ -126,24 +125,35 @@
         page_ref[peer] = page
 
 
-def serve_kernel(lengths_ref, blocks_ref, pages_ref, served_hbm, scale_ref, tok_ref, served_ref, sems):
+def unpack_kernel(own_ref, other_ref, raw_ref):
+    core = lax.axis_index("dp") % 2
     low = lax.broadcasted_iota(jnp.int32, (24, 128), 1) < 64
-
+    first = low == (core == 0)
+
+    def unpack(chip, carry):
+        own = own_ref[2 * chip + core].astype(jnp.float32)
+        other = other_ref[chip].astype(jnp.float32)
+        upper = jnp.where(first, own[48:72], other[48:72])
+        lower = pltpu.roll(jnp.where(first, other[48:72], own[48:72]), 64, 1)
+        even = jnp.where(core == 0, own[0:48], other[0:48])
+        odd = jnp.where(core == 0, other[0:48], own[0:48])
+        triple = jnp.concatenate([even, jnp.concatenate([upper, lower], axis=0), odd], axis=1)
+        raw_ref[:, pl.ds(pl.multiple_of(384 * chip, 128), 384)] = triple.astype(jnp.bfloat16)
+        return carry
+
+    lax.fori_loop(0, 32, unpack, 0, unroll=4)
+
+
+def serve_kernel(lengths_ref, blocks_ref, raw_ref, served_hbm, scale_ref, tok_ref, served_ref, sems):
     def store(step):
-        columns = pl.ds(pl.multiple_of(3072 * step, 128), 3072)
+        columns = pl.ds(3072 * step, 3072)
         return pltpu.make_async_copy(served_ref.at[:, columns], served_hbm.at[:, columns], sems.at[step])
 
     for step in range(4):
-        for pair in range(8 * step, 8 * step + 8):
-            even = pages_ref[2 * pair].astype(jnp.float32)
-            odd = pages_ref[2 * pair + 1].astype(jnp.float32)
-            upper = jnp.where(low, even[48:72], odd[48:72])
-            lower = pltpu.roll(jnp.where(low, odd[48:72], even[48:72]), 64, 1)
-            middle = jnp.concatenate([upper, lower], axis=0)
-            for part, tile in enumerate((even[0:48], middle, odd[0:48])):
-                row = 3 * pair + part
-                scale = blocks_ref[row // 12, row % 12 : row % 12 + 1, :]
-                served_ref[:, pl.ds(128 * row, 128)] = (tile * scale).astype(jnp.bfloat16)
+        for row in range(24 * step, 24 * step + 24):
+            scale = blocks_ref[row // 12, row % 12 : row % 12 + 1, :]
+            columns = pl.ds(128 * row, 128)
+            served_ref[:, columns] = (raw_ref[:, columns].astype(jnp.float32) * scale).astype(jnp.bfloat16)
         store(step).start()
     scale_ref[...] = blocks_ref[lax.axis_index("mp"), 0:12, :]
     peaks = jnp.max(blocks_ref[:, 12:16, :], axis=0)
@@ -181,7 +191,8 @@
             ],
             compiler_params=params(60),
         )(w_fc1)
-        pages = lax.all_to_all(packed, "dp", 0, 0, tiled=True)
+        kinds = [[2 * chip + core for chip in range(32)] for core in range(2)]
+        pages = lax.all_to_all(packed, "dp", 0, 0, axis_index_groups=kinds, tiled=True)
     with jax.named_scope("token_moments"):
         sums = pl.pallas_call(
             stats_kernel,
@@ -202,12 +213,21 @@
             out_specs=VMEM_SPEC,
             compiler_params=params(),
         )(lengths, sums, acts, gain, bias)
-        for bit in (1, 8):
-            maxima = jnp.maximum(maxima, swap(maxima, "dp", bit))
+        maxima = jnp.maximum(maxima, swap(maxima, "dp", 1))
         maxima, pages = lax.optimization_barrier((maxima, pages))
-        copies = jnp.broadcast_to(maxima[None], (16, 16, 128))
-        kinds = [[16 * pair + 8 * plane + 2 * y + core for pair in range(4) for y in range(4)] for plane in (0, 1) for core in (0, 1)]
+        copies = jnp.broadcast_to(maxima[None], (32, 16, 128))
         maxima = lax.all_to_all(copies, "dp", 0, 0, axis_index_groups=kinds, tiled=True)
+    with jax.named_scope("core_halves"):
+        core = lax.axis_index("dp") % 2
+        theirs = lax.dynamic_index_in_dim(pages.reshape(32, 2, 72, 128), 1 - core, 1, keepdims=False)
+        others = swap(theirs, "dp", 1)
+        raw = pl.pallas_call(
+            unpack_kernel,
+            out_shape=jax.ShapeDtypeStruct((48, D), jnp.bfloat16),
+            in_specs=[VMEM_SPEC, VMEM_SPEC],
+            out_specs=VMEM_SPEC,
+            compiler_params=params(),
+        )(pages, others)
     with jax.named_scope("token_peaks"):
         page = pl.pallas_call(
             peak_kernel,
@@ -229,7 +249,7 @@
             out_specs=(ANY_SPEC, VMEM_SPEC, VMEM_SPEC),
             scratch_shapes=[pltpu.VMEM((48, D), jnp.bfloat16), pltpu.SemaphoreType.DMA((4,))],
             compiler_params=params(),
-        )(lengths, blocks, pages)
+        )(lengths, blocks, raw)
     return served, scale.reshape(1536), tok.reshape(512)
 
 

time: 91.9 us -> 90.1 us (0.980)
  the two profiles are of different devices: /device:TPU:2 before, /device:TPU:1 now
where the time goes in v5:
time: 90.1 us; the launch traced here: 88.4 us
  starting transfers between devices  49.6 us (55%)
  waiting for transfers between devices  25.1 us (28%)
  Pallas kernels  11.1 us (12%)
  local copies, waits for them, and re-layouts  1.62 us (2%)
    ppermute x5, starting transfers between devices, swap(): return lax.ppermute(x, axis, [(i, i ^ bit) for i in range(size)])  18.9 us
    all_to_all x1, starting transfers between devices, body(): lax.all_to_all(packed, 'dp', 0, 0, axis_index_groups=kinds, tiled=True)  14.4 us
    all_to_all x1, starting transfers between devices, body(): lax.all_to_all(copies, 'dp', 0, 0, axis_index_groups=kinds, tiled=True)  9.68 us
    ppermute x5, waiting for transfers between devices, swap(): return lax.ppermute(x, axis, [(i, i ^ bit) for i in range(size)])  9.32 us
    all_to_all x1, waiting for transfers between devices, body(): lax.all_to_all(copies, 'dp', 0, 0, axis_index_groups=kinds, tiled=True)  8.23 us
    all_to_all x1, waiting for transfers between devices, body(): blocks = lax.all_to_all(page, 'mp', 0, 0, tiled=True)  7.31 us
    all_to_all x1, starting transfers between devices, body(): blocks = lax.all_to_all(page, 'mp', 0, 0, tiled=True)  6.59 us
    pallas_call x1, Pallas kernels, body(): pl.pallas_call(pack_kernel, out_shape=(jax.ShapeDtypeStruct((64, 72, 128)...  3.48 us
  transfers between devices with their start and end apart: 8, of which 7 were waited for; matrix products, arithmetic and copies ran while one was open for 1% of the time, Pallas kernels for 6%

profile of v5, /device:TPU:1, one launch (start us, length us, event | category | flops | bytes accessed | tf_op | source)
XLA Modules:
  0.0 88.4 jit_solution(15096967709532154338)
XLA Ops:
  0.6 3.5 %weight_exchange.1 = (bf16[64,72,128]{2,1,0:T(8,128)(2,1)}, f32[8,128]{1,0:T(8,128)}) custom-call(bf16[192,3072]{1,0:T(8,128)(2,1)} %w_hbm.1), custom_call_target="tpu_custom_call" | custom-call | tf_op jit(solution)/shard_map/weight_exchange/pallas_call | solution.py:177
  4.1 0.0 copy-start
  4.1 0.0 copy-start.3
  4.1 14.4 %all-to-all-start = ((bf16[64,72,128]{2,1,0:T(8,128)(2,1)}), bf16[64,72,128]{2,1,0:T(8,128)(2,1)S(1)}, u32[]{:S(2)}, u32[]{:S(2)}) async-start(bf16[64,72,128]{2,1,0:T(8,128)(2,1)} %get-tuple-element.11), calls=%async_computation | async-start | bytes 2359296 | tf_op jit(solution)/shard_map/weight_exchange/all_to_all | solution.py:195
  18.6 0.0 copy-start.1
  18.6 0.0 copy-start.2
  18.6 0.0 copy-start.4
  18.6 0.0 copy-done
  18.6 0.0 copy-done.3
  18.6 0.5 token_moments.1
  19.1 3.1 %collective-permute-start = (f32[16,128]{1,0:T(8,128)S(1)}, f32[16,128]{1,0:T(8,128)S(1)}, u32[]{:S(2)}, u32[]{:S(2)}) collective-permute-start(f32[16,128]{1,0:T(8,128)S(1)} %token_moments.1), channel_id=1, source_target_pairs={{0,1},{1,0},{2,3},{3,2},{4,5},{5,4},{6,7},{7,6},{8,9},{9,8},{10,11... | collective-permute-start | bytes 24584 | tf_op jit(solution)/shard_map/token_moments/ppermute | solution.py:170
  22.3 1.3 %collective-permute-done = f32[16,128]{1,0:T(8,128)S(1)} collective-permute-done((f32[16,128]{1,0:T(8,128)S(1)}, f32[16,128]{1,0:T(8,128)S(1)}, u32[]{:S(2)}, u32[]{:S(2)}) %collective-permute-start) | collective-permute-done | bytes 8224 | tf_op jit(solution)/shard_map/token_moments/ppermute | solution.py:170
  23.5 0.1 maximum_select_fusion.2
  23.6 4.6 %collective-permute-start.1 = (f32[16,128]{1,0:T(8,128)S(1)}, f32[16,128]{1,0:T(8,128)S(1)}, u32[]{:S(2)}, u32[]{:S(2)}) collective-permute-start(f32[16,128]{1,0:T(8,128)S(1)} %maximum_select_fusion.2), channel_id=1, source_target_pairs={{0,2},{1,3},{2,0},{3,1},{4,6},{5,7},{6,4},{7,5},{8,10},{9,11},{10,... | collective-permute-start | bytes 24584 | tf_op jit(solution)/shard_map/token_moments/ppermute | solution.py:170
  28.2 1.5 %collective-permute-done.1 = f32[16,128]{1,0:T(8,128)S(1)} collective-permute-done((f32[16,128]{1,0:T(8,128)S(1)}, f32[16,128]{1,0:T(8,128)S(1)}, u32[]{:S(2)}, u32[]{:S(2)}) %collective-permute-start.1) | collective-permute-done | bytes 8224 | tf_op jit(solution)/shard_map/token_moments/ppermute | solution.py:170
  29.8 0.1 maximum_select_fusion.1
  29.9 4.7 %collective-permute-start.2 = (f32[16,128]{1,0:T(8,128)S(1)}, f32[16,128]{1,0:T(8,128)S(1)}, u32[]{:S(2)}, u32[]{:S(2)}) collective-permute-start(f32[16,128]{1,0:T(8,128)S(1)} %maximum_select_fusion.1), channel_id=1, source_target_pairs={{0,4},{1,5},{2,6},{3,7},{4,0},{5,1},{6,2},{7,3},{8,12},{9,13},{10,... | collective-permute-start | bytes 24584 | tf_op jit(solution)/shard_map/token_moments/ppermute | solution.py:170
  34.6 5.7 %collective-permute-done.2 = f32[16,128]{1,0:T(8,128)S(1)} collective-permute-done((f32[16,128]{1,0:T(8,128)S(1)}, f32[16,128]{1,0:T(8,128)S(1)}, u32[]{:S(2)}, u32[]{:S(2)}) %collective-permute-start.2) | collective-permute-done | bytes 8224 | tf_op jit(solution)/shard_map/token_moments/ppermute | solution.py:170
  40.3 0.1 maximum_select_fusion.sums_ref
  40.4 0.0 copy-done.1
  40.4 0.0 copy-done.2
  40.4 0.0 copy-done.4
  40.4 1.6 %channel_maxima.1 = f32[16,128]{1,0:T(8,128)S(1)} custom-call(s32[2]{0:T(128)S(1)} %copy-done.4, f32[16,128]{1,0:T(8,128)S(1)} %maximum_select_fusion.sums_ref, bf16[512,1536]{1,0:T(8,128)(2,1)S(1)} %copy-done, f32[12,128]{1,0:T(8,128)S(1)} %bitcast.10, f32[12,128]{1,0:T(8,128)S(1)} %bitcast.12), custom_call_target="tpu_custom_call" | custom-call | tf_op jit(solution)/shard_map/channel_maxima/pallas_call | solution.py:209
  42.0 3.8 %collective-permute-start.3 = (f32[16,128]{1,0:T(8,128)S(1)}, f32[16,128]{1,0:T(8,128)S(1)}, u32[]{:S(2)}, u32[]{:S(2)}) collective-permute-start(f32[16,128]{1,0:T(8,128)S(1)} %channel_maxima.1), channel_id=1, source_target_pairs={{0,8},{8,0},{16,24},{24,16},{32,40},{40,32},{48,56},{56,48},{64,72... | collective-permute-start | bytes 24584 | tf_op jit(solution)/shard_map/channel_maxima/ppermute | solution.py:170
  45.9 0.8 collective-permute-done.3
  46.6 0.2 all-to-all-done.own_ref
  46.9 0.7 broadcast_in_dim.2
  47.6 9.7 %all-to-all-start.1 = ((f32[32,16,128]{2,1,0:T(8,128)}), f32[32,16,128]{2,1,0:T(8,128)S(1)}, u32[]{:S(2)}, u32[]{:S(2)}) async-start(f32[32,16,128]{2,1,0:T(8,128)} %broadcast_in_dim.2), calls=%async_computation.1 | async-start | bytes 524288 | tf_op jit(solution)/shard_map/channel_maxima/all_to_all | solution.py:219
  57.3 0.9 dynamic-slice_bitcast_fusion
  58.1 2.5 %collective-permute-start.4 = (bf16[32,72,128]{2,1,0:T(8,128)(2,1)}, bf16[32,72,128]{2,1,0:T(8,128)(2,1)}, u32[]{:S(2)}, u32[]{:S(2)}) collective-permute-start(bf16[32,72,128]{2,1,0:T(8,128)(2,1)} %dynamic-slice_bitcast_fusion), channel_id=1, source_target_pairs={{0,8},{8,0},{16,24},{24,16},{32,40},{40,32},{48,56},{56,48},{64,72... | collective-permute-start | bytes 1769480 | tf_op jit(solution)/shard_map/core_halves/ppermute | solution.py:170
  60.7 8.2 %all-to-all-done.1.maxima_ref = f32[32,16,128]{2,1,0:T(8,128)S(1)} async-done(((f32[32,16,128]{2,1,0:T(8,128)}), f32[32,16,128]{2,1,0:T(8,128)S(1)}, u32[]{:S(2)}, u32[]{:S(2)}) %all-to-all-start.1) | async-done | bytes 262176 | tf_op jit(solution)/shard_map/channel_maxima/all_to_all | solution.py:219
  68.9 1.6 %token_peaks.1 = f32[8,16,128]{2,1,0:T(8,128)} custom-call(f32[32,16,128]{2,1,0:T(8,128)S(1)} %all-to-all-done.1.maxima_ref, f32[16,128]{1,0:T(8,128)S(1)} %maximum_select_fusion.sums_ref, bf16[512,1536]{1,0:T(8,128)(2,1)S(1)} %copy-done, f32[12,128]{1,0:T(8,128)S(1)} %bitcast.11, f32[12,128]{1,0:T(8,128)S(1)} %bitcast.13), custom_call_target="tpu_custom_call" | custom-call | tf_op jit(solution)/shard_map/token_peaks/pallas_call | solution.py:232
  70.5 6.6 %all-to-all-start.2 = ((f32[8,16,128]{2,1,0:T(8,128)}), f32[8,16,128]{2,1,0:T(8,128)S(1)}, u32[]{:S(2)}, u32[]{:S(2)}) async-start(f32[8,16,128]{2,1,0:T(8,128)} %token_peaks.1), calls=%async_computation.2 | async-start | bytes 131072 | tf_op jit(solution)/shard_map/token_peaks/all_to_all | solution.py:239
  77.1 0.0 collective-permute-done.4.other_ref
  77.1 1.8 %core_halves.1.raw_ref = bf16[48,12288]{1,0:T(8,128)(2,1)S(1)} custom-call(bf16[64,72,128]{2,1,0:T(8,128)(2,1)S(1)} %all-to-all-done.own_ref, bf16[32,72,128]{2,1,0:T(8,128)(2,1)} %collective-permute-done.4.other_ref), custom_call_target="tpu_custom_call" | custom-call | tf_op jit(solution)/shard_map/core_halves/pallas_call | solution.py:224
  78.9 7.3 %all-to-all-done.2.blocks_ref = f32[8,16,128]{2,1,0:T(8,128)S(1)} async-done(((f32[8,16,128]{2,1,0:T(8,128)}), f32[8,16,128]{2,1,0:T(8,128)S(1)}, u32[]{:S(2)}, u32[]{:S(2)}) %all-to-all-start.2) | async-done | bytes 65568 | tf_op jit(solution)/shard_map/token_peaks/all_to_all | solution.py:239
  86.2 2.2 %smoothed_weight.1 = (bf16[48,12288]{1,0:T(8,128)(2,1)}, f32[12,128]{1,0:T(8,128)}, f32[4,128]{1,0:T(4,128)}) custom-call(s32[2]{0:T(128)S(1)} %copy-done.4, f32[8,16,128]{2,1,0:T(8,128)S(1)} %all-to-all-done.2.blocks_ref, bf16[48,12288]{1,0:T(8,128)(2,1)S(1)} %core_halves.1.raw_ref), custom_call_target="tpu_custom_call" | custom-call | tf_op jit(solution)/shard_map/smoothed_weight/pallas_call | solution.py:241
  (2 shorter events, 0.0 us)
Async XLA Ops:
  4.1 14.5 %copy-start = (bf16[512,1536]{1,0:T(8,128)(2,1)S(1)}, bf16[512,1536]{1,0:T(8,128)(2,1)}, u32[]{:S(2)}) copy-start(bf16[512,1536]{1,0:T(8,128)(2,1)} %acts_ref.5) | copy-start | bytes 4718596
  4.1 14.5 %copy-start.3 = (f32[8,128]{1,0:T(8,128)S(1)}, f32[8,128]{1,0:T(8,128)}, u32[]{:S(2)}) copy-start(f32[8,128]{1,0:T(8,128)} %get-tuple-element.10.peak_ref) | copy-start | bytes 12292
  4.1 42.7 %all-to-all-start = ((bf16[64,72,128]{2,1,0:T(8,128)(2,1)}), bf16[64,72,128]{2,1,0:T(8,128)(2,1)S(1)}, u32[]{:S(2)}, u32[]{:S(2)}) async-start(bf16[64,72,128]{2,1,0:T(8,128)(2,1)} %get-tuple-element.11), calls=%async_computation | async-start | bytes 2359296 | tf_op jit(solution)/shard_map/weight_exchange/all_to_all | solution.py:195
  18.6 21.8 %copy-start.1 = (f32[1536]{0:T(1024)S(1)}, f32[1536]{0:T(1024)}, u32[]{:S(2)}) copy-start(f32[1536]{0:T(1024)} %param.7) | copy-start | bytes 18436
  18.6 21.8 %copy-start.2 = (f32[1536]{0:T(1024)S(1)}, f32[1536]{0:T(1024)}, u32[]{:S(2)}) copy-start(f32[1536]{0:T(1024)} %param.8) | copy-start | bytes 18436
  18.6 21.8 %copy-start.4 = (s32[2]{0:T(128)S(1)}, s32[2]{0:T(128)}, u32[]{:S(2)}) copy-start(s32[2]{0:T(128)} %lengths_ref.3) | copy-start | bytes 28
  19.1 4.4 %collective-permute-start = (f32[16,128]{1,0:T(8,128)S(1)}, f32[16,128]{1,0:T(8,128)S(1)}, u32[]{:S(2)}, u32[]{:S(2)}) collective-permute-start(f32[16,128]{1,0:T(8,128)S(1)} %token_moments.1), channel_id=1, source_target_pairs={{0,1},{1,0},{2,3},{3,2},{4,5},{5,4},{6,7},{7,6},{8,9},{9,8},{10,11... | collective-permute-start | bytes 24584 | tf_op jit(solution)/shard_map/token_moments/ppermute | solution.py:170
  23.6 6.2 %collective-permute-start.1 = (f32[16,128]{1,0:T(8,128)S(1)}, f32[16,128]{1,0:T(8,128)S(1)}, u32[]{:S(2)}, u32[]{:S(2)}) collective-permute-start(f32[16,128]{1,0:T(8,128)S(1)} %maximum_select_fusion.2), channel_id=1, source_target_pairs={{0,2},{1,3},{2,0},{3,1},{4,6},{5,7},{6,4},{7,5},{8,10},{9,11},{10,... | collective-permute-start | bytes 24584 | tf_op jit(solution)/shard_map/token_moments/ppermute | solution.py:170
  29.9 10.5 %collective-permute-start.2 = (f32[16,128]{1,0:T(8,128)S(1)}, f32[16,128]{1,0:T(8,128)S(1)}, u32[]{:S(2)}, u32[]{:S(2)}) collective-permute-start(f32[16,128]{1,0:T(8,128)S(1)} %maximum_select_fusion.1), channel_id=1, source_target_pairs={{0,4},{1,5},{2,6},{3,7},{4,0},{5,1},{6,2},{7,3},{8,12},{9,13},{10,... | collective-permute-start | bytes 24584 | tf_op jit(solution)/shard_map/token_moments/ppermute | solution.py:170
  42.0 4.6 %collective-permute-start.3 = (f32[16,128]{1,0:T(8,128)S(1)}, f32[16,128]{1,0:T(8,128)S(1)}, u32[]{:S(2)}, u32[]{:S(2)}) collective-permute-start(f32[16,128]{1,0:T(8,128)S(1)} %channel_maxima.1), channel_id=1, source_target_pairs={{0,8},{8,0},{16,24},{24,16},{32,40},{40,32},{48,56},{56,48},{64,72... | collective-permute-start | bytes 24584 | tf_op jit(solution)/shard_map/channel_maxima/ppermute | solution.py:170
  47.6 21.3 %all-to-all-start.1 = ((f32[32,16,128]{2,1,0:T(8,128)}), f32[32,16,128]{2,1,0:T(8,128)S(1)}, u32[]{:S(2)}, u32[]{:S(2)}) async-start(f32[32,16,128]{2,1,0:T(8,128)} %broadcast_in_dim.2), calls=%async_computation.1 | async-start | bytes 524288 | tf_op jit(solution)/shard_map/channel_maxima/all_to_all | solution.py:219
  58.1 18.9 %collective-permute-start.4 = (bf16[32,72,128]{2,1,0:T(8,128)(2,1)}, bf16[32,72,128]{2,1,0:T(8,128)(2,1)}, u32[]{:S(2)}, u32[]{:S(2)}) collective-permute-start(bf16[32,72,128]{2,1,0:T(8,128)(2,1)} %dynamic-slice_bitcast_fusion), channel_id=1, source_target_pairs={{0,8},{8,0},{16,24},{24,16},{32,40},{40,32},{48,56},{56,48},{64,72... | collective-permute-start | bytes 1769480 | tf_op jit(solution)/shard_map/core_halves/ppermute | solution.py:170
  70.5 15.7 %all-to-all-start.2 = ((f32[8,16,128]{2,1,0:T(8,128)}), f32[8,16,128]{2,1,0:T(8,128)S(1)}, u32[]{:S(2)}, u32[]{:S(2)}) async-start(f32[8,16,128]{2,1,0:T(8,128)} %token_peaks.1), calls=%async_computation.2 | async-start | bytes 131072 | tf_op jit(solution)/shard_map/token_peaks/all_to_all | solution.py:239

commit v6 on v4

--- a/solution.py
+++ b/solution.py
@@ -17,11 +17,44 @@
     return pltpu.CompilerParams(vmem_limit_bytes=mebibytes * 1024 * 1024)
 
 
-def pack_kernel(w_hbm, page_hbm, peak_ref, w_ref, page_ref, rows_ref, in_sems, out_sems):
+def stats_kernel(acts_hbm, w_hbm, page_ref, acts_ref, w_ref, rows_ref, acts_sems, w_sems):
+    parity = lax.axis_index("dp") % 2
+    acts_copies, w_copies = [], []
+    for block in range(4):
+        tokens, rows = pl.ds(128 * block, 128), pl.ds(48 * block, 48)
+        acts_copies.append(pltpu.make_async_copy(acts_hbm.at[tokens], acts_ref.at[tokens], acts_sems.at[block]))
+        w_copies.append(pltpu.make_async_copy(w_hbm.at[rows], w_ref.at[rows], w_sems.at[block]))
+    for copy in w_copies + acts_copies:
+        copy.start()
+    rows_ref[...] = jnp.zeros_like(rows_ref)
+    for block in range(4):
+        w_copies[block].wait()
+        peak = jnp.zeros((48, 128), jnp.float32)
+        for tile in range(24):
+            peak = jnp.maximum(peak, jnp.abs(w_ref[pl.ds(48 * block, 48), pl.ds(128 * tile, 128)].astype(jnp.float32)))
+        rows_ref[pl.ds(pl.multiple_of(192 * parity + 48 * block, 16), 48), :] = peak
+    for block in range(3):
+        page_ref[0, 8 + block : 9 + block, :] = jnp.max(rows_ref[pl.ds(128 * block, 128), :].T, axis=0, keepdims=True)
+    page_ref[0, 11:16, :] = jnp.zeros((5, 128), jnp.float32)
+    for block in range(4):
+        acts_copies[block].wait()
+        total = jnp.zeros((128, 128), jnp.float32)
+        square = jnp.zeros((128, 128), jnp.float32)
+        for tile in range(12):
+            x = acts_ref[pl.ds(128 * block, 128), pl.ds(128 * tile, 128)].astype(jnp.float32)
+            total = total + x
+            square = square + x * x
+        page_ref[0, block : block + 1, :] = jnp.sum(total.T, axis=0, keepdims=True)
+        page_ref[0, 4 + block : 5 + block, :] = jnp.sum(square.T, axis=0, keepdims=True)
+    page = page_ref[0]
+    for peer in range(1, page_ref.shape[0]):
+        page_ref[peer] = page
+
+
+def pack_kernel(w_hbm, page_hbm, w_ref, page_ref, in_sems, out_sems):
     parity = lax.axis_index("dp") % 2
     low = lax.broadcasted_iota(jnp.int32, (24, 128), 1) < 64
     first = low == (parity == 0)
-    own = pl.ds(pl.multiple_of(192 * parity, 64), 192)
 
     def columns(step):
         return pl.ds(pl.multiple_of(384 * step, 128), 384)
@@ -35,13 +68,9 @@
 
     for step in range(8):
         fetch(step).start()
-    rows_ref[...] = jnp.zeros_like(rows_ref)
 
     def pack(step, carry):
         fetch(step).wait()
-        w = jnp.abs(w_ref[:, columns(step)].astype(jnp.float32))
-        peak = jnp.maximum(jnp.maximum(w[:, 0:128], w[:, 128:256]), w[:, 256:384])
-        rows_ref[own, :] = jnp.maximum(rows_ref[own, :], peak)
         full = w_ref[pl.ds(pl.multiple_of(64 * parity, 64), 128), columns(step)].astype(jnp.float32).T
         half = w_ref[pl.ds(pl.multiple_of(128 * (1 - parity), 64), 64), columns(step)].astype(jnp.float32)
         twice = jnp.concatenate([half, half], axis=0).T
@@ -54,24 +83,8 @@
         return carry
 
     lax.fori_loop(0, 8, pack, 0)
-    for block in range(3):
-        peak_ref[block : block + 1, :] = jnp.max(rows_ref[pl.ds(128 * block, 128), :].T, axis=0, keepdims=True)
-    peak_ref[3:8, :] = jnp.zeros((5, 128), jnp.float32)
     for step in range(8):
         store(step).wait()
-
-
-def stats_kernel(peak_ref, acts_ref, page_ref):
-    page_ref[8:16, :] = peak_ref[...]
-    for block in range(4):
-        total = jnp.zeros((128, 128), jnp.float32)
-        square = jnp.zeros((128, 128), jnp.float32)
-        for tile in range(12):
-            x = acts_ref[pl.ds(128 * block, 128), pl.ds(128 * tile, 128)].astype(jnp.float32)
-            total = total + x
-            square = square + x * x
-        page_ref[block : block + 1, :] = jnp.sum(total.T, axis=0, keepdims=True)
-        page_ref[4 + block : 5 + block, :] = jnp.sum(square.T, axis=0, keepdims=True)
 
 
 def moments(sums):
@@ -96,18 +109,16 @@
             peaks[tile] = jnp.maximum(peaks[tile], jnp.max(peak.reshape(16, 8, 128), axis=0))
     for tile in range(12):
         page_ref[tile : tile + 1, :] = jnp.max(peaks[tile], axis=0, keepdims=True)
-    kept = lax.axis_index("dp") // 8 == lax.axis_index("mp")
-    page_ref[12:15, :] = jnp.where(kept, sums_ref[8:11, :], 0.0)
-    page_ref[15:16, :] = jnp.zeros((1, 128), jnp.float32)
+    place = lax.axis_index("dp")
+    for slot in range(4):
+        kept = (place // 8 == lax.axis_index("mp")) & (place // 2 % 4 == slot)
+        page_ref[12 + 3 * slot : 15 + 3 * slot, :] = jnp.where(kept, sums_ref[8:11, :], 0.0)
 
 
 def peak_kernel(maxima_ref, sums_ref, acts_ref, gain_ref, bias_ref, page_ref):
     columns = moments(sums_ref[...])
-    start = 4 * (lax.axis_index("mp") // 2)
-    act = jnp.max(maxima_ref[:, 0:12, :], axis=0)
-    for slot in range(4):
-        page_ref[0, 3 * slot : 3 * slot + 3, :] = maxima_ref[start + slot, 12:15, :]
-    scale = jnp.sqrt(act + EPS) / jnp.sqrt(page_ref[0, 0:12, :] + EPS)
+    maxima = jnp.max(maxima_ref[...], axis=0)
+    scale = jnp.sqrt(maxima[0:12] + EPS) / jnp.sqrt(maxima[12:24] + EPS)
     page_ref[0, 0:12, :] = scale
     inverse = 1.0 / scale
     gain = gain_ref[...] * inverse
@@ -163,50 +174,55 @@
 def body(acts, lengths, ln_gain, ln_bias, w_fc1):
     gain = ln_gain.reshape(12, 128)
     bias = ln_bias.reshape(12, 128)
+    with jax.named_scope("token_moments"):
+        page = pl.pallas_call(
+            stats_kernel,
+            out_shape=jax.ShapeDtypeStruct((4, 16, 128), jnp.float32),
+            in_specs=[ANY_SPEC, ANY_SPEC],
+            out_specs=VMEM_SPEC,
+            scratch_shapes=[
+                pltpu.VMEM((512, 1536), jnp.bfloat16),
+                pltpu.VMEM((192, 3072), jnp.bfloat16),
+                pltpu.VMEM((384, 128), jnp.float32),
+                pltpu.SemaphoreType.DMA((4,)),
+                pltpu.SemaphoreType.DMA((4,)),
+            ],
+            compiler_params=params(60),
+        )(acts, w_fc1)
+        parts = lax.all_to_all(page, "mp", 0, 0, axis_index_groups=[[0, 1, 2, 3], [4, 5, 6, 7]], tiled=True)
     with jax.named_scope("weight_exchange"):
-        packed, w_peak = pl.pallas_call(
+        packed = pl.pallas_call(
             pack_kernel,
-            out_shape=(
-                jax.ShapeDtypeStruct((64, 72, 128), jnp.bfloat16),
-                jax.ShapeDtypeStruct((8, 128), jnp.float32),
-            ),
+            out_shape=jax.ShapeDtypeStruct((64, 72, 128), jnp.bfloat16),
             in_specs=[ANY_SPEC],
-            out_specs=(ANY_SPEC, VMEM_SPEC),
+            out_specs=ANY_SPEC,
             scratch_shapes=[
                 pltpu.VMEM((192, 3072), jnp.bfloat16),
                 pltpu.VMEM((64, 72, 128), jnp.bfloat16),
-                pltpu.VMEM((384, 128), jnp.float32),
                 pltpu.SemaphoreType.DMA((8,)),
                 pltpu.SemaphoreType.DMA((8,)),
             ],
             compiler_params=params(60),
         )(w_fc1)
+        packed, parts = lax.optimization_barrier((packed, parts))
         pages = lax.all_to_all(packed, "dp", 0, 0, tiled=True)
-    with jax.named_scope("token_moments"):
-        sums = pl.pallas_call(
-            stats_kernel,
-            out_shape=jax.ShapeDtypeStruct((16, 128), jnp.float32),
-            in_specs=[VMEM_SPEC, VMEM_SPEC],
-            out_specs=VMEM_SPEC,
-            compiler_params=params(),
-        )(w_peak, acts)
+    with jax.named_scope("channel_maxima"):
         added = lax.broadcasted_iota(jnp.int32, (16, 128), 0) < 8
-        for bit in (1, 2, 4):
-            other = swap(sums, "mp", bit)
-            sums = jnp.where(added, sums + other, jnp.maximum(sums, other))
-    with jax.named_scope("channel_maxima"):
+        sums = jnp.where(added, jnp.sum(parts, axis=0), jnp.max(parts, axis=0))
+        other = swap(sums, "mp", 4)
+        sums = jnp.where(added, sums + other, jnp.maximum(sums, other))
         maxima = pl.pallas_call(
             act_kernel,
-            out_shape=jax.ShapeDtypeStruct((16, 128), jnp.float32),
+            out_shape=jax.ShapeDtypeStruct((24, 128), jnp.float32),
             in_specs=[SMEM_SPEC] + [VMEM_SPEC] * 4,
             out_specs=VMEM_SPEC,
             compiler_params=params(),
         )(lengths, sums, acts, gain, bias)
-        for bit in (1, 8):
+        for bit in (1, 2, 4, 8):
             maxima = jnp.maximum(maxima, swap(maxima, "dp", bit))
         maxima, pages = lax.optimization_barrier((maxima, pages))
-        copies = jnp.broadcast_to(maxima[None], (16, 16, 128))
-        kinds = [[16 * pair + 8 * plane + 2 * y + core for pair in range(4) for y in range(4)] for plane in (0, 1) for core in (0, 1)]
+        copies = jnp.broadcast_to(maxima[None], (4, 24, 128))
+        kinds = [[16 * pair + rest for pair in range(4)] for rest in range(16)]
         maxima = lax.all_to_all(copies, "dp", 0, 0, axis_index_groups=kinds, tiled=True)
     with jax.named_scope("token_peaks"):
         page = pl.pallas_call(

time: 91.9 us -> 107 us (1.16)
  the two profiles are of different devices: /device:TPU:2 before, /device:TPU:24 now
where the time goes in v6:
time: 107 us; the launch traced here: 106 us
  starting transfers between devices  32.6 us (30%)
  waiting for transfers between devices  32.3 us (30%)
  blocking collectives  29.4 us (27%)
  Pallas kernels  10.9 us (10%)
    ppermute x5, waiting for transfers between devices, swap(): return lax.ppermute(x, axis, [(i, i ^ bit) for i in range(size)])  29.7 us
    all_to_all x1, blocking collectives, body(): blocks = lax.all_to_all(page, 'mp', 0, 0, tiled=True)  14.8 us
    all_to_all x1, blocking collectives, body(): lax.all_to_all(copies, 'dp', 0, 0, axis_index_groups=kinds, tiled=True)  14.6 us
    all_to_all x1, starting transfers between devices, body(): pages = lax.all_to_all(packed, 'dp', 0, 0, tiled=True)  14.1 us
    ppermute x5, starting transfers between devices, swap(): return lax.ppermute(x, axis, [(i, i ^ bit) for i in range(size)])  14.1 us
    all_to_all x1, starting transfers between devices, body(): lax.all_to_all(page, 'mp', 0, 0, axis_index_groups=[[0, 1, 2, 3], [4, 5,...  4.3 us
    pallas_call x1, Pallas kernels, body(): pl.pallas_call(stats_kernel, out_shape=jax.ShapeDtypeStruct((4, 16, 128),...  3.17 us
    pallas_call x1, Pallas kernels, body(): pl.pallas_call(pack_kernel, out_shape=jax.ShapeDtypeStruct((64, 72, 128),...  2.83 us
  transfers between devices with their start and end apart: 7, of which 6 were waited for; matrix products, arithmetic and copies ran while one was open for 0% of the time, Pallas kernels for 4%

profile of v6, /device:TPU:24, one launch (start us, length us, event | category | flops | bytes accessed | tf_op | source)
XLA Modules:
  0.0 106.1 jit_solution(3282615470975496884)
XLA Ops:
  0.6 3.2 %token_moments.1 = f32[4,16,128]{2,1,0:T(8,128)} custom-call(bf16[512,1536]{1,0:T(8,128)(2,1)} %acts_ref.3, bf16[192,3072]{1,0:T(8,128)(2,1)} %w_hbm.3), custom_call_target="tpu_custom_call" | custom-call | tf_op jit(solution)/shard_map/token_moments/pallas_call | solution.py:178
  3.8 4.3 %all-to-all-start = ((f32[4,16,128]{2,1,0:T(8,128)}), f32[4,16,128]{2,1,0:T(8,128)S(1)}, u32[]{:S(2)}, u32[]{:S(2)}) async-start(f32[4,16,128]{2,1,0:T(8,128)} %token_moments.1), calls=%async_computation | async-start | bytes 65536 | tf_op jit(solution)/shard_map/token_moments/all_to_all | solution.py:192
  8.1 2.8 %weight_exchange.1 = bf16[64,72,128]{2,1,0:T(8,128)(2,1)} custom-call(bf16[192,3072]{1,0:T(8,128)(2,1)} %w_hbm.3), custom_call_target="tpu_custom_call" | custom-call | tf_op jit(solution)/shard_map/weight_exchange/pallas_call | solution.py:194
  11.0 0.0 copy-start
  11.0 0.0 copy-start.1
  11.0 0.0 copy-start.2
  11.0 0.0 copy-start.3
  11.0 2.6 %all-to-all-done = f32[4,16,128]{2,1,0:T(8,128)S(1)} async-done(((f32[4,16,128]{2,1,0:T(8,128)}), f32[4,16,128]{2,1,0:T(8,128)S(1)}, u32[]{:S(2)}, u32[]{:S(2)}) %all-to-all-start) | async-done | bytes 32800 | tf_op jit(solution)/shard_map/token_moments/all_to_all | solution.py:192
  13.6 14.1 %all-to-all-start.1 = ((bf16[64,72,128]{2,1,0:T(8,128)(2,1)}), bf16[64,72,128]{2,1,0:T(8,128)(2,1)S(1)}, u32[]{:S(2)}, u32[]{:S(2)}) async-start(bf16[64,72,128]{2,1,0:T(8,128)(2,1)} %weight_exchange.1), calls=%async_computation.1 | async-start | bytes 2359296 | tf_op jit(solution)/shard_map/weight_exchange/all_to_all | solution.py:208
  27.7 0.1 broadcast_select_fusion
  27.8 5.0 %collective-permute-start = (f32[16,128]{1,0:T(8,128)S(1)}, f32[16,128]{1,0:T(8,128)S(1)}, u32[]{:S(2)}, u32[]{:S(2)}) collective-permute-start(f32[16,128]{1,0:T(8,128)S(1)} %broadcast_select_fusion), channel_id=1, source_target_pairs={{0,4},{1,5},{2,6},{3,7},{4,0},{5,1},{6,2},{7,3},{8,12},{9,13},{10,... | collective-permute-start | bytes 24584 | tf_op jit(solution)/shard_map/channel_maxima/ppermute | solution.py:171
  32.8 18.1 %collective-permute-done = f32[16,128]{1,0:T(8,128)S(1)} collective-permute-done((f32[16,128]{1,0:T(8,128)S(1)}, f32[16,128]{1,0:T(8,128)S(1)}, u32[]{:S(2)}, u32[]{:S(2)}) %collective-permute-start) | collective-permute-done | bytes 8224 | tf_op jit(solution)/shard_map/channel_maxima/ppermute | solution.py:171
  51.0 0.1 maximum_select_fusion.sums_ref
  51.1 0.0 copy-done
  51.1 0.0 copy-done.1
  51.1 0.0 copy-done.2
  51.1 0.0 copy-done.3
  51.1 1.6 %channel_maxima.1 = f32[24,128]{1,0:T(8,128)S(1)} custom-call(s32[2]{0:T(128)S(1)} %copy-done.3, f32[16,128]{1,0:T(8,128)S(1)} %maximum_select_fusion.sums_ref, bf16[512,1536]{1,0:T(8,128)(2,1)S(1)} %copy-done, f32[12,128]{1,0:T(8,128)S(1)} %bitcast.4, f32[12,128]{1,0:T(8,128)S(1)} %bitcast.6), custom_call_target="tpu_custom_call" | custom-call | tf_op jit(solution)/shard_map/channel_maxima/pallas_call | solution.py:214
  52.7 1.9 %collective-permute-start.1 = (f32[24,128]{1,0:T(8,128)S(1)}, f32[24,128]{1,0:T(8,128)S(1)}, u32[]{:S(2)}, u32[]{:S(2)}) collective-permute-start(f32[24,128]{1,0:T(8,128)S(1)} %channel_maxima.1), channel_id=1, source_target_pairs={{0,8},{8,0},{16,24},{24,16},{32,40},{40,32},{48,56},{56,48},{64,72... | collective-permute-start | bytes 36872 | tf_op jit(solution)/shard_map/channel_maxima/ppermute | solution.py:171
  54.6 1.1 %collective-permute-done.1 = f32[24,128]{1,0:T(8,128)S(1)} collective-permute-done((f32[24,128]{1,0:T(8,128)S(1)}, f32[24,128]{1,0:T(8,128)S(1)}, u32[]{:S(2)}, u32[]{:S(2)}) %collective-permute-start.1) | collective-permute-done | bytes 12320 | tf_op jit(solution)/shard_map/channel_maxima/ppermute | solution.py:171
  55.7 1.9 %collective-permute-start.2 = (f32[24,128]{1,0:T(8,128)S(1)}, f32[24,128]{1,0:T(8,128)S(1)}, u32[]{:S(2)}, u32[]{:S(2)}) collective-permute-start(f32[24,128]{1,0:T(8,128)S(1)} %max.16), channel_id=1, source_target_pairs={{0,16},{8,24},{16,0},{24,8},{32,48},{40,56},{48,32},{56,40},{64,80... | collective-permute-start | bytes 36872 | tf_op jit(solution)/shard_map/channel_maxima/ppermute | solution.py:171
  57.7 3.7 %collective-permute-done.2 = f32[24,128]{1,0:T(8,128)S(1)} collective-permute-done((f32[24,128]{1,0:T(8,128)S(1)}, f32[24,128]{1,0:T(8,128)S(1)}, u32[]{:S(2)}, u32[]{:S(2)}) %collective-permute-start.2) | collective-permute-done | bytes 12320 | tf_op jit(solution)/shard_map/channel_maxima/ppermute | solution.py:171
  61.3 1.9 %collective-permute-start.3 = (f32[24,128]{1,0:T(8,128)S(1)}, f32[24,128]{1,0:T(8,128)S(1)}, u32[]{:S(2)}, u32[]{:S(2)}) collective-permute-start(f32[24,128]{1,0:T(8,128)S(1)} %max.17), channel_id=1, source_target_pairs={{0,32},{8,40},{16,48},{24,56},{32,0},{40,8},{48,16},{56,24},{64,96... | collective-permute-start | bytes 36872 | tf_op jit(solution)/shard_map/channel_maxima/ppermute | solution.py:171
  63.2 4.6 %collective-permute-done.3 = f32[24,128]{1,0:T(8,128)S(1)} collective-permute-done((f32[24,128]{1,0:T(8,128)S(1)}, f32[24,128]{1,0:T(8,128)S(1)}, u32[]{:S(2)}, u32[]{:S(2)}) %collective-permute-start.3) | collective-permute-done | bytes 12320 | tf_op jit(solution)/shard_map/channel_maxima/ppermute | solution.py:171
  67.8 3.4 %collective-permute-start.4 = (f32[24,128]{1,0:T(8,128)S(1)}, f32[24,128]{1,0:T(8,128)S(1)}, u32[]{:S(2)}, u32[]{:S(2)}) collective-permute-start(f32[24,128]{1,0:T(8,128)S(1)} %max.18), channel_id=1, source_target_pairs={{0,64},{8,72},{16,80},{24,88},{32,96},{40,104},{48,112},{56,120},{... | collective-permute-start | bytes 36872 | tf_op jit(solution)/shard_map/channel_maxima/ppermute | solution.py:171
  71.2 2.2 %collective-permute-done.4 = f32[24,128]{1,0:T(8,128)S(1)} collective-permute-done((f32[24,128]{1,0:T(8,128)S(1)}, f32[24,128]{1,0:T(8,128)S(1)}, u32[]{:S(2)}, u32[]{:S(2)}) %collective-permute-start.4) | collective-permute-done | bytes 12320 | tf_op jit(solution)/shard_map/channel_maxima/ppermute | solution.py:171
  73.4 0.0 all-to-all-done.1.pages_ref
  73.4 14.6 %all_to_all.20.maxima_ref = f32[4,24,128]{2,1,0:T(8,128)S(1)} all-to-all(f32[4,24,128]{2,1,0:T(8,128)S(1)} %broadcast_in_dim.2), channel_id=1, replica_groups={{0,128,256,384},{8,136,264,392},{16,144,272,400},{24,152,280,408},{32,1..., dimensions={0} | all-to-all | bytes 98304 | tf_op jit(solution)/shard_map/channel_maxima/all_to_all | solution.py:226
  88.0 0.9 token_peaks.1
  89.0 14.8 %all_to_all.21.blocks_ref = f32[8,16,128]{2,1,0:T(8,128)S(1)} all-to-all(f32[8,16,128]{2,1,0:T(8,128)S(1)} %token_peaks.1), channel_id=1, replica_groups=mesh['dp'=64,'mp'=8] {'mp'}, dimensions={0} | all-to-all | bytes 131072 | tf_op jit(solution)/shard_map/token_peaks/all_to_all | solution.py:235
  103.8 2.3 %smoothed_weight.1 = (bf16[48,12288]{1,0:T(8,128)(2,1)}, f32[12,128]{1,0:T(8,128)}, f32[4,128]{1,0:T(4,128)}) custom-call(s32[2]{0:T(128)S(1)} %copy-done.3, f32[8,16,128]{2,1,0:T(8,128)S(1)} %all_to_all.21.blocks_ref, bf16[64,72,128]{2,1,0:T(8,128)(2,1)S(1)} %all-to-all-done.1.pages_ref), custom_call_target="tpu_custom_call" | custom-call | tf_op jit(solution)/shard_map/smoothed_weight/pallas_call | solution.py:237
  (7 shorter events, 0.0 us)
Async XLA Ops:
  3.8 9.8 %all-to-all-start = ((f32[4,16,128]{2,1,0:T(8,128)}), f32[4,16,128]{2,1,0:T(8,128)S(1)}, u32[]{:S(2)}, u32[]{:S(2)}) async-start(f32[4,16,128]{2,1,0:T(8,128)} %token_moments.1), calls=%async_computation | async-start | bytes 65536 | tf_op jit(solution)/shard_map/token_moments/all_to_all | solution.py:192
  11.0 40.1 %copy-start = (bf16[512,1536]{1,0:T(8,128)(2,1)S(1)}, bf16[512,1536]{1,0:T(8,128)(2,1)}, u32[]{:S(2)}) copy-start(bf16[512,1536]{1,0:T(8,128)(2,1)} %acts_ref.3) | copy-start | bytes 4718596
  11.0 40.1 %copy-start.1 = (f32[1536]{0:T(1024)S(1)}, f32[1536]{0:T(1024)}, u32[]{:S(2)}) copy-start(f32[1536]{0:T(1024)} %param.7) | copy-start | bytes 18436
  11.0 40.1 %copy-start.2 = (f32[1536]{0:T(1024)S(1)}, f32[1536]{0:T(1024)}, u32[]{:S(2)}) copy-start(f32[1536]{0:T(1024)} %param.8) | copy-start | bytes 18436
  11.0 40.1 %copy-start.3 = (s32[2]{0:T(128)S(1)}, s32[2]{0:T(128)}, u32[]{:S(2)}) copy-start(s32[2]{0:T(128)} %lengths_ref.3) | copy-start | bytes 28
  13.6 59.8 %all-to-all-start.1 = ((bf16[64,72,128]{2,1,0:T(8,128)(2,1)}), bf16[64,72,128]{2,1,0:T(8,128)(2,1)S(1)}, u32[]{:S(2)}, u32[]{:S(2)}) async-start(bf16[64,72,128]{2,1,0:T(8,128)(2,1)} %weight_exchange.1), calls=%async_computation.1 | async-start | bytes 2359296 | tf_op jit(solution)/shard_map/weight_exchange/all_to_all | solution.py:208
  27.8 23.2 %collective-permute-start = (f32[16,128]{1,0:T(8,128)S(1)}, f32[16,128]{1,0:T(8,128)S(1)}, u32[]{:S(2)}, u32[]{:S(2)}) collective-permute-start(f32[16,128]{1,0:T(8,128)S(1)} %broadcast_select_fusion), channel_id=1, source_target_pairs={{0,4},{1,5},{2,6},{3,7},{4,0},{5,1},{6,2},{7,3},{8,12},{9,13},{10,... | collective-permute-start | bytes 24584 | tf_op jit(solution)/shard_map/channel_maxima/ppermute | solution.py:171
  52.7 3.1 %collective-permute-start.1 = (f32[24,128]{1,0:T(8,128)S(1)}, f32[24,128]{1,0:T(8,128)S(1)}, u32[]{:S(2)}, u32[]{:S(2)}) collective-permute-start(f32[24,128]{1,0:T(8,128)S(1)} %channel_maxima.1), channel_id=1, source_target_pairs={{0,8},{8,0},{16,24},{24,16},{32,40},{40,32},{48,56},{56,48},{64,72... | collective-permute-start | bytes 36872 | tf_op jit(solution)/shard_map/channel_maxima/ppermute | solution.py:171
  55.7 5.6 %collective-permute-start.2 = (f32[24,128]{1,0:T(8,128)S(1)}, f32[24,128]{1,0:T(8,128)S(1)}, u32[]{:S(2)}, u32[]{:S(2)}) collective-permute-start(f32[24,128]{1,0:T(8,128)S(1)} %max.16), channel_id=1, source_target_pairs={{0,16},{8,24},{16,0},{24,8},{32,48},{40,56},{48,32},{56,40},{64,80... | collective-permute-start | bytes 36872 | tf_op jit(solution)/shard_map/channel_maxima/ppermute | solution.py:171
  61.3 6.5 %collective-permute-start.3 = (f32[24,128]{1,0:T(8,128)S(1)}, f32[24,128]{1,0:T(8,128)S(1)}, u32[]{:S(2)}, u32[]{:S(2)}) collective-permute-start(f32[24,128]{1,0:T(8,128)S(1)} %max.17), channel_id=1, source_target_pairs={{0,32},{8,40},{16,48},{24,56},{32,0},{40,8},{48,16},{56,24},{64,96... | collective-permute-start | bytes 36872 | tf_op jit(solution)/shard_map/channel_maxima/ppermute | solution.py:171
  67.8 5.6 %collective-permute-start.4 = (f32[24,128]{1,0:T(8,128)S(1)}, f32[24,128]{1,0:T(8,128)S(1)}, u32[]{:S(2)}, u32[]{:S(2)}) collective-permute-start(f32[24,128]{1,0:T(8,128)S(1)} %max.18), channel_id=1, source_target_pairs={{0,64},{8,72},{16,80},{24,88},{32,96},{40,104},{48,112},{56,120},{... | collective-permute-start | bytes 36872 | tf_op jit(solution)/shard_map/channel_maxima/ppermute | solution.py:171

commit v7 on v4

--- a/solution.py
+++ b/solution.py
@@ -21,7 +21,6 @@
     parity = lax.axis_index("dp") % 2
     low = lax.broadcasted_iota(jnp.int32, (24, 128), 1) < 64
     first = low == (parity == 0)
-    own = pl.ds(pl.multiple_of(192 * parity, 64), 192)
 
     def columns(step):
         return pl.ds(pl.multiple_of(384 * step, 128), 384)
@@ -36,26 +35,28 @@
     for step in range(8):
         fetch(step).start()
     rows_ref[...] = jnp.zeros_like(rows_ref)
+    own = pl.ds(pl.multiple_of(192 * parity, 64), 192)
 
     def pack(step, carry):
         fetch(step).wait()
-        w = jnp.abs(w_ref[:, columns(step)].astype(jnp.float32))
+        w = jnp.abs(w_ref[:, columns(step)])
         peak = jnp.maximum(jnp.maximum(w[:, 0:128], w[:, 128:256]), w[:, 256:384])
         rows_ref[own, :] = jnp.maximum(rows_ref[own, :], peak)
-        full = w_ref[pl.ds(pl.multiple_of(64 * parity, 64), 128), columns(step)].astype(jnp.float32).T
-        half = w_ref[pl.ds(pl.multiple_of(128 * (1 - parity), 64), 64), columns(step)].astype(jnp.float32)
-        twice = jnp.concatenate([half, half], axis=0).T
+        full = w_ref[pl.ds(pl.multiple_of(64 * parity, 64), 128), columns(step)].T
+        half = w_ref[pl.ds(pl.multiple_of(128 * (1 - parity), 64), 64), columns(step)]
+        twice = jnp.concatenate([half, half], axis=0).T.astype(jnp.float32)
         for peer in range(8):
             upper = twice[48 * peer : 48 * peer + 24]
             lower = twice[48 * peer + 24 : 48 * peer + 48]
-            page = jnp.concatenate([full[48 * peer : 48 * peer + 48], jnp.where(first, upper, lower)], axis=0)
-            page_ref[8 * step + peer] = page.astype(jnp.bfloat16)
+            halves = jnp.where(first, upper, lower).astype(jnp.bfloat16)
+            page_ref[8 * step + peer] = jnp.concatenate([full[48 * peer : 48 * peer + 48], halves], axis=0)
         store(step).start()
         return carry
 
     lax.fori_loop(0, 8, pack, 0)
     for block in range(3):
-        peak_ref[block : block + 1, :] = jnp.max(rows_ref[pl.ds(128 * block, 128), :].T, axis=0, keepdims=True)
+        rows = rows_ref[pl.ds(128 * block, 128), :].astype(jnp.float32)
+        peak_ref[block : block + 1, :] = jnp.max(rows.T, axis=0, keepdims=True)
     peak_ref[3:8, :] = jnp.zeros((5, 128), jnp.float32)
     for step in range(8):
         store(step).wait()
@@ -96,14 +97,13 @@
             peaks[tile] = jnp.maximum(peaks[tile], jnp.max(peak.reshape(16, 8, 128), axis=0))
     for tile in range(12):
         page_ref[tile : tile + 1, :] = jnp.max(peaks[tile], axis=0, keepdims=True)
-    kept = lax.axis_index("dp") // 8 == lax.axis_index("mp")
-    page_ref[12:15, :] = jnp.where(kept, sums_ref[8:11, :], 0.0)
+    page_ref[12:15, :] = sums_ref[8:11, :]
     page_ref[15:16, :] = jnp.zeros((1, 128), jnp.float32)
 
 
 def peak_kernel(maxima_ref, sums_ref, acts_ref, gain_ref, bias_ref, page_ref):
     columns = moments(sums_ref[...])
-    start = 4 * (lax.axis_index("mp") // 2)
+    start = 4 * lax.axis_index("mp")
     act = jnp.max(maxima_ref[:, 0:12, :], axis=0)
     for slot in range(4):
         page_ref[0, 3 * slot : 3 * slot + 3, :] = maxima_ref[start + slot, 12:15, :]
@@ -130,11 +130,11 @@
     low = lax.broadcasted_iota(jnp.int32, (24, 128), 1) < 64
 
     def store(step):
-        columns = pl.ds(pl.multiple_of(3072 * step, 128), 3072)
+        columns = pl.ds(1536 * step, 1536)
         return pltpu.make_async_copy(served_ref.at[:, columns], served_hbm.at[:, columns], sems.at[step])
 
-    for step in range(4):
-        for pair in range(8 * step, 8 * step + 8):
+    for step in range(8):
+        for pair in range(4 * step, 4 * step + 4):
             even = pages_ref[2 * pair].astype(jnp.float32)
             odd = pages_ref[2 * pair + 1].astype(jnp.float32)
             upper = jnp.where(low, even[48:72], odd[48:72])
@@ -151,7 +151,7 @@
     for block in range(4):
         valid = lane + 128 * (block % 2) < lengths_ref[block // 2]
         tok_ref[block : block + 1, :] = jnp.where(valid, peaks[block : block + 1], 0.0)
-    for step in range(4):
+    for step in range(8):
         store(step).wait()
 
 
@@ -175,7 +175,7 @@
             scratch_shapes=[
                 pltpu.VMEM((192, 3072), jnp.bfloat16),
                 pltpu.VMEM((64, 72, 128), jnp.bfloat16),
-                pltpu.VMEM((384, 128), jnp.float32),
+                pltpu.VMEM((384, 128), jnp.bfloat16),
                 pltpu.SemaphoreType.DMA((8,)),
                 pltpu.SemaphoreType.DMA((8,)),
             ],
@@ -202,11 +202,10 @@
             out_specs=VMEM_SPEC,
             compiler_params=params(),
         )(lengths, sums, acts, gain, bias)
-        for bit in (1, 8):
-            maxima = jnp.maximum(maxima, swap(maxima, "dp", bit))
+        maxima = jnp.maximum(maxima, swap(maxima, "dp", 1))
         maxima, pages = lax.optimization_barrier((maxima, pages))
-        copies = jnp.broadcast_to(maxima[None], (16, 16, 128))
-        kinds = [[16 * pair + 8 * plane + 2 * y + core for pair in range(4) for y in range(4)] for plane in (0, 1) for core in (0, 1)]
+        copies = jnp.broadcast_to(maxima[None], (32, 16, 128))
+        kinds = [[2 * chip + core for chip in range(32)] for core in range(2)]
         maxima = lax.all_to_all(copies, "dp", 0, 0, axis_index_groups=kinds, tiled=True)
     with jax.named_scope("token_peaks"):
         page = pl.pallas_call(
@@ -227,7 +226,7 @@
             ),
             in_specs=[SMEM_SPEC, VMEM_SPEC, VMEM_SPEC],
             out_specs=(ANY_SPEC, VMEM_SPEC, VMEM_SPEC),
-            scratch_shapes=[pltpu.VMEM((48, D), jnp.bfloat16), pltpu.SemaphoreType.DMA((4,))],
+            scratch_shapes=[pltpu.VMEM((48, D), jnp.bfloat16), pltpu.SemaphoreType.DMA((8,))],
             compiler_params=params(),
         )(lengths, blocks, pages)
     return served, scale.reshape(1536), tok.reshape(512)

time: 91.9 us -> 88.8 us (0.966)
  the two profiles are of different devices: /device:TPU:2 before, /device:TPU:1 now
where the time goes in v7:
time: 88.8 us; the launch traced here: 87.3 us
  blocking collectives  32.9 us (37%)
  starting transfers between devices  30.9 us (35%)
  waiting for transfers between devices  13.7 us (15%)
  Pallas kernels  8.76 us (10%)
    all_to_all x1, blocking collectives, body(): lax.all_to_all(copies, 'dp', 0, 0, axis_index_groups=kinds, tiled=True)  17.7 us
    all_to_all x1, starting transfers between devices, body(): pages = lax.all_to_all(packed, 'dp', 0, 0, tiled=True)  15.6 us
    ppermute x4, starting transfers between devices, swap(): return lax.ppermute(x, axis, [(i, i ^ bit) for i in range(size)])  15.3 us
    all_to_all x1, blocking collectives, body(): blocks = lax.all_to_all(page, 'mp', 0, 0, tiled=True)  15.2 us
    ppermute x4, waiting for transfers between devices, swap(): return lax.ppermute(x, axis, [(i, i ^ bit) for i in range(size)])  10.2 us
    all_to_all x1, waiting for transfers between devices, body(): pages = lax.all_to_all(packed, 'dp', 0, 0, tiled=True)  3.5 us
    pallas_call x1, Pallas kernels, body(): pl.pallas_call(pack_kernel, out_shape=(jax.ShapeDtypeStruct((64, 72, 128)...  3.42 us
    pallas_call x1, Pallas kernels, body(): pl.pallas_call(serve_kernel, out_shape=(jax.ShapeDtypeStruct((48, D), jnp...  2.36 us
  transfers between devices with their start and end apart: 5, of which 5 were waited for; matrix products, arithmetic and copies ran while one was open for 0% of the time, Pallas kernels for 2%

profile of v7, /device:TPU:1, one launch (start us, length us, event | category | flops | bytes accessed | tf_op | source)
XLA Modules:
  0.0 87.3 jit_solution(13400853851898025347)
XLA Ops:
  0.6 3.4 %weight_exchange.1 = (bf16[64,72,128]{2,1,0:T(8,128)(2,1)}, f32[8,128]{1,0:T(8,128)}) custom-call(bf16[192,3072]{1,0:T(8,128)(2,1)} %w_hbm.1), custom_call_target="tpu_custom_call" | custom-call | tf_op jit(solution)/shard_map/weight_exchange/pallas_call | solution.py:167
  4.1 0.0 copy-start
  4.1 0.0 copy-start.3
  4.1 15.6 %all-to-all-start = ((bf16[64,72,128]{2,1,0:T(8,128)(2,1)}), bf16[64,72,128]{2,1,0:T(8,128)(2,1)S(1)}, u32[]{:S(2)}, u32[]{:S(2)}) async-start(bf16[64,72,128]{2,1,0:T(8,128)(2,1)} %get-tuple-element.11), calls=%async_computation | async-start | bytes 2359296 | tf_op jit(solution)/shard_map/weight_exchange/all_to_all | solution.py:184
  19.6 0.0 copy-start.1
  19.7 0.0 copy-start.2
  19.7 0.0 copy-start.4
  19.7 0.0 copy-done
  19.7 0.0 copy-done.3
  19.7 0.5 token_moments.1
  20.2 3.1 %collective-permute-start = (f32[16,128]{1,0:T(8,128)S(1)}, f32[16,128]{1,0:T(8,128)S(1)}, u32[]{:S(2)}, u32[]{:S(2)}) collective-permute-start(f32[16,128]{1,0:T(8,128)S(1)} %token_moments.1), channel_id=1, source_target_pairs={{0,1},{1,0},{2,3},{3,2},{4,5},{5,4},{6,7},{7,6},{8,9},{9,8},{10,11... | collective-permute-start | bytes 24584 | tf_op jit(solution)/shard_map/token_moments/ppermute | solution.py:160
  23.3 1.6 %collective-permute-done = f32[16,128]{1,0:T(8,128)S(1)} collective-permute-done((f32[16,128]{1,0:T(8,128)S(1)}, f32[16,128]{1,0:T(8,128)S(1)}, u32[]{:S(2)}, u32[]{:S(2)}) %collective-permute-start) | collective-permute-done | bytes 8224 | tf_op jit(solution)/shard_map/token_moments/ppermute | solution.py:160
  24.9 0.1 maximum_select_fusion.2
  24.9 4.6 %collective-permute-start.1 = (f32[16,128]{1,0:T(8,128)S(1)}, f32[16,128]{1,0:T(8,128)S(1)}, u32[]{:S(2)}, u32[]{:S(2)}) collective-permute-start(f32[16,128]{1,0:T(8,128)S(1)} %maximum_select_fusion.2), channel_id=1, source_target_pairs={{0,2},{1,3},{2,0},{3,1},{4,6},{5,7},{6,4},{7,5},{8,10},{9,11},{10,... | collective-permute-start | bytes 24584 | tf_op jit(solution)/shard_map/token_moments/ppermute | solution.py:160
  29.6 1.5 %collective-permute-done.1 = f32[16,128]{1,0:T(8,128)S(1)} collective-permute-done((f32[16,128]{1,0:T(8,128)S(1)}, f32[16,128]{1,0:T(8,128)S(1)}, u32[]{:S(2)}, u32[]{:S(2)}) %collective-permute-start.1) | collective-permute-done | bytes 8224 | tf_op jit(solution)/shard_map/token_moments/ppermute | solution.py:160
  31.1 0.1 maximum_select_fusion.1
  31.2 4.7 %collective-permute-start.2 = (f32[16,128]{1,0:T(8,128)S(1)}, f32[16,128]{1,0:T(8,128)S(1)}, u32[]{:S(2)}, u32[]{:S(2)}) collective-permute-start(f32[16,128]{1,0:T(8,128)S(1)} %maximum_select_fusion.1), channel_id=1, source_target_pairs={{0,4},{1,5},{2,6},{3,7},{4,0},{5,1},{6,2},{7,3},{8,12},{9,13},{10,... | collective-permute-start | bytes 24584 | tf_op jit(solution)/shard_map/token_moments/ppermute | solution.py:160
  36.0 6.3 %collective-permute-done.2 = f32[16,128]{1,0:T(8,128)S(1)} collective-permute-done((f32[16,128]{1,0:T(8,128)S(1)}, f32[16,128]{1,0:T(8,128)S(1)}, u32[]{:S(2)}, u32[]{:S(2)}) %collective-permute-start.2) | collective-permute-done | bytes 8224 | tf_op jit(solution)/shard_map/token_moments/ppermute | solution.py:160
  42.3 0.1 maximum_select_fusion.sums_ref
  42.4 0.0 copy-done.1
  42.4 0.0 copy-done.2
  42.4 0.0 copy-done.4
  42.4 1.6 %channel_maxima.1 = f32[16,128]{1,0:T(8,128)S(1)} custom-call(s32[2]{0:T(128)S(1)} %copy-done.4, f32[16,128]{1,0:T(8,128)S(1)} %maximum_select_fusion.sums_ref, bf16[512,1536]{1,0:T(8,128)(2,1)S(1)} %copy-done, f32[12,128]{1,0:T(8,128)S(1)} %bitcast.4, f32[12,128]{1,0:T(8,128)S(1)} %bitcast.6), custom_call_target="tpu_custom_call" | custom-call | tf_op jit(solution)/shard_map/channel_maxima/pallas_call | solution.py:198
  43.9 2.8 %collective-permute-start.3 = (f32[16,128]{1,0:T(8,128)S(1)}, f32[16,128]{1,0:T(8,128)S(1)}, u32[]{:S(2)}, u32[]{:S(2)}) collective-permute-start(f32[16,128]{1,0:T(8,128)S(1)} %channel_maxima.1), channel_id=1, source_target_pairs={{0,8},{8,0},{16,24},{24,16},{32,40},{40,32},{48,56},{56,48},{64,72... | collective-permute-start | bytes 24584 | tf_op jit(solution)/shard_map/channel_maxima/ppermute | solution.py:160
  46.8 0.8 collective-permute-done.3
  47.6 3.5 %all-to-all-done.pages_ref = bf16[64,72,128]{2,1,0:T(8,128)(2,1)S(1)} async-done(((bf16[64,72,128]{2,1,0:T(8,128)(2,1)}), bf16[64,72,128]{2,1,0:T(8,128)(2,1)S(1)}, u32[]{:S(2)}, u32[]{:S(2)}) %all-to-all-start) | async-done | bytes 1179680 | tf_op jit(solution)/shard_map/weight_exchange/all_to_all | solution.py:184
  51.1 17.7 %all_to_all.15.maxima_ref = f32[32,16,128]{2,1,0:T(8,128)S(1)} all-to-all(f32[32,16,128]{2,1,0:T(8,128)S(1)} %broadcast_in_dim.2), channel_id=1, replica_groups={{0,16,32,48,64,80,96,112,128,144,160,176,192,208,224,240,256,272,288,30..., dimensions={0} | all-to-all | bytes 524288 | tf_op jit(solution)/shard_map/channel_maxima/all_to_all | solution.py:209
  68.8 0.9 %token_peaks.1 = f32[8,16,128]{2,1,0:T(8,128)S(1)} custom-call(f32[32,16,128]{2,1,0:T(8,128)S(1)} %all_to_all.15.maxima_ref, f32[16,128]{1,0:T(8,128)S(1)} %maximum_select_fusion.sums_ref, bf16[512,1536]{1,0:T(8,128)(2,1)S(1)} %copy-done, f32[12,128]{1,0:T(8,128)S(1)} %bitcast.5, f32[12,128]{1,0:T(8,128)S(1)} %bitcast.7), custom_call_target="tpu_custom_call" | custom-call | tf_op jit(solution)/shard_map/token_peaks/pallas_call | solution.py:211
  69.8 15.2 %all_to_all.16.blocks_ref = f32[8,16,128]{2,1,0:T(8,128)S(1)} all-to-all(f32[8,16,128]{2,1,0:T(8,128)S(1)} %token_peaks.1), channel_id=1, replica_groups=mesh['dp'=64,'mp'=8] {'mp'}, dimensions={0} | all-to-all | bytes 131072 | tf_op jit(solution)/shard_map/token_peaks/all_to_all | solution.py:218
  84.9 2.4 %smoothed_weight.1 = (bf16[48,12288]{1,0:T(8,128)(2,1)}, f32[12,128]{1,0:T(8,128)}, f32[4,128]{1,0:T(4,128)}) custom-call(s32[2]{0:T(128)S(1)} %copy-done.4, f32[8,16,128]{2,1,0:T(8,128)S(1)} %all_to_all.16.blocks_ref, bf16[64,72,128]{2,1,0:T(8,128)(2,1)S(1)} %all-to-all-done.pages_ref), custom_call_target="tpu_custom_call" | custom-call | tf_op jit(solution)/shard_map/smoothed_weight/pallas_call | solution.py:220
  (3 shorter events, 0.0 us)
Async XLA Ops:
  4.1 15.6 %copy-start = (bf16[512,1536]{1,0:T(8,128)(2,1)S(1)}, bf16[512,1536]{1,0:T(8,128)(2,1)}, u32[]{:S(2)}) copy-start(bf16[512,1536]{1,0:T(8,128)(2,1)} %acts_ref.5) | copy-start | bytes 4718596
  4.1 15.6 %copy-start.3 = (f32[8,128]{1,0:T(8,128)S(1)}, f32[8,128]{1,0:T(8,128)}, u32[]{:S(2)}) copy-start(f32[8,128]{1,0:T(8,128)} %get-tuple-element.10.peak_ref) | copy-start | bytes 12292
  4.1 47.0 %all-to-all-start = ((bf16[64,72,128]{2,1,0:T(8,128)(2,1)}), bf16[64,72,128]{2,1,0:T(8,128)(2,1)S(1)}, u32[]{:S(2)}, u32[]{:S(2)}) async-start(bf16[64,72,128]{2,1,0:T(8,128)(2,1)} %get-tuple-element.11), calls=%async_computation | async-start | bytes 2359296 | tf_op jit(solution)/shard_map/weight_exchange/all_to_all | solution.py:184
  19.6 22.7 %copy-start.1 = (f32[1536]{0:T(1024)S(1)}, f32[1536]{0:T(1024)}, u32[]{:S(2)}) copy-start(f32[1536]{0:T(1024)} %param.7) | copy-start | bytes 18436
  19.7 22.7 %copy-start.2 = (f32[1536]{0:T(1024)S(1)}, f32[1536]{0:T(1024)}, u32[]{:S(2)}) copy-start(f32[1536]{0:T(1024)} %param.8) | copy-start | bytes 18436
  19.7 22.7 %copy-start.4 = (s32[2]{0:T(128)S(1)}, s32[2]{0:T(128)}, u32[]{:S(2)}) copy-start(s32[2]{0:T(128)} %lengths_ref.3) | copy-start | bytes 28
  20.2 4.7 %collective-permute-start = (f32[16,128]{1,0:T(8,128)S(1)}, f32[16,128]{1,0:T(8,128)S(1)}, u32[]{:S(2)}, u32[]{:S(2)}) collective-permute-start(f32[16,128]{1,0:T(8,128)S(1)} %token_moments.1), channel_id=1, source_target_pairs={{0,1},{1,0},{2,3},{3,2},{4,5},{5,4},{6,7},{7,6},{8,9},{9,8},{10,11... | collective-permute-start | bytes 24584 | tf_op jit(solution)/shard_map/token_moments/ppermute | solution.py:160
  24.9 6.2 %collective-permute-start.1 = (f32[16,128]{1,0:T(8,128)S(1)}, f32[16,128]{1,0:T(8,128)S(1)}, u32[]{:S(2)}, u32[]{:S(2)}) collective-permute-start(f32[16,128]{1,0:T(8,128)S(1)} %maximum_select_fusion.2), channel_id=1, source_target_pairs={{0,2},{1,3},{2,0},{3,1},{4,6},{5,7},{6,4},{7,5},{8,10},{9,11},{10,... | collective-permute-start | bytes 24584 | tf_op jit(solution)/shard_map/token_moments/ppermute | solution.py:160
  31.2 11.1 %collective-permute-start.2 = (f32[16,128]{1,0:T(8,128)S(1)}, f32[16,128]{1,0:T(8,128)S(1)}, u32[]{:S(2)}, u32[]{:S(2)}) collective-permute-start(f32[16,128]{1,0:T(8,128)S(1)} %maximum_select_fusion.1), channel_id=1, source_target_pairs={{0,4},{1,5},{2,6},{3,7},{4,0},{5,1},{6,2},{7,3},{8,12},{9,13},{10,... | collective-permute-start | bytes 24584 | tf_op jit(solution)/shard_map/token_moments/ppermute | solution.py:160
  43.9 3.6 %collective-permute-start.3 = (f32[16,128]{1,0:T(8,128)S(1)}, f32[16,128]{1,0:T(8,128)S(1)}, u32[]{:S(2)}, u32[]{:S(2)}) collective-permute-start(f32[16,128]{1,0:T(8,128)S(1)} %channel_maxima.1), channel_id=1, source_target_pairs={{0,8},{8,0},{16,24},{24,16},{32,40},{40,32},{48,56},{56,48},{64,72... | collective-permute-start | bytes 24584 | tf_op jit(solution)/shard_map/channel_maxima/ppermute | solution.py:160

commit v8 on v7

--- a/solution.py
+++ b/solution.py
@@ -17,7 +17,7 @@
     return pltpu.CompilerParams(vmem_limit_bytes=mebibytes * 1024 * 1024)
 
 
-def pack_kernel(w_hbm, page_hbm, peak_ref, w_ref, page_ref, rows_ref, in_sems, out_sems):
+def pack_kernel(w_hbm, page_hbm, w_ref, page_ref, in_sems, out_sems):
     parity = lax.axis_index("dp") % 2
     low = lax.broadcasted_iota(jnp.int32, (24, 128), 1) < 64
     first = low == (parity == 0)
@@ -34,14 +34,9 @@
 
     for step in range(8):
         fetch(step).start()
-    rows_ref[...] = jnp.zeros_like(rows_ref)
-    own = pl.ds(pl.multiple_of(192 * parity, 64), 192)
 
     def pack(step, carry):
         fetch(step).wait()
-        w = jnp.abs(w_ref[:, columns(step)])
-        peak = jnp.maximum(jnp.maximum(w[:, 0:128], w[:, 128:256]), w[:, 256:384])
-        rows_ref[own, :] = jnp.maximum(rows_ref[own, :], peak)
         full = w_ref[pl.ds(pl.multiple_of(64 * parity, 64), 128), columns(step)].T
         half = w_ref[pl.ds(pl.multiple_of(128 * (1 - parity), 64), 64), columns(step)]
         twice = jnp.concatenate([half, half], axis=0).T.astype(jnp.float32)
@@ -54,16 +49,19 @@
         return carry
 
     lax.fori_loop(0, 8, pack, 0)
+    for step in range(8):
+        store(step).wait()
+
+
+def stats_kernel(acts_ref, w_ref, page_ref, rows_ref):
+    rows_ref[...] = jnp.zeros_like(rows_ref)
+    peak = jnp.zeros((192, 128), jnp.bfloat16)
+    for tile in range(24):
+        peak = jnp.maximum(peak, jnp.abs(w_ref[:, pl.ds(128 * tile, 128)]))
+    rows_ref[pl.ds(pl.multiple_of(192 * (lax.axis_index("dp") % 2), 64), 192), :] = peak.astype(jnp.float32)
     for block in range(3):
-        rows = rows_ref[pl.ds(128 * block, 128), :].astype(jnp.float32)
-        peak_ref[block : block + 1, :] = jnp.max(rows.T, axis=0, keepdims=True)
-    peak_ref[3:8, :] = jnp.zeros((5, 128), jnp.float32)
-    for step in range(8):
-        store(step).wait()
-
-
-def stats_kernel(peak_ref, acts_ref, page_ref):
-    page_ref[8:16, :] = peak_ref[...]
+        page_ref[8 + block : 9 + block, :] = jnp.max(rows_ref[pl.ds(128 * block, 128), :].T, axis=0, keepdims=True)
+    page_ref[11:16, :] = jnp.zeros((5, 128), jnp.float32)
     for block in range(4):
         total = jnp.zeros((128, 128), jnp.float32)
         square = jnp.zeros((128, 128), jnp.float32)
@@ -164,18 +162,14 @@
     gain = ln_gain.reshape(12, 128)
     bias = ln_bias.reshape(12, 128)
     with jax.named_scope("weight_exchange"):
-        packed, w_peak = pl.pallas_call(
+        packed = pl.pallas_call(
             pack_kernel,
-            out_shape=(
-                jax.ShapeDtypeStruct((64, 72, 128), jnp.bfloat16),
-                jax.ShapeDtypeStruct((8, 128), jnp.float32),
-            ),
+            out_shape=jax.ShapeDtypeStruct((64, 72, 128), jnp.bfloat16),
             in_specs=[ANY_SPEC],
-            out_specs=(ANY_SPEC, VMEM_SPEC),
+            out_specs=ANY_SPEC,
             scratch_shapes=[
                 pltpu.VMEM((192, 3072), jnp.bfloat16),
                 pltpu.VMEM((64, 72, 128), jnp.bfloat16),
-                pltpu.VMEM((384, 128), jnp.bfloat16),
                 pltpu.SemaphoreType.DMA((8,)),
                 pltpu.SemaphoreType.DMA((8,)),
             ],
@@ -188,8 +182,9 @@
             out_shape=jax.ShapeDtypeStruct((16, 128), jnp.float32),
             in_specs=[VMEM_SPEC, VMEM_SPEC],
             out_specs=VMEM_SPEC,
-            compiler_params=params(),
-        )(w_peak, acts)
+            scratch_shapes=[pltpu.VMEM((384, 128), jnp.float32)],
+            compiler_params=params(),
+        )(acts, w_fc1)
         added = lax.broadcasted_iota(jnp.int32, (16, 128), 0) < 8
         for bit in (1, 2, 4):
             other = swap(sums, "mp", bit)

time: 88.8 us -> 89.4 us (level)
  waiting for transfers between devices: 13.7 us -> 11 us
  blocking collectives: 32.9 us -> 34.3 us
  local copies, waits for them, and re-layouts: 0.05 us -> 1.3 us
  starting transfers between devices: 30.9 us -> 32.1 us
    ppermute x4, waiting for transfers between devices: 10.2 us -> 8.75 us  [swap(): return lax.ppermute(x, axis, [(i, i ^ bit) for i in range(size)])]
    unnamed x10, local copies, waits for them, and re-layouts: 0.03 us -> 1.28 us
    all_to_all x1, waiting for transfers between devices: 3.5 us -> 2.28 us  [body(): pages = lax.all_to_all(packed, 'dp', 0, 0, tiled=True)]
    ppermute x4, starting transfers between devices: 15.3 us -> 16.5 us  [swap(): return lax.ppermute(x, axis, [(i, i ^ bit) for i in range(size)])]
    all_to_all x1, blocking collectives: 17.7 us -> 18.8 us  [body(): lax.all_to_all(copies, 'dp', 0, 0, axis_index_groups=kinds, tiled=True)]
  transfers between devices with their start and end apart: 5 -> 5, of which waited for: 5 -> 5; matrix products, arithmetic and copies ran while one was open for 0% -> 0% of each run, Pallas kernels for 2% -> 3%
where the time goes in v8:
time: 89.4 us; the launch traced here: 87.9 us
  blocking collectives  34.3 us (38%)
  starting transfers between devices  32.1 us (36%)
  waiting for transfers between devices  11 us (12%)
  Pallas kernels  8.17 us (9%)
  local copies, waits for them, and re-layouts  1.3 us (1%)
    all_to_all x1, blocking collectives, body(): lax.all_to_all(copies, 'dp', 0, 0, axis_index_groups=kinds, tiled=True)  18.8 us
    ppermute x4, starting transfers between devices, swap(): return lax.ppermute(x, axis, [(i, i ^ bit) for i in range(size)])  16.5 us
    all_to_all x1, starting transfers between devices, body(): pages = lax.all_to_all(packed, 'dp', 0, 0, tiled=True)  15.6 us
    all_to_all x1, blocking collectives, body(): blocks = lax.all_to_all(page, 'mp', 0, 0, tiled=True)  15.5 us
    ppermute x4, waiting for transfers between devices, swap(): return lax.ppermute(x, axis, [(i, i ^ bit) for i in range(size)])  8.75 us
    pallas_call x1, Pallas kernels, body(): pl.pallas_call(pack_kernel, out_shape=jax.ShapeDtypeStruct((64, 72, 128),...  2.59 us
    pallas_call x1, Pallas kernels, body(): pl.pallas_call(serve_kernel, out_shape=(jax.ShapeDtypeStruct((48, D), jnp...  2.36 us
    all_to_all x1, waiting for transfers between devices, body(): pages = lax.all_to_all(packed, 'dp', 0, 0, tiled=True)  2.28 us
  transfers between devices with their start and end apart: 5, of which 5 were waited for; matrix products, arithmetic and copies ran while one was open for 0% of the time, Pallas kernels for 3%

profile of v8, /device:TPU:1, one launch (start us, length us, event | category | flops | bytes accessed | tf_op | source)
XLA Modules:
  0.0 87.9 jit_solution(9632267088305297775)
XLA Ops:
  0.6 2.6 %weight_exchange.1 = bf16[64,72,128]{2,1,0:T(8,128)(2,1)} custom-call(bf16[192,3072]{1,0:T(8,128)(2,1)} %w_hbm.1), custom_call_target="tpu_custom_call" | custom-call | tf_op jit(solution)/shard_map/weight_exchange/pallas_call | solution.py:165
  3.2 0.0 copy-start
  3.2 15.6 %all-to-all-start = ((bf16[64,72,128]{2,1,0:T(8,128)(2,1)}), bf16[64,72,128]{2,1,0:T(8,128)(2,1)S(1)}, u32[]{:S(2)}, u32[]{:S(2)}) async-start(bf16[64,72,128]{2,1,0:T(8,128)(2,1)} %weight_exchange.1), calls=%async_computation | async-start | bytes 2359296 | tf_op jit(solution)/shard_map/weight_exchange/all_to_all | solution.py:178
  18.8 0.0 copy-done
  18.8 0.0 copy-start.1
  18.8 1.3 %copy-done.1 = bf16[192,3072]{1,0:T(8,128)(2,1)S(1)} copy-done((bf16[192,3072]{1,0:T(8,128)(2,1)S(1)}, bf16[192,3072]{1,0:T(8,128)(2,1)}, u32[]{:S(2)}) %copy-start.1) | copy-done | bytes 1179672
  20.1 0.0 copy-start.2
  20.1 0.0 copy-start.3
  20.1 0.0 copy-start.4
  20.1 0.7 token_moments.1
  20.8 3.1 %collective-permute-start = (f32[16,128]{1,0:T(8,128)S(1)}, f32[16,128]{1,0:T(8,128)S(1)}, u32[]{:S(2)}, u32[]{:S(2)}) collective-permute-start(f32[16,128]{1,0:T(8,128)S(1)} %token_moments.1), channel_id=1, source_target_pairs={{0,1},{1,0},{2,3},{3,2},{4,5},{5,4},{6,7},{7,6},{8,9},{9,8},{10,11... | collective-permute-start | bytes 24584 | tf_op jit(solution)/shard_map/token_moments/ppermute | solution.py:158
  23.9 1.6 %collective-permute-done = f32[16,128]{1,0:T(8,128)S(1)} collective-permute-done((f32[16,128]{1,0:T(8,128)S(1)}, f32[16,128]{1,0:T(8,128)S(1)}, u32[]{:S(2)}, u32[]{:S(2)}) %collective-permute-start) | collective-permute-done | bytes 8224 | tf_op jit(solution)/shard_map/token_moments/ppermute | solution.py:158
  25.5 0.1 maximum_select_fusion.2
  25.6 4.6 %collective-permute-start.1 = (f32[16,128]{1,0:T(8,128)S(1)}, f32[16,128]{1,0:T(8,128)S(1)}, u32[]{:S(2)}, u32[]{:S(2)}) collective-permute-start(f32[16,128]{1,0:T(8,128)S(1)} %maximum_select_fusion.2), channel_id=1, source_target_pairs={{0,2},{1,3},{2,0},{3,1},{4,6},{5,7},{6,4},{7,5},{8,10},{9,11},{10,... | collective-permute-start | bytes 24584 | tf_op jit(solution)/shard_map/token_moments/ppermute | solution.py:158
  30.2 1.5 %collective-permute-done.1 = f32[16,128]{1,0:T(8,128)S(1)} collective-permute-done((f32[16,128]{1,0:T(8,128)S(1)}, f32[16,128]{1,0:T(8,128)S(1)}, u32[]{:S(2)}, u32[]{:S(2)}) %collective-permute-start.1) | collective-permute-done | bytes 8224 | tf_op jit(solution)/shard_map/token_moments/ppermute | solution.py:158
  31.8 0.1 maximum_select_fusion.1
  31.8 4.7 %collective-permute-start.2 = (f32[16,128]{1,0:T(8,128)S(1)}, f32[16,128]{1,0:T(8,128)S(1)}, u32[]{:S(2)}, u32[]{:S(2)}) collective-permute-start(f32[16,128]{1,0:T(8,128)S(1)} %maximum_select_fusion.1), channel_id=1, source_target_pairs={{0,4},{1,5},{2,6},{3,7},{4,0},{5,1},{6,2},{7,3},{8,12},{9,13},{10,... | collective-permute-start | bytes 24584 | tf_op jit(solution)/shard_map/token_moments/ppermute | solution.py:158
  36.6 4.9 %collective-permute-done.2 = f32[16,128]{1,0:T(8,128)S(1)} collective-permute-done((f32[16,128]{1,0:T(8,128)S(1)}, f32[16,128]{1,0:T(8,128)S(1)}, u32[]{:S(2)}, u32[]{:S(2)}) %collective-permute-start.2) | collective-permute-done | bytes 8224 | tf_op jit(solution)/shard_map/token_moments/ppermute | solution.py:158
  41.4 0.1 maximum_select_fusion.sums_ref
  41.5 0.0 copy-done.2
  41.5 0.0 copy-done.3
  41.5 0.0 copy-done.4
  41.5 1.6 %channel_maxima.1 = f32[16,128]{1,0:T(8,128)S(1)} custom-call(s32[2]{0:T(128)S(1)} %copy-done.4, f32[16,128]{1,0:T(8,128)S(1)} %maximum_select_fusion.sums_ref, bf16[512,1536]{1,0:T(8,128)(2,1)S(1)} %copy-done, f32[12,128]{1,0:T(8,128)S(1)} %bitcast.4, f32[12,128]{1,0:T(8,128)S(1)} %bitcast.6), custom_call_target="tpu_custom_call" | custom-call | tf_op jit(solution)/shard_map/channel_maxima/pallas_call | solution.py:193
  43.1 4.0 %collective-permute-start.3 = (f32[16,128]{1,0:T(8,128)S(1)}, f32[16,128]{1,0:T(8,128)S(1)}, u32[]{:S(2)}, u32[]{:S(2)}) collective-permute-start(f32[16,128]{1,0:T(8,128)S(1)} %channel_maxima.1), channel_id=1, source_target_pairs={{0,8},{8,0},{16,24},{24,16},{32,40},{40,32},{48,56},{56,48},{64,72... | collective-permute-start | bytes 24584 | tf_op jit(solution)/shard_map/channel_maxima/ppermute | solution.py:158
  47.1 0.8 collective-permute-done.3
  48.0 2.3 %all-to-all-done.pages_ref = bf16[64,72,128]{2,1,0:T(8,128)(2,1)S(1)} async-done(((bf16[64,72,128]{2,1,0:T(8,128)(2,1)}), bf16[64,72,128]{2,1,0:T(8,128)(2,1)S(1)}, u32[]{:S(2)}, u32[]{:S(2)}) %all-to-all-start) | async-done | bytes 1179680 | tf_op jit(solution)/shard_map/weight_exchange/all_to_all | solution.py:178
  50.3 18.8 %all_to_all.15.maxima_ref = f32[32,16,128]{2,1,0:T(8,128)S(1)} all-to-all(f32[32,16,128]{2,1,0:T(8,128)S(1)} %broadcast_in_dim.2), channel_id=1, replica_groups={{0,16,32,48,64,80,96,112,128,144,160,176,192,208,224,240,256,272,288,30..., dimensions={0} | all-to-all | bytes 524288 | tf_op jit(solution)/shard_map/channel_maxima/all_to_all | solution.py:204
  69.1 0.9 %token_peaks.1 = f32[8,16,128]{2,1,0:T(8,128)S(1)} custom-call(f32[32,16,128]{2,1,0:T(8,128)S(1)} %all_to_all.15.maxima_ref, f32[16,128]{1,0:T(8,128)S(1)} %maximum_select_fusion.sums_ref, bf16[512,1536]{1,0:T(8,128)(2,1)S(1)} %copy-done, f32[12,128]{1,0:T(8,128)S(1)} %bitcast.5, f32[12,128]{1,0:T(8,128)S(1)} %bitcast.7), custom_call_target="tpu_custom_call" | custom-call | tf_op jit(solution)/shard_map/token_peaks/pallas_call | solution.py:206
  70.1 15.5 %all_to_all.16.blocks_ref = f32[8,16,128]{2,1,0:T(8,128)S(1)} all-to-all(f32[8,16,128]{2,1,0:T(8,128)S(1)} %token_peaks.1), channel_id=1, replica_groups=mesh['dp'=64,'mp'=8] {'mp'}, dimensions={0} | all-to-all | bytes 131072 | tf_op jit(solution)/shard_map/token_peaks/all_to_all | solution.py:213
  85.5 2.4 %smoothed_weight.1 = (bf16[48,12288]{1,0:T(8,128)(2,1)}, f32[12,128]{1,0:T(8,128)}, f32[4,128]{1,0:T(4,128)}) custom-call(s32[2]{0:T(128)S(1)} %copy-done.4, f32[8,16,128]{2,1,0:T(8,128)S(1)} %all_to_all.16.blocks_ref, bf16[64,72,128]{2,1,0:T(8,128)(2,1)S(1)} %all-to-all-done.pages_ref), custom_call_target="tpu_custom_call" | custom-call | tf_op jit(solution)/shard_map/smoothed_weight/pallas_call | solution.py:215
  (3 shorter events, 0.0 us)
Async XLA Ops:
  3.2 15.6 %copy-start = (bf16[512,1536]{1,0:T(8,128)(2,1)S(1)}, bf16[512,1536]{1,0:T(8,128)(2,1)}, u32[]{:S(2)}) copy-start(bf16[512,1536]{1,0:T(8,128)(2,1)} %acts_ref.5) | copy-start | bytes 4718596
  3.2 47.0 %all-to-all-start = ((bf16[64,72,128]{2,1,0:T(8,128)(2,1)}), bf16[64,72,128]{2,1,0:T(8,128)(2,1)S(1)}, u32[]{:S(2)}, u32[]{:S(2)}) async-start(bf16[64,72,128]{2,1,0:T(8,128)(2,1)} %weight_exchange.1), calls=%async_computation | async-start | bytes 2359296 | tf_op jit(solution)/shard_map/weight_exchange/all_to_all | solution.py:178
  18.8 1.3 %copy-start.1 = (bf16[192,3072]{1,0:T(8,128)(2,1)S(1)}, bf16[192,3072]{1,0:T(8,128)(2,1)}, u32[]{:S(2)}) copy-start(bf16[192,3072]{1,0:T(8,128)(2,1)} %w_hbm.1) | copy-start | bytes 3538948
  20.1 21.4 %copy-start.2 = (f32[1536]{0:T(1024)S(1)}, f32[1536]{0:T(1024)}, u32[]{:S(2)}) copy-start(f32[1536]{0:T(1024)} %param.7) | copy-start | bytes 18436
  20.1 21.4 %copy-start.3 = (f32[1536]{0:T(1024)S(1)}, f32[1536]{0:T(1024)}, u32[]{:S(2)}) copy-start(f32[1536]{0:T(1024)} %param.8) | copy-start | bytes 18436
  20.1 21.4 %copy-start.4 = (s32[2]{0:T(128)S(1)}, s32[2]{0:T(128)}, u32[]{:S(2)}) copy-start(s32[2]{0:T(128)} %lengths_ref.3) | copy-start | bytes 28
  20.8 4.7 %collective-permute-start = (f32[16,128]{1,0:T(8,128)S(1)}, f32[16,128]{1,0:T(8,128)S(1)}, u32[]{:S(2)}, u32[]{:S(2)}) collective-permute-start(f32[16,128]{1,0:T(8,128)S(1)} %token_moments.1), channel_id=1, source_target_pairs={{0,1},{1,0},{2,3},{3,2},{4,5},{5,4},{6,7},{7,6},{8,9},{9,8},{10,11... | collective-permute-start | bytes 24584 | tf_op jit(solution)/shard_map/token_moments/ppermute | solution.py:158
  25.6 6.2 %collective-permute-start.1 = (f32[16,128]{1,0:T(8,128)S(1)}, f32[16,128]{1,0:T(8,128)S(1)}, u32[]{:S(2)}, u32[]{:S(2)}) collective-permute-start(f32[16,128]{1,0:T(8,128)S(1)} %maximum_select_fusion.2), channel_id=1, source_target_pairs={{0,2},{1,3},{2,0},{3,1},{4,6},{5,7},{6,4},{7,5},{8,10},{9,11},{10,... | collective-permute-start | bytes 24584 | tf_op jit(solution)/shard_map/token_moments/ppermute | solution.py:158
  31.8 9.6 %collective-permute-start.2 = (f32[16,128]{1,0:T(8,128)S(1)}, f32[16,128]{1,0:T(8,128)S(1)}, u32[]{:S(2)}, u32[]{:S(2)}) collective-permute-start(f32[16,128]{1,0:T(8,128)S(1)} %maximum_select_fusion.1), channel_id=1, source_target_pairs={{0,4},{1,5},{2,6},{3,7},{4,0},{5,1},{6,2},{7,3},{8,12},{9,13},{10,... | collective-permute-start | bytes 24584 | tf_op jit(solution)/shard_map/token_moments/ppermute | solution.py:158
  43.1 4.9 %collective-permute-start.3 = (f32[16,128]{1,0:T(8,128)S(1)}, f32[16,128]{1,0:T(8,128)S(1)}, u32[]{:S(2)}, u32[]{:S(2)}) collective-permute-start(f32[16,128]{1,0:T(8,128)S(1)} %channel_maxima.1), channel_id=1, source_target_pairs={{0,8},{8,0},{16,24},{24,16},{32,40},{40,32},{48,56},{56,48},{64,72... | collective-permute-start | bytes 24584 | tf_op jit(solution)/shard_map/channel_maxima/ppermute | solution.py:158

commit v9 on v7

--- a/solution.py
+++ b/solution.py
@@ -35,13 +35,9 @@
     for step in range(8):
         fetch(step).start()
     rows_ref[...] = jnp.zeros_like(rows_ref)
-    own = pl.ds(pl.multiple_of(192 * parity, 64), 192)
 
     def pack(step, carry):
         fetch(step).wait()
-        w = jnp.abs(w_ref[:, columns(step)])
-        peak = jnp.maximum(jnp.maximum(w[:, 0:128], w[:, 128:256]), w[:, 256:384])
-        rows_ref[own, :] = jnp.maximum(rows_ref[own, :], peak)
         full = w_ref[pl.ds(pl.multiple_of(64 * parity, 64), 128), columns(step)].T
         half = w_ref[pl.ds(pl.multiple_of(128 * (1 - parity), 64), 64), columns(step)]
         twice = jnp.concatenate([half, half], axis=0).T.astype(jnp.float32)
@@ -54,9 +50,12 @@
         return carry
 
     lax.fori_loop(0, 8, pack, 0)
+    peak = jnp.zeros((192, 128), jnp.bfloat16)
+    for tile in range(24):
+        peak = jnp.maximum(peak, jnp.abs(w_ref[:, pl.ds(128 * tile, 128)]))
+    rows_ref[pl.ds(pl.multiple_of(192 * parity, 64), 192), :] = peak.astype(jnp.float32)
     for block in range(3):
-        rows = rows_ref[pl.ds(128 * block, 128), :].astype(jnp.float32)
-        peak_ref[block : block + 1, :] = jnp.max(rows.T, axis=0, keepdims=True)
+        peak_ref[block : block + 1, :] = jnp.max(rows_ref[pl.ds(128 * block, 128), :].T, axis=0, keepdims=True)
     peak_ref[3:8, :] = jnp.zeros((5, 128), jnp.float32)
     for step in range(8):
         store(step).wait()
@@ -84,19 +83,25 @@
 
 def act_kernel(lengths_ref, sums_ref, acts_ref, gain_ref, bias_ref, page_ref):
     columns = moments(sums_ref[...])
-    place = lax.broadcasted_iota(jnp.int32, (128, 128), 0)
-    peaks = [jnp.zeros((8, 128), jnp.float32)] * 12
-    for block in range(4):
-        mean = jnp.broadcast_to(columns[:, block : block + 1], (128, 128))
-        rstd = jnp.broadcast_to(columns[:, 4 + block : 5 + block], (128, 128))
-        valid = place + 128 * (block % 2) < lengths_ref[block // 2]
+    place = lax.broadcasted_iota(jnp.int32, (16, 128), 0)
+    most = [jnp.full((8, 128), -jnp.inf, jnp.float32)] * 12
+    least = [jnp.full((8, 128), jnp.inf, jnp.float32)] * 12
+    for group in range(32):
+        block, row = group // 8, 16 * (group % 8)
+        mean = jnp.broadcast_to(columns[row : row + 16, block : block + 1], (16, 128))
+        rstd = jnp.broadcast_to(columns[row : row + 16, 4 + block : 5 + block], (16, 128))
+        valid = place + 16 * (group % 16) < lengths_ref[group // 16]
         for tile in range(12):
-            x = acts_ref[pl.ds(128 * block, 128), pl.ds(128 * tile, 128)].astype(jnp.float32)
-            normed = (x - mean) * rstd * gain_ref[tile : tile + 1, :] + bias_ref[tile : tile + 1, :]
-            peak = jnp.where(valid, jnp.abs(normed), 0.0)
-            peaks[tile] = jnp.maximum(peaks[tile], jnp.max(peak.reshape(16, 8, 128), axis=0))
+            x = (acts_ref[pl.ds(16 * group, 16), pl.ds(128 * tile, 128)].astype(jnp.float32) - mean) * rstd
+            high = jnp.where(valid, x, -jnp.inf)
+            low = jnp.where(valid, x, jnp.inf)
+            most[tile] = jnp.maximum(most[tile], jnp.maximum(high[0:8], high[8:16]))
+            least[tile] = jnp.minimum(least[tile], jnp.minimum(low[0:8], low[8:16]))
     for tile in range(12):
-        page_ref[tile : tile + 1, :] = jnp.max(peaks[tile], axis=0, keepdims=True)
+        gain, bias = gain_ref[tile : tile + 1, :], bias_ref[tile : tile + 1, :]
+        high = jnp.max(most[tile], axis=0, keepdims=True) * gain + bias
+        low = jnp.min(least[tile], axis=0, keepdims=True) * gain + bias
+        page_ref[tile : tile + 1, :] = jnp.maximum(jnp.abs(high), jnp.abs(low))
     page_ref[12:15, :] = sums_ref[8:11, :]
     page_ref[15:16, :] = jnp.zeros((1, 128), jnp.float32)
 
@@ -175,7 +180,7 @@
             scratch_shapes=[
                 pltpu.VMEM((192, 3072), jnp.bfloat16),
                 pltpu.VMEM((64, 72, 128), jnp.bfloat16),
-                pltpu.VMEM((384, 128), jnp.bfloat16),
+                pltpu.VMEM((384, 128), jnp.float32),
                 pltpu.SemaphoreType.DMA((8,)),
                 pltpu.SemaphoreType.DMA((8,)),
             ],

time: 88.8 us -> 88.5 us (level)
  no operation moved by 1% of the time
where the time goes in v9:
time: 88.5 us; the launch traced here: 87 us
  blocking collectives  32.8 us (37%)
  starting transfers between devices  30.9 us (35%)
  waiting for transfers between devices  13.8 us (16%)
  Pallas kernels  8.44 us (10%)
    all_to_all x1, blocking collectives, body(): lax.all_to_all(copies, 'dp', 0, 0, axis_index_groups=kinds, tiled=True)  17.6 us
    all_to_all x1, starting transfers between devices, body(): pages = lax.all_to_all(packed, 'dp', 0, 0, tiled=True)  15.6 us
    ppermute x4, starting transfers between devices, swap(): return lax.ppermute(x, axis, [(i, i ^ bit) for i in range(size)])  15.3 us
    all_to_all x1, blocking collectives, body(): blocks = lax.all_to_all(page, 'mp', 0, 0, tiled=True)  15.2 us
    ppermute x4, waiting for transfers between devices, swap(): return lax.ppermute(x, axis, [(i, i ^ bit) for i in range(size)])  10.2 us
    all_to_all x1, waiting for transfers between devices, body(): pages = lax.all_to_all(packed, 'dp', 0, 0, tiled=True)  3.58 us
    pallas_call x1, Pallas kernels, body(): pl.pallas_call(pack_kernel, out_shape=(jax.ShapeDtypeStruct((64, 72, 128)...  3.18 us
    pallas_call x1, Pallas kernels, body(): pl.pallas_call(serve_kernel, out_shape=(jax.ShapeDtypeStruct((48, D), jnp...  2.36 us
  transfers between devices with their start and end apart: 5, of which 5 were waited for; matrix products, arithmetic and copies ran while one was open for 0% of the time, Pallas kernels for 2%

profile of v9, /device:TPU:1, one launch (start us, length us, event | category | flops | bytes accessed | tf_op | source)
XLA Modules:
  0.0 87.0 jit_solution(7732816880030772418)
XLA Ops:
  0.6 3.2 %weight_exchange.1 = (bf16[64,72,128]{2,1,0:T(8,128)(2,1)}, f32[8,128]{1,0:T(8,128)}) custom-call(bf16[192,3072]{1,0:T(8,128)(2,1)} %w_hbm.1), custom_call_target="tpu_custom_call" | custom-call | tf_op jit(solution)/shard_map/weight_exchange/pallas_call | solution.py:172
  3.8 0.0 copy-start
  3.8 0.0 copy-start.3
  3.8 15.6 %all-to-all-start = ((bf16[64,72,128]{2,1,0:T(8,128)(2,1)}), bf16[64,72,128]{2,1,0:T(8,128)(2,1)S(1)}, u32[]{:S(2)}, u32[]{:S(2)}) async-start(bf16[64,72,128]{2,1,0:T(8,128)(2,1)} %get-tuple-element.11), calls=%async_computation | async-start | bytes 2359296 | tf_op jit(solution)/shard_map/weight_exchange/all_to_all | solution.py:189
  19.4 0.0 copy-start.1
  19.4 0.0 copy-start.2
  19.4 0.0 copy-start.4
  19.4 0.0 copy-done
  19.5 0.0 copy-done.3
  19.5 0.5 token_moments.1
  19.9 3.1 %collective-permute-start = (f32[16,128]{1,0:T(8,128)S(1)}, f32[16,128]{1,0:T(8,128)S(1)}, u32[]{:S(2)}, u32[]{:S(2)}) collective-permute-start(f32[16,128]{1,0:T(8,128)S(1)} %token_moments.1), channel_id=1, source_target_pairs={{0,1},{1,0},{2,3},{3,2},{4,5},{5,4},{6,7},{7,6},{8,9},{9,8},{10,11... | collective-permute-start | bytes 24584 | tf_op jit(solution)/shard_map/token_moments/ppermute | solution.py:165
  23.1 1.6 %collective-permute-done = f32[16,128]{1,0:T(8,128)S(1)} collective-permute-done((f32[16,128]{1,0:T(8,128)S(1)}, f32[16,128]{1,0:T(8,128)S(1)}, u32[]{:S(2)}, u32[]{:S(2)}) %collective-permute-start) | collective-permute-done | bytes 8224 | tf_op jit(solution)/shard_map/token_moments/ppermute | solution.py:165
  24.6 0.1 maximum_select_fusion.2
  24.7 4.6 %collective-permute-start.1 = (f32[16,128]{1,0:T(8,128)S(1)}, f32[16,128]{1,0:T(8,128)S(1)}, u32[]{:S(2)}, u32[]{:S(2)}) collective-permute-start(f32[16,128]{1,0:T(8,128)S(1)} %maximum_select_fusion.2), channel_id=1, source_target_pairs={{0,2},{1,3},{2,0},{3,1},{4,6},{5,7},{6,4},{7,5},{8,10},{9,11},{10,... | collective-permute-start | bytes 24584 | tf_op jit(solution)/shard_map/token_moments/ppermute | solution.py:165
  29.4 1.5 %collective-permute-done.1 = f32[16,128]{1,0:T(8,128)S(1)} collective-permute-done((f32[16,128]{1,0:T(8,128)S(1)}, f32[16,128]{1,0:T(8,128)S(1)}, u32[]{:S(2)}, u32[]{:S(2)}) %collective-permute-start.1) | collective-permute-done | bytes 8224 | tf_op jit(solution)/shard_map/token_moments/ppermute | solution.py:165
  30.9 0.1 maximum_select_fusion.1
  31.0 4.7 %collective-permute-start.2 = (f32[16,128]{1,0:T(8,128)S(1)}, f32[16,128]{1,0:T(8,128)S(1)}, u32[]{:S(2)}, u32[]{:S(2)}) collective-permute-start(f32[16,128]{1,0:T(8,128)S(1)} %maximum_select_fusion.1), channel_id=1, source_target_pairs={{0,4},{1,5},{2,6},{3,7},{4,0},{5,1},{6,2},{7,3},{8,12},{9,13},{10,... | collective-permute-start | bytes 24584 | tf_op jit(solution)/shard_map/token_moments/ppermute | solution.py:165
  35.7 6.3 %collective-permute-done.2 = f32[16,128]{1,0:T(8,128)S(1)} collective-permute-done((f32[16,128]{1,0:T(8,128)S(1)}, f32[16,128]{1,0:T(8,128)S(1)}, u32[]{:S(2)}, u32[]{:S(2)}) %collective-permute-start.2) | collective-permute-done | bytes 8224 | tf_op jit(solution)/shard_map/token_moments/ppermute | solution.py:165
  42.0 0.1 maximum_select_fusion.sums_ref
  42.1 0.0 copy-done.1
  42.1 0.0 copy-done.2
  42.1 0.0 copy-done.4
  42.1 1.5 %channel_maxima.1 = f32[16,128]{1,0:T(8,128)S(1)} custom-call(s32[2]{0:T(128)S(1)} %copy-done.4, f32[16,128]{1,0:T(8,128)S(1)} %maximum_select_fusion.sums_ref, bf16[512,1536]{1,0:T(8,128)(2,1)S(1)} %copy-done, f32[12,128]{1,0:T(8,128)S(1)} %bitcast.4, f32[12,128]{1,0:T(8,128)S(1)} %bitcast.6), custom_call_target="tpu_custom_call" | custom-call | tf_op jit(solution)/shard_map/channel_maxima/pallas_call | solution.py:203
  43.6 2.8 %collective-permute-start.3 = (f32[16,128]{1,0:T(8,128)S(1)}, f32[16,128]{1,0:T(8,128)S(1)}, u32[]{:S(2)}, u32[]{:S(2)}) collective-permute-start(f32[16,128]{1,0:T(8,128)S(1)} %channel_maxima.1), channel_id=1, source_target_pairs={{0,8},{8,0},{16,24},{24,16},{32,40},{40,32},{48,56},{56,48},{64,72... | collective-permute-start | bytes 24584 | tf_op jit(solution)/shard_map/channel_maxima/ppermute | solution.py:165
  46.4 0.8 collective-permute-done.3
  47.3 3.6 %all-to-all-done.pages_ref = bf16[64,72,128]{2,1,0:T(8,128)(2,1)S(1)} async-done(((bf16[64,72,128]{2,1,0:T(8,128)(2,1)}), bf16[64,72,128]{2,1,0:T(8,128)(2,1)S(1)}, u32[]{:S(2)}, u32[]{:S(2)}) %all-to-all-start) | async-done | bytes 1179680 | tf_op jit(solution)/shard_map/weight_exchange/all_to_all | solution.py:189
  50.9 17.6 %all_to_all.15.maxima_ref = f32[32,16,128]{2,1,0:T(8,128)S(1)} all-to-all(f32[32,16,128]{2,1,0:T(8,128)S(1)} %broadcast_in_dim.2), channel_id=1, replica_groups={{0,16,32,48,64,80,96,112,128,144,160,176,192,208,224,240,256,272,288,30..., dimensions={0} | all-to-all | bytes 524288 | tf_op jit(solution)/shard_map/channel_maxima/all_to_all | solution.py:214
  68.5 0.9 %token_peaks.1 = f32[8,16,128]{2,1,0:T(8,128)S(1)} custom-call(f32[32,16,128]{2,1,0:T(8,128)S(1)} %all_to_all.15.maxima_ref, f32[16,128]{1,0:T(8,128)S(1)} %maximum_select_fusion.sums_ref, bf16[512,1536]{1,0:T(8,128)(2,1)S(1)} %copy-done, f32[12,128]{1,0:T(8,128)S(1)} %bitcast.5, f32[12,128]{1,0:T(8,128)S(1)} %bitcast.7), custom_call_target="tpu_custom_call" | custom-call | tf_op jit(solution)/shard_map/token_peaks/pallas_call | solution.py:216
  69.5 15.2 %all_to_all.16.blocks_ref = f32[8,16,128]{2,1,0:T(8,128)S(1)} all-to-all(f32[8,16,128]{2,1,0:T(8,128)S(1)} %token_peaks.1), channel_id=1, replica_groups=mesh['dp'=64,'mp'=8] {'mp'}, dimensions={0} | all-to-all | bytes 131072 | tf_op jit(solution)/shard_map/token_peaks/all_to_all | solution.py:223
  84.6 2.4 %smoothed_weight.1 = (bf16[48,12288]{1,0:T(8,128)(2,1)}, f32[12,128]{1,0:T(8,128)}, f32[4,128]{1,0:T(4,128)}) custom-call(s32[2]{0:T(128)S(1)} %copy-done.4, f32[8,16,128]{2,1,0:T(8,128)S(1)} %all_to_all.16.blocks_ref, bf16[64,72,128]{2,1,0:T(8,128)(2,1)S(1)} %all-to-all-done.pages_ref), custom_call_target="tpu_custom_call" | custom-call | tf_op jit(solution)/shard_map/smoothed_weight/pallas_call | solution.py:225
  (3 shorter events, 0.0 us)
Async XLA Ops:
  3.8 15.6 %copy-start = (bf16[512,1536]{1,0:T(8,128)(2,1)S(1)}, bf16[512,1536]{1,0:T(8,128)(2,1)}, u32[]{:S(2)}) copy-start(bf16[512,1536]{1,0:T(8,128)(2,1)} %acts_ref.5) | copy-start | bytes 4718596
  3.8 15.6 %copy-start.3 = (f32[8,128]{1,0:T(8,128)S(1)}, f32[8,128]{1,0:T(8,128)}, u32[]{:S(2)}) copy-start(f32[8,128]{1,0:T(8,128)} %get-tuple-element.10.peak_ref) | copy-start | bytes 12292
  3.8 47.0 %all-to-all-start = ((bf16[64,72,128]{2,1,0:T(8,128)(2,1)}), bf16[64,72,128]{2,1,0:T(8,128)(2,1)S(1)}, u32[]{:S(2)}, u32[]{:S(2)}) async-start(bf16[64,72,128]{2,1,0:T(8,128)(2,1)} %get-tuple-element.11), calls=%async_computation | async-start | bytes 2359296 | tf_op jit(solution)/shard_map/weight_exchange/all_to_all | solution.py:189
  19.4 22.7 %copy-start.1 = (f32[1536]{0:T(1024)S(1)}, f32[1536]{0:T(1024)}, u32[]{:S(2)}) copy-start(f32[1536]{0:T(1024)} %param.7) | copy-start | bytes 18436
  19.4 22.7 %copy-start.2 = (f32[1536]{0:T(1024)S(1)}, f32[1536]{0:T(1024)}, u32[]{:S(2)}) copy-start(f32[1536]{0:T(1024)} %param.8) | copy-start | bytes 18436
  19.4 22.7 %copy-start.4 = (s32[2]{0:T(128)S(1)}, s32[2]{0:T(128)}, u32[]{:S(2)}) copy-start(s32[2]{0:T(128)} %lengths_ref.3) | copy-start | bytes 28
  19.9 4.7 %collective-permute-start = (f32[16,128]{1,0:T(8,128)S(1)}, f32[16,128]{1,0:T(8,128)S(1)}, u32[]{:S(2)}, u32[]{:S(2)}) collective-permute-start(f32[16,128]{1,0:T(8,128)S(1)} %token_moments.1), channel_id=1, source_target_pairs={{0,1},{1,0},{2,3},{3,2},{4,5},{5,4},{6,7},{7,6},{8,9},{9,8},{10,11... | collective-permute-start | bytes 24584 | tf_op jit(solution)/shard_map/token_moments/ppermute | solution.py:165
  24.7 6.2 %collective-permute-start.1 = (f32[16,128]{1,0:T(8,128)S(1)}, f32[16,128]{1,0:T(8,128)S(1)}, u32[]{:S(2)}, u32[]{:S(2)}) collective-permute-start(f32[16,128]{1,0:T(8,128)S(1)} %maximum_select_fusion.2), channel_id=1, source_target_pairs={{0,2},{1,3},{2,0},{3,1},{4,6},{5,7},{6,4},{7,5},{8,10},{9,11},{10,... | collective-permute-start | bytes 24584 | tf_op jit(solution)/shard_map/token_moments/ppermute | solution.py:165
  31.0 11.1 %collective-permute-start.2 = (f32[16,128]{1,0:T(8,128)S(1)}, f32[16,128]{1,0:T(8,128)S(1)}, u32[]{:S(2)}, u32[]{:S(2)}) collective-permute-start(f32[16,128]{1,0:T(8,128)S(1)} %maximum_select_fusion.1), channel_id=1, source_target_pairs={{0,4},{1,5},{2,6},{3,7},{4,0},{5,1},{6,2},{7,3},{8,12},{9,13},{10,... | collective-permute-start | bytes 24584 | tf_op jit(solution)/shard_map/token_moments/ppermute | solution.py:165
  43.6 3.6 %collective-permute-start.3 = (f32[16,128]{1,0:T(8,128)S(1)}, f32[16,128]{1,0:T(8,128)S(1)}, u32[]{:S(2)}, u32[]{:S(2)}) collective-permute-start(f32[16,128]{1,0:T(8,128)S(1)} %channel_maxima.1), channel_id=1, source_target_pairs={{0,8},{8,0},{16,24},{24,16},{32,40},{40,32},{48,56},{56,48},{64,72... | collective-permute-start | bytes 24584 | tf_op jit(solution)/shard_map/channel_maxima/ppermute | solution.py:165

commit v10 on v9

--- a/solution.py
+++ b/solution.py
@@ -17,7 +17,7 @@
     return pltpu.CompilerParams(vmem_limit_bytes=mebibytes * 1024 * 1024)
 
 
-def pack_kernel(w_hbm, page_hbm, peak_ref, w_ref, page_ref, rows_ref, in_sems, out_sems):
+def pack_kernel(w_hbm, page_hbm, peak_hbm, w_ref, page_ref, peak_ref, in_sems, out_sems, peak_sem):
     parity = lax.axis_index("dp") % 2
     low = lax.broadcasted_iota(jnp.int32, (24, 128), 1) < 64
     first = low == (parity == 0)
@@ -34,10 +34,11 @@
 
     for step in range(8):
         fetch(step).start()
-    rows_ref[...] = jnp.zeros_like(rows_ref)
-
-    def pack(step, carry):
+
+    def pack(step, peak):
         fetch(step).wait()
+        w = jnp.abs(w_ref[:, columns(step)])
+        peak = jnp.maximum(peak, jnp.maximum(jnp.maximum(w[:, 0:128], w[:, 128:256]), w[:, 256:384]))
         full = w_ref[pl.ds(pl.multiple_of(64 * parity, 64), 128), columns(step)].T
         half = w_ref[pl.ds(pl.multiple_of(128 * (1 - parity), 64), 64), columns(step)]
         twice = jnp.concatenate([half, half], axis=0).T.astype(jnp.float32)
@@ -47,22 +48,23 @@
             halves = jnp.where(first, upper, lower).astype(jnp.bfloat16)
             page_ref[8 * step + peer] = jnp.concatenate([full[48 * peer : 48 * peer + 48], halves], axis=0)
         store(step).start()
-        return carry
-
-    lax.fori_loop(0, 8, pack, 0)
-    peak = jnp.zeros((192, 128), jnp.bfloat16)
-    for tile in range(24):
-        peak = jnp.maximum(peak, jnp.abs(w_ref[:, pl.ds(128 * tile, 128)]))
-    rows_ref[pl.ds(pl.multiple_of(192 * parity, 64), 192), :] = peak.astype(jnp.float32)
+        return peak
+
+    peak_ref[...] = lax.fori_loop(0, 8, pack, jnp.zeros((192, 128), jnp.bfloat16))
+    peak_copy = pltpu.make_async_copy(peak_ref, peak_hbm, peak_sem)
+    peak_copy.start()
+    for step in range(8):
+        store(step).wait()
+    peak_copy.wait()
+
+
+def stats_kernel(peak_ref, acts_ref, page_ref, rows_ref):
+    rows_ref[...] = jnp.zeros_like(rows_ref)
+    own = pl.ds(pl.multiple_of(192 * (lax.axis_index("dp") % 2), 64), 192)
+    rows_ref[own, :] = peak_ref[...].astype(jnp.float32)
     for block in range(3):
-        peak_ref[block : block + 1, :] = jnp.max(rows_ref[pl.ds(128 * block, 128), :].T, axis=0, keepdims=True)
-    peak_ref[3:8, :] = jnp.zeros((5, 128), jnp.float32)
-    for step in range(8):
-        store(step).wait()
-
-
-def stats_kernel(peak_ref, acts_ref, page_ref):
-    page_ref[8:16, :] = peak_ref[...]
+        page_ref[8 + block : 9 + block, :] = jnp.max(rows_ref[pl.ds(128 * block, 128), :].T, axis=0, keepdims=True)
+    page_ref[11:16, :] = jnp.zeros((5, 128), jnp.float32)
     for block in range(4):
         total = jnp.zeros((128, 128), jnp.float32)
         square = jnp.zeros((128, 128), jnp.float32)
@@ -173,16 +175,17 @@
             pack_kernel,
             out_shape=(
                 jax.ShapeDtypeStruct((64, 72, 128), jnp.bfloat16),
-                jax.ShapeDtypeStruct((8, 128), jnp.float32),
+                jax.ShapeDtypeStruct((192, 128), jnp.bfloat16),
             ),
             in_specs=[ANY_SPEC],
-            out_specs=(ANY_SPEC, VMEM_SPEC),
+            out_specs=(ANY_SPEC, ANY_SPEC),
             scratch_shapes=[
                 pltpu.VMEM((192, 3072), jnp.bfloat16),
                 pltpu.VMEM((64, 72, 128), jnp.bfloat16),
-                pltpu.VMEM((384, 128), jnp.float32),
+                pltpu.VMEM((192, 128), jnp.bfloat16),
                 pltpu.SemaphoreType.DMA((8,)),
                 pltpu.SemaphoreType.DMA((8,)),
+                pltpu.SemaphoreType.DMA,
             ],
             compiler_params=params(60),
         )(w_fc1)
@@ -193,6 +196,7 @@
             out_shape=jax.ShapeDtypeStruct((16, 128), jnp.float32),
             in_specs=[VMEM_SPEC, VMEM_SPEC],
             out_specs=VMEM_SPEC,
+            scratch_shapes=[pltpu.VMEM((384, 128), jnp.float32)],
             compiler_params=params(),
         )(w_peak, acts)
         added = lax.broadcasted_iota(jnp.int32, (16, 128), 0) < 8

time: 88.5 us -> 88.2 us (level)
  no operation moved by 1% of the time
where the time goes in v10:
time: 88.2 us; the launch traced here: 86.7 us
  blocking collectives  32.8 us (37%)
  starting transfers between devices  30.9 us (35%)
  waiting for transfers between devices  13.8 us (16%)
  Pallas kernels  8.17 us (9%)
    all_to_all x1, blocking collectives, body(): lax.all_to_all(copies, 'dp', 0, 0, axis_index_groups=kinds, tiled=True)  17.6 us
    all_to_all x1, starting transfers between devices, body(): pages = lax.all_to_all(packed, 'dp', 0, 0, tiled=True)  15.6 us
    ppermute x4, starting transfers between devices, swap(): return lax.ppermute(x, axis, [(i, i ^ bit) for i in range(size)])  15.3 us
    all_to_all x1, blocking collectives, body(): blocks = lax.all_to_all(page, 'mp', 0, 0, tiled=True)  15.2 us
    ppermute x4, waiting for transfers between devices, swap(): return lax.ppermute(x, axis, [(i, i ^ bit) for i in range(size)])  10.2 us
    all_to_all x1, waiting for transfers between devices, body(): pages = lax.all_to_all(packed, 'dp', 0, 0, tiled=True)  3.58 us
    pallas_call x1, Pallas kernels, body(): pl.pallas_call(pack_kernel, out_shape=(jax.ShapeDtypeStruct((64, 72, 128)...  2.89 us
    pallas_call x1, Pallas kernels, body(): pl.pallas_call(serve_kernel, out_shape=(jax.ShapeDtypeStruct((48, D), jnp...  2.36 us
  transfers between devices with their start and end apart: 5, of which 5 were waited for; matrix products, arithmetic and copies ran while one was open for 0% of the time, Pallas kernels for 2%

profile of v10, /device:TPU:1, one launch (start us, length us, event | category | flops | bytes accessed | tf_op | source)
XLA Modules:
  0.0 86.7 jit_solution(4100231491003417840)
XLA Ops:
  0.6 2.9 %weight_exchange.1 = (bf16[64,72,128]{2,1,0:T(8,128)(2,1)}, bf16[192,128]{1,0:T(8,128)(2,1)}) custom-call(bf16[192,3072]{1,0:T(8,128)(2,1)} %w_hbm.1), custom_call_target="tpu_custom_call" | custom-call | tf_op jit(solution)/shard_map/weight_exchange/pallas_call | solution.py:174
  3.5 0.0 copy-start
  3.5 0.0 copy-start.1
  3.5 15.6 %all-to-all-start = ((bf16[64,72,128]{2,1,0:T(8,128)(2,1)}), bf16[64,72,128]{2,1,0:T(8,128)(2,1)S(1)}, u32[]{:S(2)}, u32[]{:S(2)}) async-start(bf16[64,72,128]{2,1,0:T(8,128)(2,1)} %get-tuple-element.11), calls=%async_computation | async-start | bytes 2359296 | tf_op jit(solution)/shard_map/weight_exchange/all_to_all | solution.py:192
  19.1 0.0 copy-start.2
  19.1 0.0 copy-start.3
  19.1 0.0 copy-start.4
  19.1 0.0 copy-done
  19.2 0.0 copy-done.1
  19.2 0.5 token_moments.1
  19.7 3.1 %collective-permute-start = (f32[16,128]{1,0:T(8,128)S(1)}, f32[16,128]{1,0:T(8,128)S(1)}, u32[]{:S(2)}, u32[]{:S(2)}) collective-permute-start(f32[16,128]{1,0:T(8,128)S(1)} %token_moments.1), channel_id=1, source_target_pairs={{0,1},{1,0},{2,3},{3,2},{4,5},{5,4},{6,7},{7,6},{8,9},{9,8},{10,11... | collective-permute-start | bytes 24584 | tf_op jit(solution)/shard_map/token_moments/ppermute | solution.py:167
  22.8 1.6 %collective-permute-done = f32[16,128]{1,0:T(8,128)S(1)} collective-permute-done((f32[16,128]{1,0:T(8,128)S(1)}, f32[16,128]{1,0:T(8,128)S(1)}, u32[]{:S(2)}, u32[]{:S(2)}) %collective-permute-start) | collective-permute-done | bytes 8224 | tf_op jit(solution)/shard_map/token_moments/ppermute | solution.py:167
  24.4 0.1 maximum_select_fusion.2
  24.4 4.6 %collective-permute-start.1 = (f32[16,128]{1,0:T(8,128)S(1)}, f32[16,128]{1,0:T(8,128)S(1)}, u32[]{:S(2)}, u32[]{:S(2)}) collective-permute-start(f32[16,128]{1,0:T(8,128)S(1)} %maximum_select_fusion.2), channel_id=1, source_target_pairs={{0,2},{1,3},{2,0},{3,1},{4,6},{5,7},{6,4},{7,5},{8,10},{9,11},{10,... | collective-permute-start | bytes 24584 | tf_op jit(solution)/shard_map/token_moments/ppermute | solution.py:167
  29.1 1.5 %collective-permute-done.1 = f32[16,128]{1,0:T(8,128)S(1)} collective-permute-done((f32[16,128]{1,0:T(8,128)S(1)}, f32[16,128]{1,0:T(8,128)S(1)}, u32[]{:S(2)}, u32[]{:S(2)}) %collective-permute-start.1) | collective-permute-done | bytes 8224 | tf_op jit(solution)/shard_map/token_moments/ppermute | solution.py:167
  30.6 0.1 maximum_select_fusion.1
  30.7 4.7 %collective-permute-start.2 = (f32[16,128]{1,0:T(8,128)S(1)}, f32[16,128]{1,0:T(8,128)S(1)}, u32[]{:S(2)}, u32[]{:S(2)}) collective-permute-start(f32[16,128]{1,0:T(8,128)S(1)} %maximum_select_fusion.1), channel_id=1, source_target_pairs={{0,4},{1,5},{2,6},{3,7},{4,0},{5,1},{6,2},{7,3},{8,12},{9,13},{10,... | collective-permute-start | bytes 24584 | tf_op jit(solution)/shard_map/token_moments/ppermute | solution.py:167
  35.4 6.3 %collective-permute-done.2 = f32[16,128]{1,0:T(8,128)S(1)} collective-permute-done((f32[16,128]{1,0:T(8,128)S(1)}, f32[16,128]{1,0:T(8,128)S(1)}, u32[]{:S(2)}, u32[]{:S(2)}) %collective-permute-start.2) | collective-permute-done | bytes 8224 | tf_op jit(solution)/shard_map/token_moments/ppermute | solution.py:167
  41.7 0.1 maximum_select_fusion.sums_ref
  41.8 0.0 copy-done.2
  41.8 0.0 copy-done.3
  41.8 0.0 copy-done.4
  41.8 1.5 %channel_maxima.1 = f32[16,128]{1,0:T(8,128)S(1)} custom-call(s32[2]{0:T(128)S(1)} %copy-done.4, f32[16,128]{1,0:T(8,128)S(1)} %maximum_select_fusion.sums_ref, bf16[512,1536]{1,0:T(8,128)(2,1)S(1)} %copy-done, f32[12,128]{1,0:T(8,128)S(1)} %bitcast.4, f32[12,128]{1,0:T(8,128)S(1)} %bitcast.6), custom_call_target="tpu_custom_call" | custom-call | tf_op jit(solution)/shard_map/channel_maxima/pallas_call | solution.py:207
  43.3 2.8 %collective-permute-start.3 = (f32[16,128]{1,0:T(8,128)S(1)}, f32[16,128]{1,0:T(8,128)S(1)}, u32[]{:S(2)}, u32[]{:S(2)}) collective-permute-start(f32[16,128]{1,0:T(8,128)S(1)} %channel_maxima.1), channel_id=1, source_target_pairs={{0,8},{8,0},{16,24},{24,16},{32,40},{40,32},{48,56},{56,48},{64,72... | collective-permute-start | bytes 24584 | tf_op jit(solution)/shard_map/channel_maxima/ppermute | solution.py:167
  46.1 0.8 collective-permute-done.3
  47.0 3.6 %all-to-all-done.pages_ref = bf16[64,72,128]{2,1,0:T(8,128)(2,1)S(1)} async-done(((bf16[64,72,128]{2,1,0:T(8,128)(2,1)}), bf16[64,72,128]{2,1,0:T(8,128)(2,1)S(1)}, u32[]{:S(2)}, u32[]{:S(2)}) %all-to-all-start) | async-done | bytes 1179680 | tf_op jit(solution)/shard_map/weight_exchange/all_to_all | solution.py:192
  50.6 17.6 %all_to_all.15.maxima_ref = f32[32,16,128]{2,1,0:T(8,128)S(1)} all-to-all(f32[32,16,128]{2,1,0:T(8,128)S(1)} %broadcast_in_dim.2), channel_id=1, replica_groups={{0,16,32,48,64,80,96,112,128,144,160,176,192,208,224,240,256,272,288,30..., dimensions={0} | all-to-all | bytes 524288 | tf_op jit(solution)/shard_map/channel_maxima/all_to_all | solution.py:218
  68.2 0.9 %token_peaks.1 = f32[8,16,128]{2,1,0:T(8,128)S(1)} custom-call(f32[32,16,128]{2,1,0:T(8,128)S(1)} %all_to_all.15.maxima_ref, f32[16,128]{1,0:T(8,128)S(1)} %maximum_select_fusion.sums_ref, bf16[512,1536]{1,0:T(8,128)(2,1)S(1)} %copy-done, f32[12,128]{1,0:T(8,128)S(1)} %bitcast.5, f32[12,128]{1,0:T(8,128)S(1)} %bitcast.7), custom_call_target="tpu_custom_call" | custom-call | tf_op jit(solution)/shard_map/token_peaks/pallas_call | solution.py:220
  69.2 15.2 %all_to_all.16.blocks_ref = f32[8,16,128]{2,1,0:T(8,128)S(1)} all-to-all(f32[8,16,128]{2,1,0:T(8,128)S(1)} %token_peaks.1), channel_id=1, replica_groups=mesh['dp'=64,'mp'=8] {'mp'}, dimensions={0} | all-to-all | bytes 131072 | tf_op jit(solution)/shard_map/token_peaks/all_to_all | solution.py:227
  84.3 2.4 %smoothed_weight.1 = (bf16[48,12288]{1,0:T(8,128)(2,1)}, f32[12,128]{1,0:T(8,128)}, f32[4,128]{1,0:T(4,128)}) custom-call(s32[2]{0:T(128)S(1)} %copy-done.4, f32[8,16,128]{2,1,0:T(8,128)S(1)} %all_to_all.16.blocks_ref, bf16[64,72,128]{2,1,0:T(8,128)(2,1)S(1)} %all-to-all-done.pages_ref), custom_call_target="tpu_custom_call" | custom-call | tf_op jit(solution)/shard_map/smoothed_weight/pallas_call | solution.py:229
  (3 shorter events, 0.0 us)
Async XLA Ops:
  3.5 15.6 %copy-start = (bf16[512,1536]{1,0:T(8,128)(2,1)S(1)}, bf16[512,1536]{1,0:T(8,128)(2,1)}, u32[]{:S(2)}) copy-start(bf16[512,1536]{1,0:T(8,128)(2,1)} %acts_ref.5) | copy-start | bytes 4718596
  3.5 15.6 %copy-start.1 = (bf16[192,128]{1,0:T(8,128)(2,1)S(1)}, bf16[192,128]{1,0:T(8,128)(2,1)}, u32[]{:S(2)}) copy-start(bf16[192,128]{1,0:T(8,128)(2,1)} %get-tuple-element.10.peak_ref) | copy-start | bytes 147460
  3.5 47.0 %all-to-all-start = ((bf16[64,72,128]{2,1,0:T(8,128)(2,1)}), bf16[64,72,128]{2,1,0:T(8,128)(2,1)S(1)}, u32[]{:S(2)}, u32[]{:S(2)}) async-start(bf16[64,72,128]{2,1,0:T(8,128)(2,1)} %get-tuple-element.11), calls=%async_computation | async-start | bytes 2359296 | tf_op jit(solution)/shard_map/weight_exchange/all_to_all | solution.py:192
  19.1 22.7 %copy-start.2 = (f32[1536]{0:T(1024)S(1)}, f32[1536]{0:T(1024)}, u32[]{:S(2)}) copy-start(f32[1536]{0:T(1024)} %param.7) | copy-start | bytes 18436
  19.1 22.7 %copy-start.3 = (f32[1536]{0:T(1024)S(1)}, f32[1536]{0:T(1024)}, u32[]{:S(2)}) copy-start(f32[1536]{0:T(1024)} %param.8) | copy-start | bytes 18436
  19.1 22.7 %copy-start.4 = (s32[2]{0:T(128)S(1)}, s32[2]{0:T(128)}, u32[]{:S(2)}) copy-start(s32[2]{0:T(128)} %lengths_ref.3) | copy-start | bytes 28
  19.7 4.7 %collective-permute-start = (f32[16,128]{1,0:T(8,128)S(1)}, f32[16,128]{1,0:T(8,128)S(1)}, u32[]{:S(2)}, u32[]{:S(2)}) collective-permute-start(f32[16,128]{1,0:T(8,128)S(1)} %token_moments.1), channel_id=1, source_target_pairs={{0,1},{1,0},{2,3},{3,2},{4,5},{5,4},{6,7},{7,6},{8,9},{9,8},{10,11... | collective-permute-start | bytes 24584 | tf_op jit(solution)/shard_map/token_moments/ppermute | solution.py:167
  24.4 6.2 %collective-permute-start.1 = (f32[16,128]{1,0:T(8,128)S(1)}, f32[16,128]{1,0:T(8,128)S(1)}, u32[]{:S(2)}, u32[]{:S(2)}) collective-permute-start(f32[16,128]{1,0:T(8,128)S(1)} %maximum_select_fusion.2), channel_id=1, source_target_pairs={{0,2},{1,3},{2,0},{3,1},{4,6},{5,7},{6,4},{7,5},{8,10},{9,11},{10,... | collective-permute-start | bytes 24584 | tf_op jit(solution)/shard_map/token_moments/ppermute | solution.py:167
  30.7 11.1 %collective-permute-start.2 = (f32[16,128]{1,0:T(8,128)S(1)}, f32[16,128]{1,0:T(8,128)S(1)}, u32[]{:S(2)}, u32[]{:S(2)}) collective-permute-start(f32[16,128]{1,0:T(8,128)S(1)} %maximum_select_fusion.1), channel_id=1, source_target_pairs={{0,4},{1,5},{2,6},{3,7},{4,0},{5,1},{6,2},{7,3},{8,12},{9,13},{10,... | collective-permute-start | bytes 24584 | tf_op jit(solution)/shard_map/token_moments/ppermute | solution.py:167
  43.3 3.6 %collective-permute-start.3 = (f32[16,128]{1,0:T(8,128)S(1)}, f32[16,128]{1,0:T(8,128)S(1)}, u32[]{:S(2)}, u32[]{:S(2)}) collective-permute-start(f32[16,128]{1,0:T(8,128)S(1)} %channel_maxima.1), channel_id=1, source_target_pairs={{0,8},{8,0},{16,24},{24,16},{32,40},{40,32},{48,56},{56,48},{64,72... | collective-permute-start | bytes 24584 | tf_op jit(solution)/shard_map/channel_maxima/ppermute | solution.py:167

commit v11 on v10

--- a/solution.py
+++ b/solution.py
@@ -133,22 +133,24 @@
         page_ref[peer] = page
 
 
-def serve_kernel(lengths_ref, blocks_ref, pages_ref, served_hbm, scale_ref, tok_ref, served_ref, sems):
-    low = lax.broadcasted_iota(jnp.int32, (24, 128), 1) < 64
+def serve_kernel(lengths_ref, blocks_ref, own_ref, other_ref, served_hbm, scale_ref, tok_ref, served_ref, sems):
+    core = lax.axis_index("dp") % 2
+    first = (lax.broadcasted_iota(jnp.int32, (24, 128), 1) < 64) == (core == 0)
 
     def store(step):
         columns = pl.ds(1536 * step, 1536)
         return pltpu.make_async_copy(served_ref.at[:, columns], served_hbm.at[:, columns], sems.at[step])
 
     for step in range(8):
-        for pair in range(4 * step, 4 * step + 4):
-            even = pages_ref[2 * pair].astype(jnp.float32)
-            odd = pages_ref[2 * pair + 1].astype(jnp.float32)
-            upper = jnp.where(low, even[48:72], odd[48:72])
-            lower = pltpu.roll(jnp.where(low, odd[48:72], even[48:72]), 64, 1)
-            middle = jnp.concatenate([upper, lower], axis=0)
-            for part, tile in enumerate((even[0:48], middle, odd[0:48])):
-                row = 3 * pair + part
+        for chip in range(4 * step, 4 * step + 4):
+            own = own_ref[2 * chip + core].astype(jnp.float32)
+            other = other_ref[chip].astype(jnp.float32)
+            upper = jnp.where(first, own[48:72], other[48:72])
+            lower = pltpu.roll(jnp.where(first, other[48:72], own[48:72]), 64, 1)
+            even = jnp.where(core == 0, own[0:48], other[0:48])
+            odd = jnp.where(core == 0, other[0:48], own[0:48])
+            for part, tile in enumerate((even, jnp.concatenate([upper, lower], axis=0), odd)):
+                row = 3 * chip + part
                 scale = blocks_ref[row // 12, row % 12 : row % 12 + 1, :]
                 served_ref[:, pl.ds(128 * row, 128)] = (tile * scale).astype(jnp.bfloat16)
         store(step).start()
@@ -189,7 +191,8 @@
             ],
             compiler_params=params(60),
         )(w_fc1)
-        pages = lax.all_to_all(packed, "dp", 0, 0, tiled=True)
+        kinds = [[2 * chip + core for chip in range(32)] for core in range(2)]
+        pages = lax.all_to_all(packed, "dp", 0, 0, axis_index_groups=kinds, tiled=True)
     with jax.named_scope("token_moments"):
         sums = pl.pallas_call(
             stats_kernel,
@@ -214,8 +217,11 @@
         maxima = jnp.maximum(maxima, swap(maxima, "dp", 1))
         maxima, pages = lax.optimization_barrier((maxima, pages))
         copies = jnp.broadcast_to(maxima[None], (32, 16, 128))
-        kinds = [[2 * chip + core for chip in range(32)] for core in range(2)]
         maxima = lax.all_to_all(copies, "dp", 0, 0, axis_index_groups=kinds, tiled=True)
+    with jax.named_scope("core_halves"):
+        theirs = lax.dynamic_index_in_dim(pages.reshape(32, 2, 72, 128), 1 - lax.axis_index("dp") % 2, 1, keepdims=False)
+        others = swap(theirs, "dp", 1)
+        maxima, others = lax.optimization_barrier((maxima, others))
     with jax.named_scope("token_peaks"):
         page = pl.pallas_call(
             peak_kernel,
@@ -233,11 +239,11 @@
                 jax.ShapeDtypeStruct((12, 128), jnp.float32),
                 jax.ShapeDtypeStruct((4, 128), jnp.float32),
             ),
-            in_specs=[SMEM_SPEC, VMEM_SPEC, VMEM_SPEC],
+            in_specs=[SMEM_SPEC, VMEM_SPEC, VMEM_SPEC, VMEM_SPEC],
             out_specs=(ANY_SPEC, VMEM_SPEC, VMEM_SPEC),
             scratch_shapes=[pltpu.VMEM((48, D), jnp.bfloat16), pltpu.SemaphoreType.DMA((8,))],
             compiler_params=params(),
-        )(lengths, blocks, pages)
+        )(lengths, blocks, pages, others)
     return served, scale.reshape(1536), tok.reshape(512)
 
 

time: 88.2 us -> 90 us (1.020)
  starting transfers between devices: 30.9 us -> 35.9 us
  waiting for transfers between devices: 13.8 us -> 9.59 us
  blocking collectives: 32.8 us -> 33.9 us
    ppermute x4 -> x5, starting transfers between devices: 15.3 us -> 21.4 us  [swap(): return lax.ppermute(x, axis, [(i, i ^ bit) for i in range(size)])]
    all_to_all x1, waiting for transfers between devices: 3.58 us -> 0.29 us  [body(): lax.all_to_all(packed, 'dp', 0, 0, axis_index_groups=kinds, tiled=True)]
    all_to_all x1, starting transfers between devices: 15.6 us -> 14.4 us  [body(): lax.all_to_all(packed, 'dp', 0, 0, axis_index_groups=kinds, tiled=True)]
    ppermute x4 -> x5, waiting for transfers between devices: 10.2 us -> 9.3 us  [swap(): return lax.ppermute(x, axis, [(i, i ^ bit) for i in range(size)])]
  transfers between devices with their start and end apart: 5 -> 6, of which waited for: 5 -> 5; matrix products, arithmetic and copies ran while one was open for 0% -> 0% of each run, Pallas kernels for 2% -> 2%
where the time goes in v11:
time: 90 us; the launch traced here: 88.7 us
  starting transfers between devices  35.9 us (40%)
  blocking collectives  33.9 us (38%)
  waiting for transfers between devices  9.59 us (11%)
  Pallas kernels  8.25 us (9%)
    ppermute x5, starting transfers between devices, swap(): return lax.ppermute(x, axis, [(i, i ^ bit) for i in range(size)])  21.4 us
    all_to_all x1, blocking collectives, body(): lax.all_to_all(copies, 'dp', 0, 0, axis_index_groups=kinds, tiled=True)  18.4 us
    all_to_all x1, blocking collectives, body(): blocks = lax.all_to_all(page, 'mp', 0, 0, tiled=True)  15.5 us
    all_to_all x1, starting transfers between devices, body(): lax.all_to_all(packed, 'dp', 0, 0, axis_index_groups=kinds, tiled=True)  14.4 us
    ppermute x5, waiting for transfers between devices, swap(): return lax.ppermute(x, axis, [(i, i ^ bit) for i in range(size)])  9.3 us
    pallas_call x1, Pallas kernels, body(): pl.pallas_call(pack_kernel, out_shape=(jax.ShapeDtypeStruct((64, 72, 128)...  2.9 us
    pallas_call x1, Pallas kernels, body(): pl.pallas_call(serve_kernel, out_shape=(jax.ShapeDtypeStruct((48, D), jnp...  2.42 us
  transfers between devices with their start and end apart: 6, of which 5 were waited for; matrix products, arithmetic and copies ran while one was open for 0% of the time, Pallas kernels for 2%

profile of v11, /device:TPU:1, one launch (start us, length us, event | category | flops | bytes accessed | tf_op | source)
XLA Modules:
  0.0 88.7 jit_solution(13269254610982600280)
XLA Ops:
  0.6 2.9 %weight_exchange.1 = (bf16[64,72,128]{2,1,0:T(8,128)(2,1)}, bf16[192,128]{1,0:T(8,128)(2,1)}) custom-call(bf16[192,3072]{1,0:T(8,128)(2,1)} %w_hbm.1), custom_call_target="tpu_custom_call" | custom-call | tf_op jit(solution)/shard_map/weight_exchange/pallas_call | solution.py:176
  3.5 0.0 copy-start
  3.5 0.0 copy-start.1
  3.6 14.4 %all-to-all-start = ((bf16[64,72,128]{2,1,0:T(8,128)(2,1)}), bf16[64,72,128]{2,1,0:T(8,128)(2,1)S(1)}, u32[]{:S(2)}, u32[]{:S(2)}) async-start(bf16[64,72,128]{2,1,0:T(8,128)(2,1)} %get-tuple-element.13), calls=%async_computation | async-start | bytes 2359296 | tf_op jit(solution)/shard_map/weight_exchange/all_to_all | solution.py:195
  18.0 0.0 copy-start.2
  18.0 0.0 copy-start.3
  18.0 0.0 copy-start.4
  18.0 0.0 copy-done
  18.1 0.0 copy-done.1
  18.1 0.5 token_moments.1
  18.6 3.1 %collective-permute-start = (f32[16,128]{1,0:T(8,128)S(1)}, f32[16,128]{1,0:T(8,128)S(1)}, u32[]{:S(2)}, u32[]{:S(2)}) collective-permute-start(f32[16,128]{1,0:T(8,128)S(1)} %token_moments.1), channel_id=1, source_target_pairs={{0,1},{1,0},{2,3},{3,2},{4,5},{5,4},{6,7},{7,6},{8,9},{9,8},{10,11... | collective-permute-start | bytes 24584 | tf_op jit(solution)/shard_map/token_moments/ppermute | solution.py:169
  21.7 1.3 %collective-permute-done = f32[16,128]{1,0:T(8,128)S(1)} collective-permute-done((f32[16,128]{1,0:T(8,128)S(1)}, f32[16,128]{1,0:T(8,128)S(1)}, u32[]{:S(2)}, u32[]{:S(2)}) %collective-permute-start) | collective-permute-done | bytes 8224 | tf_op jit(solution)/shard_map/token_moments/ppermute | solution.py:169
  23.0 0.1 maximum_select_fusion.2
  23.0 4.6 %collective-permute-start.1 = (f32[16,128]{1,0:T(8,128)S(1)}, f32[16,128]{1,0:T(8,128)S(1)}, u32[]{:S(2)}, u32[]{:S(2)}) collective-permute-start(f32[16,128]{1,0:T(8,128)S(1)} %maximum_select_fusion.2), channel_id=1, source_target_pairs={{0,2},{1,3},{2,0},{3,1},{4,6},{5,7},{6,4},{7,5},{8,10},{9,11},{10,... | collective-permute-start | bytes 24584 | tf_op jit(solution)/shard_map/token_moments/ppermute | solution.py:169
  27.7 1.5 %collective-permute-done.1 = f32[16,128]{1,0:T(8,128)S(1)} collective-permute-done((f32[16,128]{1,0:T(8,128)S(1)}, f32[16,128]{1,0:T(8,128)S(1)}, u32[]{:S(2)}, u32[]{:S(2)}) %collective-permute-start.1) | collective-permute-done | bytes 8224 | tf_op jit(solution)/shard_map/token_moments/ppermute | solution.py:169
  29.2 0.1 maximum_select_fusion.1
  29.3 4.7 %collective-permute-start.2 = (f32[16,128]{1,0:T(8,128)S(1)}, f32[16,128]{1,0:T(8,128)S(1)}, u32[]{:S(2)}, u32[]{:S(2)}) collective-permute-start(f32[16,128]{1,0:T(8,128)S(1)} %maximum_select_fusion.1), channel_id=1, source_target_pairs={{0,4},{1,5},{2,6},{3,7},{4,0},{5,1},{6,2},{7,3},{8,12},{9,13},{10,... | collective-permute-start | bytes 24584 | tf_op jit(solution)/shard_map/token_moments/ppermute | solution.py:169
  34.0 5.7 %collective-permute-done.2 = f32[16,128]{1,0:T(8,128)S(1)} collective-permute-done((f32[16,128]{1,0:T(8,128)S(1)}, f32[16,128]{1,0:T(8,128)S(1)}, u32[]{:S(2)}, u32[]{:S(2)}) %collective-permute-start.2) | collective-permute-done | bytes 8224 | tf_op jit(solution)/shard_map/token_moments/ppermute | solution.py:169
  39.8 0.1 maximum_select_fusion.sums_ref
  39.8 0.0 copy-done.2
  39.8 0.0 copy-done.3
  39.8 0.0 copy-done.4
  39.8 1.5 %channel_maxima.1 = f32[16,128]{1,0:T(8,128)S(1)} custom-call(s32[2]{0:T(128)S(1)} %copy-done.4, f32[16,128]{1,0:T(8,128)S(1)} %maximum_select_fusion.sums_ref, bf16[512,1536]{1,0:T(8,128)(2,1)S(1)} %copy-done, f32[12,128]{1,0:T(8,128)S(1)} %bitcast.10, f32[12,128]{1,0:T(8,128)S(1)} %bitcast.12), custom_call_target="tpu_custom_call" | custom-call | tf_op jit(solution)/shard_map/channel_maxima/pallas_call | solution.py:210
  41.3 3.8 %collective-permute-start.3 = (f32[16,128]{1,0:T(8,128)S(1)}, f32[16,128]{1,0:T(8,128)S(1)}, u32[]{:S(2)}, u32[]{:S(2)}) collective-permute-start(f32[16,128]{1,0:T(8,128)S(1)} %channel_maxima.1), channel_id=1, source_target_pairs={{0,8},{8,0},{16,24},{24,16},{32,40},{40,32},{48,56},{56,48},{64,72... | collective-permute-start | bytes 24584 | tf_op jit(solution)/shard_map/channel_maxima/ppermute | solution.py:169
  45.2 0.8 collective-permute-done.3
  46.0 0.3 all-to-all-done.own_ref
  46.3 5.1 %collective-permute-start.4 = (bf16[32,72,128]{2,1,0:T(8,128)(2,1)S(1)}, bf16[32,72,128]{2,1,0:T(8,128)(2,1)S(1)}, u32[]{:S(2)}, u32[]{:S(2)}) collective-permute-start(bf16[32,72,128]{2,1,0:T(8,128)(2,1)S(1)} %dynamic-slice_bitcast_fusion), channel_id=1, source_target_pairs={{0,8},{8,0},{16,24},{24,16},{32,40},{40,32},{48,56},{56,48},{64,72... | collective-permute-start | bytes 1769480 | tf_op jit(solution)/shard_map/core_halves/ppermute | solution.py:169
  51.4 18.4 %all_to_all.15.maxima_ref = f32[32,16,128]{2,1,0:T(8,128)S(1)} all-to-all(f32[32,16,128]{2,1,0:T(8,128)S(1)} %broadcast_in_dim.2), channel_id=1, replica_groups={{0,16,32,48,64,80,96,112,128,144,160,176,192,208,224,240,256,272,288,30..., dimensions={0} | all-to-all | bytes 524288 | tf_op jit(solution)/shard_map/channel_maxima/all_to_all | solution.py:220
  69.8 0.0 collective-permute-done.4.other_ref
  69.8 0.9 %token_peaks.1 = f32[8,16,128]{2,1,0:T(8,128)S(1)} custom-call(f32[32,16,128]{2,1,0:T(8,128)S(1)} %all_to_all.15.maxima_ref, f32[16,128]{1,0:T(8,128)S(1)} %maximum_select_fusion.sums_ref, bf16[512,1536]{1,0:T(8,128)(2,1)S(1)} %copy-done, f32[12,128]{1,0:T(8,128)S(1)} %bitcast.11, f32[12,128]{1,0:T(8,128)S(1)} %bitcast.13), custom_call_target="tpu_custom_call" | custom-call | tf_op jit(solution)/shard_map/token_peaks/pallas_call | solution.py:226
  70.8 15.5 %all_to_all.16.blocks_ref = f32[8,16,128]{2,1,0:T(8,128)S(1)} all-to-all(f32[8,16,128]{2,1,0:T(8,128)S(1)} %token_peaks.1), channel_id=1, replica_groups=mesh['dp'=64,'mp'=8] {'mp'}, dimensions={0} | all-to-all | bytes 131072 | tf_op jit(solution)/shard_map/token_peaks/all_to_all | solution.py:233
  86.2 2.4 %smoothed_weight.1 = (bf16[48,12288]{1,0:T(8,128)(2,1)}, f32[12,128]{1,0:T(8,128)}, f32[4,128]{1,0:T(4,128)}) custom-call(s32[2]{0:T(128)S(1)} %copy-done.4, f32[8,16,128]{2,1,0:T(8,128)S(1)} %all_to_all.16.blocks_ref, bf16[64,72,128]{2,1,0:T(8,128)(2,1)S(1)} %all-to-all-done.own_ref, bf16[32,72,128]{2,1,0:T(8,128)(2,1)S(1)} %collective-permute-done.4.other_ref), custom_call_target="tpu_custom_call" | custom-call | tf_op jit(solution)/shard_map/smoothed_weight/pallas_call | solution.py:235
  (4 shorter events, 0.1 us)
Async XLA Ops:
  3.5 14.5 %copy-start = (bf16[512,1536]{1,0:T(8,128)(2,1)S(1)}, bf16[512,1536]{1,0:T(8,128)(2,1)}, u32[]{:S(2)}) copy-start(bf16[512,1536]{1,0:T(8,128)(2,1)} %acts_ref.5) | copy-start | bytes 4718596
  3.5 14.5 %copy-start.1 = (bf16[192,128]{1,0:T(8,128)(2,1)S(1)}, bf16[192,128]{1,0:T(8,128)(2,1)}, u32[]{:S(2)}) copy-start(bf16[192,128]{1,0:T(8,128)(2,1)} %get-tuple-element.12.peak_ref) | copy-start | bytes 147460
  3.6 42.7 %all-to-all-start = ((bf16[64,72,128]{2,1,0:T(8,128)(2,1)}), bf16[64,72,128]{2,1,0:T(8,128)(2,1)S(1)}, u32[]{:S(2)}, u32[]{:S(2)}) async-start(bf16[64,72,128]{2,1,0:T(8,128)(2,1)} %get-tuple-element.13), calls=%async_computation | async-start | bytes 2359296 | tf_op jit(solution)/shard_map/weight_exchange/all_to_all | solution.py:195
  18.0 21.8 %copy-start.2 = (f32[1536]{0:T(1024)S(1)}, f32[1536]{0:T(1024)}, u32[]{:S(2)}) copy-start(f32[1536]{0:T(1024)} %param.7) | copy-start | bytes 18436
  18.0 21.8 %copy-start.3 = (f32[1536]{0:T(1024)S(1)}, f32[1536]{0:T(1024)}, u32[]{:S(2)}) copy-start(f32[1536]{0:T(1024)} %param.8) | copy-start | bytes 18436
  18.0 21.8 %copy-start.4 = (s32[2]{0:T(128)S(1)}, s32[2]{0:T(128)}, u32[]{:S(2)}) copy-start(s32[2]{0:T(128)} %lengths_ref.3) | copy-start | bytes 28
  18.6 4.4 %collective-permute-start = (f32[16,128]{1,0:T(8,128)S(1)}, f32[16,128]{1,0:T(8,128)S(1)}, u32[]{:S(2)}, u32[]{:S(2)}) collective-permute-start(f32[16,128]{1,0:T(8,128)S(1)} %token_moments.1), channel_id=1, source_target_pairs={{0,1},{1,0},{2,3},{3,2},{4,5},{5,4},{6,7},{7,6},{8,9},{9,8},{10,11... | collective-permute-start | bytes 24584 | tf_op jit(solution)/shard_map/token_moments/ppermute | solution.py:169
  23.0 6.2 %collective-permute-start.1 = (f32[16,128]{1,0:T(8,128)S(1)}, f32[16,128]{1,0:T(8,128)S(1)}, u32[]{:S(2)}, u32[]{:S(2)}) collective-permute-start(f32[16,128]{1,0:T(8,128)S(1)} %maximum_select_fusion.2), channel_id=1, source_target_pairs={{0,2},{1,3},{2,0},{3,1},{4,6},{5,7},{6,4},{7,5},{8,10},{9,11},{10,... | collective-permute-start | bytes 24584 | tf_op jit(solution)/shard_map/token_moments/ppermute | solution.py:169
  29.3 10.5 %collective-permute-start.2 = (f32[16,128]{1,0:T(8,128)S(1)}, f32[16,128]{1,0:T(8,128)S(1)}, u32[]{:S(2)}, u32[]{:S(2)}) collective-permute-start(f32[16,128]{1,0:T(8,128)S(1)} %maximum_select_fusion.1), channel_id=1, source_target_pairs={{0,4},{1,5},{2,6},{3,7},{4,0},{5,1},{6,2},{7,3},{8,12},{9,13},{10,... | collective-permute-start | bytes 24584 | tf_op jit(solution)/shard_map/token_moments/ppermute | solution.py:169
  41.3 4.7 %collective-permute-start.3 = (f32[16,128]{1,0:T(8,128)S(1)}, f32[16,128]{1,0:T(8,128)S(1)}, u32[]{:S(2)}, u32[]{:S(2)}) collective-permute-start(f32[16,128]{1,0:T(8,128)S(1)} %channel_maxima.1), channel_id=1, source_target_pairs={{0,8},{8,0},{16,24},{24,16},{32,40},{40,32},{48,56},{56,48},{64,72... | collective-permute-start | bytes 24584 | tf_op jit(solution)/shard_map/channel_maxima/ppermute | solution.py:169
  46.3 23.5 %collective-permute-start.4 = (bf16[32,72,128]{2,1,0:T(8,128)(2,1)S(1)}, bf16[32,72,128]{2,1,0:T(8,128)(2,1)S(1)}, u32[]{:S(2)}, u32[]{:S(2)}) collective-permute-start(bf16[32,72,128]{2,1,0:T(8,128)(2,1)S(1)} %dynamic-slice_bitcast_fusion), channel_id=1, source_target_pairs={{0,8},{8,0},{16,24},{24,16},{32,40},{40,32},{48,56},{56,48},{64,72... | collective-permute-start | bytes 1769480 | tf_op jit(solution)/shard_map/core_halves/ppermute | solution.py:169

commit v12 on v10

--- a/solution.py
+++ b/solution.py
@@ -83,22 +83,32 @@
     return jnp.concatenate([mean, rstd], axis=0).T
 
 
-def act_kernel(lengths_ref, sums_ref, acts_ref, gain_ref, bias_ref, page_ref):
+def act_kernel(lengths_ref, sums_ref, acts_ref, gain_ref, bias_ref, page_ref, mean_ref, rstd_ref):
     columns = moments(sums_ref[...])
     place = lax.broadcasted_iota(jnp.int32, (16, 128), 0)
-    most = [jnp.full((8, 128), -jnp.inf, jnp.float32)] * 12
-    least = [jnp.full((8, 128), jnp.inf, jnp.float32)] * 12
-    for group in range(32):
-        block, row = group // 8, 16 * (group % 8)
-        mean = jnp.broadcast_to(columns[row : row + 16, block : block + 1], (16, 128))
-        rstd = jnp.broadcast_to(columns[row : row + 16, 4 + block : 5 + block], (16, 128))
+    for block in range(4):
+        mean_ref[128 * block : 128 * block + 128, :] = jnp.broadcast_to(columns[:, block : block + 1], (128, 128))
+        rstd_ref[128 * block : 128 * block + 128, :] = jnp.broadcast_to(columns[:, 4 + block : 5 + block], (128, 128))
+
+    def extend(group, carry):
+        most, least = carry
+        rows = pl.ds(pl.multiple_of(16 * group, 16), 16)
+        mean, rstd = mean_ref[rows, :], rstd_ref[rows, :]
         valid = place + 16 * (group % 16) < lengths_ref[group // 16]
+        highs, lows = [], []
         for tile in range(12):
-            x = (acts_ref[pl.ds(16 * group, 16), pl.ds(128 * tile, 128)].astype(jnp.float32) - mean) * rstd
+            x = (acts_ref[rows, pl.ds(128 * tile, 128)].astype(jnp.float32) - mean) * rstd
             high = jnp.where(valid, x, -jnp.inf)
             low = jnp.where(valid, x, jnp.inf)
-            most[tile] = jnp.maximum(most[tile], jnp.maximum(high[0:8], high[8:16]))
-            least[tile] = jnp.minimum(least[tile], jnp.minimum(low[0:8], low[8:16]))
+            highs.append(jnp.maximum(most[tile], jnp.maximum(high[0:8], high[8:16])))
+            lows.append(jnp.minimum(least[tile], jnp.minimum(low[0:8], low[8:16])))
+        return tuple(highs), tuple(lows)
+
+    start = (
+        tuple(jnp.full((8, 128), -jnp.inf, jnp.float32) for _ in range(12)),
+        tuple(jnp.full((8, 128), jnp.inf, jnp.float32) for _ in range(12)),
+    )
+    most, least = lax.fori_loop(0, 32, extend, start)
     for tile in range(12):
         gain, bias = gain_ref[tile : tile + 1, :], bias_ref[tile : tile + 1, :]
         high = jnp.max(most[tile], axis=0, keepdims=True) * gain + bias
@@ -108,7 +118,7 @@
     page_ref[15:16, :] = jnp.zeros((1, 128), jnp.float32)
 
 
-def peak_kernel(maxima_ref, sums_ref, acts_ref, gain_ref, bias_ref, page_ref):
+def peak_kernel(maxima_ref, sums_ref, acts_ref, gain_ref, bias_ref, page_ref, mean_ref, rstd_ref):
     columns = moments(sums_ref[...])
     start = 4 * lax.axis_index("mp")
     act = jnp.max(maxima_ref[:, 0:12, :], axis=0)
@@ -120,14 +130,21 @@
     gain = gain_ref[...] * inverse
     bias = bias_ref[...] * inverse
     for block in range(4):
-        mean = jnp.broadcast_to(columns[:, block : block + 1], (128, 128))
-        rstd = jnp.broadcast_to(columns[:, 4 + block : 5 + block], (128, 128))
+        mean_ref[128 * block : 128 * block + 128, :] = jnp.broadcast_to(columns[:, block : block + 1], (128, 128))
+        rstd_ref[128 * block : 128 * block + 128, :] = jnp.broadcast_to(columns[:, 4 + block : 5 + block], (128, 128))
+
+    def find(block, carry):
+        rows = pl.ds(pl.multiple_of(128 * block, 128), 128)
+        mean, rstd = mean_ref[rows, :], rstd_ref[rows, :]
         peak = jnp.zeros((128, 128), jnp.float32)
         for tile in range(12):
-            x = acts_ref[pl.ds(128 * block, 128), pl.ds(128 * tile, 128)].astype(jnp.float32)
+            x = acts_ref[rows, pl.ds(128 * tile, 128)].astype(jnp.float32)
             smoothed = (x - mean) * rstd * gain[tile : tile + 1] + bias[tile : tile + 1]
             peak = jnp.maximum(peak, jnp.abs(smoothed))
-        page_ref[0, 12 + block : 13 + block, :] = jnp.max(peak.T, axis=0, keepdims=True)
+        page_ref[0, pl.ds(12 + block, 1), :] = jnp.max(peak.T, axis=0, keepdims=True)
+        return carry
+
+    lax.fori_loop(0, 4, find, 0)
     page = page_ref[0]
     for peer in range(1, page_ref.shape[0]):
         page_ref[peer] = page
@@ -137,21 +154,24 @@
     low = lax.broadcasted_iota(jnp.int32, (24, 128), 1) < 64
 
     def store(step):
-        columns = pl.ds(1536 * step, 1536)
+        columns = pl.ds(pl.multiple_of(1536 * step, 128), 1536)
         return pltpu.make_async_copy(served_ref.at[:, columns], served_hbm.at[:, columns], sems.at[step])
 
-    for step in range(8):
-        for pair in range(4 * step, 4 * step + 4):
-            even = pages_ref[2 * pair].astype(jnp.float32)
-            odd = pages_ref[2 * pair + 1].astype(jnp.float32)
+    def serve(step, carry):
+        for pair in range(4):
+            even = pages_ref[8 * step + 2 * pair].astype(jnp.float32)
+            odd = pages_ref[8 * step + 2 * pair + 1].astype(jnp.float32)
             upper = jnp.where(low, even[48:72], odd[48:72])
             lower = pltpu.roll(jnp.where(low, odd[48:72], even[48:72]), 64, 1)
             middle = jnp.concatenate([upper, lower], axis=0)
             for part, tile in enumerate((even[0:48], middle, odd[0:48])):
                 row = 3 * pair + part
-                scale = blocks_ref[row // 12, row % 12 : row % 12 + 1, :]
-                served_ref[:, pl.ds(128 * row, 128)] = (tile * scale).astype(jnp.bfloat16)
+                columns = pl.ds(pl.multiple_of(1536 * step + 128 * row, 128), 128)
+                served_ref[:, columns] = (tile * blocks_ref[step, row : row + 1, :]).astype(jnp.bfloat16)
         store(step).start()
+        return carry
+
+    lax.fori_loop(0, 8, serve, 0)
     scale_ref[...] = blocks_ref[lax.axis_index("mp"), 0:12, :]
     peaks = jnp.max(blocks_ref[:, 12:16, :], axis=0)
     lane = lax.broadcasted_iota(jnp.int32, (1, 128), 1)
@@ -209,6 +229,7 @@
             out_shape=jax.ShapeDtypeStruct((16, 128), jnp.float32),
             in_specs=[SMEM_SPEC] + [VMEM_SPEC] * 4,
             out_specs=VMEM_SPEC,
+            scratch_shapes=[pltpu.VMEM((512, 128), jnp.float32)] * 2,
             compiler_params=params(),
         )(lengths, sums, acts, gain, bias)
         maxima = jnp.maximum(maxima, swap(maxima, "dp", 1))
@@ -222,6 +243,7 @@
             out_shape=jax.ShapeDtypeStruct((8, 16, 128), jnp.float32),
             in_specs=[VMEM_SPEC] * 5,
             out_specs=VMEM_SPEC,
+            scratch_shapes=[pltpu.VMEM((512, 128), jnp.float32)] * 2,
             compiler_params=params(),
         )(maxima, sums, acts, gain, bias)
         blocks = lax.all_to_all(page, "mp", 0, 0, tiled=True)

time: 88.2 us -> 89.5 us (1.015)
  Pallas kernels: 8.17 us -> 9.52 us
  transfers between devices with their start and end apart: 5 -> 5, of which waited for: 5 -> 5; matrix products, arithmetic and copies ran while one was open for 0% -> 0% of each run, Pallas kernels for 2% -> 3%
where the time goes in v12:
time: 89.5 us; the launch traced here: 88 us
  blocking collectives  33.4 us (37%)
  starting transfers between devices  30.9 us (35%)
  waiting for transfers between devices  13.2 us (15%)
  Pallas kernels  9.52 us (11%)
    all_to_all x1, blocking collectives, body(): lax.all_to_all(copies, 'dp', 0, 0, axis_index_groups=kinds, tiled=True)  18.2 us
    all_to_all x1, starting transfers between devices, body(): pages = lax.all_to_all(packed, 'dp', 0, 0, tiled=True)  15.6 us
    ppermute x4, starting transfers between devices, swap(): return lax.ppermute(x, axis, [(i, i ^ bit) for i in range(size)])  15.3 us
    all_to_all x1, blocking collectives, body(): blocks = lax.all_to_all(page, 'mp', 0, 0, tiled=True)  15.2 us
    ppermute x4, waiting for transfers between devices, swap(): return lax.ppermute(x, axis, [(i, i ^ bit) for i in range(size)])  10.2 us
    all_to_all x1, waiting for transfers between devices, body(): pages = lax.all_to_all(packed, 'dp', 0, 0, tiled=True)  2.98 us
    pallas_call x1, Pallas kernels, body(): pl.pallas_call(pack_kernel, out_shape=(jax.ShapeDtypeStruct((64, 72, 128)...  2.89 us
    pallas_call x1, Pallas kernels, body(): pl.pallas_call(serve_kernel, out_shape=(jax.ShapeDtypeStruct((48, D), jnp...  2.66 us
  transfers between devices with their start and end apart: 5, of which 5 were waited for; matrix products, arithmetic and copies ran while one was open for 0% of the time, Pallas kernels for 3%

profile of v12, /device:TPU:1, one launch (start us, length us, event | category | flops | bytes accessed | tf_op | source)
XLA Modules:
  0.0 88.0 jit_solution(16942059471361752941)
XLA Ops:
  0.6 2.9 %weight_exchange.1 = (bf16[64,72,128]{2,1,0:T(8,128)(2,1)}, bf16[192,128]{1,0:T(8,128)(2,1)}) custom-call(bf16[192,3072]{1,0:T(8,128)(2,1)} %w_hbm.1), custom_call_target="tpu_custom_call" | custom-call | tf_op jit(solution)/shard_map/weight_exchange/pallas_call | solution.py:194
  3.5 0.0 copy-start
  3.5 0.0 copy-start.1
  3.5 15.6 %all-to-all-start = ((bf16[64,72,128]{2,1,0:T(8,128)(2,1)}), bf16[64,72,128]{2,1,0:T(8,128)(2,1)S(1)}, u32[]{:S(2)}, u32[]{:S(2)}) async-start(bf16[64,72,128]{2,1,0:T(8,128)(2,1)} %get-tuple-element.11), calls=%async_computation | async-start | bytes 2359296 | tf_op jit(solution)/shard_map/weight_exchange/all_to_all | solution.py:212
  19.1 0.0 copy-start.2
  19.1 0.0 copy-start.3
  19.1 0.0 copy-start.4
  19.1 0.0 copy-done
  19.2 0.0 copy-done.1
  19.2 0.5 token_moments.1
  19.7 3.1 %collective-permute-start = (f32[16,128]{1,0:T(8,128)S(1)}, f32[16,128]{1,0:T(8,128)S(1)}, u32[]{:S(2)}, u32[]{:S(2)}) collective-permute-start(f32[16,128]{1,0:T(8,128)S(1)} %token_moments.1), channel_id=1, source_target_pairs={{0,1},{1,0},{2,3},{3,2},{4,5},{5,4},{6,7},{7,6},{8,9},{9,8},{10,11... | collective-permute-start | bytes 24584 | tf_op jit(solution)/shard_map/token_moments/ppermute | solution.py:187
  22.8 1.6 %collective-permute-done = f32[16,128]{1,0:T(8,128)S(1)} collective-permute-done((f32[16,128]{1,0:T(8,128)S(1)}, f32[16,128]{1,0:T(8,128)S(1)}, u32[]{:S(2)}, u32[]{:S(2)}) %collective-permute-start) | collective-permute-done | bytes 8224 | tf_op jit(solution)/shard_map/token_moments/ppermute | solution.py:187
  24.4 0.1 maximum_select_fusion.2
  24.4 4.6 %collective-permute-start.1 = (f32[16,128]{1,0:T(8,128)S(1)}, f32[16,128]{1,0:T(8,128)S(1)}, u32[]{:S(2)}, u32[]{:S(2)}) collective-permute-start(f32[16,128]{1,0:T(8,128)S(1)} %maximum_select_fusion.2), channel_id=1, source_target_pairs={{0,2},{1,3},{2,0},{3,1},{4,6},{5,7},{6,4},{7,5},{8,10},{9,11},{10,... | collective-permute-start | bytes 24584 | tf_op jit(solution)/shard_map/token_moments/ppermute | solution.py:187
  29.1 1.5 %collective-permute-done.1 = f32[16,128]{1,0:T(8,128)S(1)} collective-permute-done((f32[16,128]{1,0:T(8,128)S(1)}, f32[16,128]{1,0:T(8,128)S(1)}, u32[]{:S(2)}, u32[]{:S(2)}) %collective-permute-start.1) | collective-permute-done | bytes 8224 | tf_op jit(solution)/shard_map/token_moments/ppermute | solution.py:187
  30.6 0.1 maximum_select_fusion.1
  30.7 4.7 %collective-permute-start.2 = (f32[16,128]{1,0:T(8,128)S(1)}, f32[16,128]{1,0:T(8,128)S(1)}, u32[]{:S(2)}, u32[]{:S(2)}) collective-permute-start(f32[16,128]{1,0:T(8,128)S(1)} %maximum_select_fusion.1), channel_id=1, source_target_pairs={{0,4},{1,5},{2,6},{3,7},{4,0},{5,1},{6,2},{7,3},{8,12},{9,13},{10,... | collective-permute-start | bytes 24584 | tf_op jit(solution)/shard_map/token_moments/ppermute | solution.py:187
  35.4 6.3 %collective-permute-done.2 = f32[16,128]{1,0:T(8,128)S(1)} collective-permute-done((f32[16,128]{1,0:T(8,128)S(1)}, f32[16,128]{1,0:T(8,128)S(1)}, u32[]{:S(2)}, u32[]{:S(2)}) %collective-permute-start.2) | collective-permute-done | bytes 8224 | tf_op jit(solution)/shard_map/token_moments/ppermute | solution.py:187
  41.7 0.1 maximum_select_fusion.sums_ref
  41.8 0.0 copy-done.2
  41.8 0.0 copy-done.3
  41.8 0.0 copy-done.4
  41.8 2.1 %channel_maxima.1 = f32[16,128]{1,0:T(8,128)S(1)} custom-call(s32[2]{0:T(128)S(1)} %copy-done.4, f32[16,128]{1,0:T(8,128)S(1)} %maximum_select_fusion.sums_ref, bf16[512,1536]{1,0:T(8,128)(2,1)S(1)} %copy-done, f32[12,128]{1,0:T(8,128)S(1)} %bitcast.4, f32[12,128]{1,0:T(8,128)S(1)} %bitcast.6), custom_call_target="tpu_custom_call" | custom-call | tf_op jit(solution)/shard_map/channel_maxima/pallas_call | solution.py:227
  43.9 2.8 %collective-permute-start.3 = (f32[16,128]{1,0:T(8,128)S(1)}, f32[16,128]{1,0:T(8,128)S(1)}, u32[]{:S(2)}, u32[]{:S(2)}) collective-permute-start(f32[16,128]{1,0:T(8,128)S(1)} %channel_maxima.1), channel_id=1, source_target_pairs={{0,8},{8,0},{16,24},{24,16},{32,40},{40,32},{48,56},{56,48},{64,72... | collective-permute-start | bytes 24584 | tf_op jit(solution)/shard_map/channel_maxima/ppermute | solution.py:187
  46.8 0.8 collective-permute-done.3
  47.6 3.0 %all-to-all-done.pages_ref = bf16[64,72,128]{2,1,0:T(8,128)(2,1)S(1)} async-done(((bf16[64,72,128]{2,1,0:T(8,128)(2,1)}), bf16[64,72,128]{2,1,0:T(8,128)(2,1)S(1)}, u32[]{:S(2)}, u32[]{:S(2)}) %all-to-all-start) | async-done | bytes 1179680 | tf_op jit(solution)/shard_map/weight_exchange/all_to_all | solution.py:212
  50.6 18.2 %all_to_all.15.maxima_ref = f32[32,16,128]{2,1,0:T(8,128)S(1)} all-to-all(f32[32,16,128]{2,1,0:T(8,128)S(1)} %broadcast_in_dim.2), channel_id=1, replica_groups={{0,16,32,48,64,80,96,112,128,144,160,176,192,208,224,240,256,272,288,30..., dimensions={0} | all-to-all | bytes 524288 | tf_op jit(solution)/shard_map/channel_maxima/all_to_all | solution.py:239
  68.8 1.4 %token_peaks.1 = f32[8,16,128]{2,1,0:T(8,128)S(1)} custom-call(f32[32,16,128]{2,1,0:T(8,128)S(1)} %all_to_all.15.maxima_ref, f32[16,128]{1,0:T(8,128)S(1)} %maximum_select_fusion.sums_ref, bf16[512,1536]{1,0:T(8,128)(2,1)S(1)} %copy-done, f32[12,128]{1,0:T(8,128)S(1)} %bitcast.5, f32[12,128]{1,0:T(8,128)S(1)} %bitcast.7), custom_call_target="tpu_custom_call" | custom-call | tf_op jit(solution)/shard_map/token_peaks/pallas_call | solution.py:241
  70.2 15.2 %all_to_all.16.blocks_ref = f32[8,16,128]{2,1,0:T(8,128)S(1)} all-to-all(f32[8,16,128]{2,1,0:T(8,128)S(1)} %token_peaks.1), channel_id=1, replica_groups=mesh['dp'=64,'mp'=8] {'mp'}, dimensions={0} | all-to-all | bytes 131072 | tf_op jit(solution)/shard_map/token_peaks/all_to_all | solution.py:249
  85.4 2.7 %smoothed_weight.1 = (bf16[48,12288]{1,0:T(8,128)(2,1)}, f32[12,128]{1,0:T(8,128)}, f32[4,128]{1,0:T(4,128)}) custom-call(s32[2]{0:T(128)S(1)} %copy-done.4, f32[8,16,128]{2,1,0:T(8,128)S(1)} %all_to_all.16.blocks_ref, bf16[64,72,128]{2,1,0:T(8,128)(2,1)S(1)} %all-to-all-done.pages_ref), custom_call_target="tpu_custom_call" | custom-call | tf_op jit(solution)/shard_map/smoothed_weight/pallas_call | solution.py:251
  (3 shorter events, 0.0 us)
Async XLA Ops:
  3.5 15.6 %copy-start = (bf16[512,1536]{1,0:T(8,128)(2,1)S(1)}, bf16[512,1536]{1,0:T(8,128)(2,1)}, u32[]{:S(2)}) copy-start(bf16[512,1536]{1,0:T(8,128)(2,1)} %acts_ref.5) | copy-start | bytes 4718596
  3.5 15.6 %copy-start.1 = (bf16[192,128]{1,0:T(8,128)(2,1)S(1)}, bf16[192,128]{1,0:T(8,128)(2,1)}, u32[]{:S(2)}) copy-start(bf16[192,128]{1,0:T(8,128)(2,1)} %get-tuple-element.10.peak_ref) | copy-start | bytes 147460
  3.5 47.0 %all-to-all-start = ((bf16[64,72,128]{2,1,0:T(8,128)(2,1)}), bf16[64,72,128]{2,1,0:T(8,128)(2,1)S(1)}, u32[]{:S(2)}, u32[]{:S(2)}) async-start(bf16[64,72,128]{2,1,0:T(8,128)(2,1)} %get-tuple-element.11), calls=%async_computation | async-start | bytes 2359296 | tf_op jit(solution)/shard_map/weight_exchange/all_to_all | solution.py:212
  19.1 22.7 %copy-start.2 = (f32[1536]{0:T(1024)S(1)}, f32[1536]{0:T(1024)}, u32[]{:S(2)}) copy-start(f32[1536]{0:T(1024)} %param.7) | copy-start | bytes 18436
  19.1 22.7 %copy-start.3 = (f32[1536]{0:T(1024)S(1)}, f32[1536]{0:T(1024)}, u32[]{:S(2)}) copy-start(f32[1536]{0:T(1024)} %param.8) | copy-start | bytes 18436
  19.1 22.7 %copy-start.4 = (s32[2]{0:T(128)S(1)}, s32[2]{0:T(128)}, u32[]{:S(2)}) copy-start(s32[2]{0:T(128)} %lengths_ref.3) | copy-start | bytes 28
  19.7 4.7 %collective-permute-start = (f32[16,128]{1,0:T(8,128)S(1)}, f32[16,128]{1,0:T(8,128)S(1)}, u32[]{:S(2)}, u32[]{:S(2)}) collective-permute-start(f32[16,128]{1,0:T(8,128)S(1)} %token_moments.1), channel_id=1, source_target_pairs={{0,1},{1,0},{2,3},{3,2},{4,5},{5,4},{6,7},{7,6},{8,9},{9,8},{10,11... | collective-permute-start | bytes 24584 | tf_op jit(solution)/shard_map/token_moments/ppermute | solution.py:187
  24.4 6.2 %collective-permute-start.1 = (f32[16,128]{1,0:T(8,128)S(1)}, f32[16,128]{1,0:T(8,128)S(1)}, u32[]{:S(2)}, u32[]{:S(2)}) collective-permute-start(f32[16,128]{1,0:T(8,128)S(1)} %maximum_select_fusion.2), channel_id=1, source_target_pairs={{0,2},{1,3},{2,0},{3,1},{4,6},{5,7},{6,4},{7,5},{8,10},{9,11},{10,... | collective-permute-start | bytes 24584 | tf_op jit(solution)/shard_map/token_moments/ppermute | solution.py:187
  30.7 11.1 %collective-permute-start.2 = (f32[16,128]{1,0:T(8,128)S(1)}, f32[16,128]{1,0:T(8,128)S(1)}, u32[]{:S(2)}, u32[]{:S(2)}) collective-permute-start(f32[16,128]{1,0:T(8,128)S(1)} %maximum_select_fusion.1), channel_id=1, source_target_pairs={{0,4},{1,5},{2,6},{3,7},{4,0},{5,1},{6,2},{7,3},{8,12},{9,13},{10,... | collective-permute-start | bytes 24584 | tf_op jit(solution)/shard_map/token_moments/ppermute | solution.py:187
  43.9 3.6 %collective-permute-start.3 = (f32[16,128]{1,0:T(8,128)S(1)}, f32[16,128]{1,0:T(8,128)S(1)}, u32[]{:S(2)}, u32[]{:S(2)}) collective-permute-start(f32[16,128]{1,0:T(8,128)S(1)} %channel_maxima.1), channel_id=1, source_target_pairs={{0,8},{8,0},{16,24},{24,16},{32,40},{40,32},{48,56},{56,48},{64,72... | collective-permute-start | bytes 24584 | tf_op jit(solution)/shard_map/channel_maxima/ppermute | solution.py:187

commit v13 on v10

--- a/solution.py
+++ b/solution.py
@@ -50,7 +50,7 @@
         store(step).start()
         return peak
 
-    peak_ref[...] = lax.fori_loop(0, 8, pack, jnp.zeros((192, 128), jnp.bfloat16))
+    peak_ref[...] = lax.fori_loop(0, 8, pack, jnp.zeros((192, 128), jnp.bfloat16), unroll=True)
     peak_copy = pltpu.make_async_copy(peak_ref, peak_hbm, peak_sem)
     peak_copy.start()
     for step in range(8):
@@ -133,13 +133,23 @@
         page_ref[peer] = page
 
 
-def serve_kernel(lengths_ref, blocks_ref, pages_ref, served_hbm, scale_ref, tok_ref, served_ref, sems):
+def serve_kernel(lengths_ref, blocks_ref, pages_ref, served_hbm, scale_hbm, tok_hbm, served_ref, scale_ref, tok_ref, sems, scale_sem, tok_sem):
     low = lax.broadcasted_iota(jnp.int32, (24, 128), 1) < 64
 
     def store(step):
         columns = pl.ds(1536 * step, 1536)
         return pltpu.make_async_copy(served_ref.at[:, columns], served_hbm.at[:, columns], sems.at[step])
 
+    scale_ref[...] = blocks_ref[lax.axis_index("mp"), 0:12, :]
+    peaks = jnp.max(blocks_ref[:, 12:16, :], axis=0)
+    lane = lax.broadcasted_iota(jnp.int32, (1, 128), 1)
+    for block in range(4):
+        valid = lane + 128 * (block % 2) < lengths_ref[block // 2]
+        tok_ref[block : block + 1, :] = jnp.where(valid, peaks[block : block + 1], 0.0)
+    scale_copy = pltpu.make_async_copy(scale_ref, scale_hbm, scale_sem)
+    tok_copy = pltpu.make_async_copy(tok_ref, tok_hbm, tok_sem)
+    scale_copy.start()
+    tok_copy.start()
     for step in range(8):
         for pair in range(4 * step, 4 * step + 4):
             even = pages_ref[2 * pair].astype(jnp.float32)
@@ -152,14 +162,10 @@
                 scale = blocks_ref[row // 12, row % 12 : row % 12 + 1, :]
                 served_ref[:, pl.ds(128 * row, 128)] = (tile * scale).astype(jnp.bfloat16)
         store(step).start()
-    scale_ref[...] = blocks_ref[lax.axis_index("mp"), 0:12, :]
-    peaks = jnp.max(blocks_ref[:, 12:16, :], axis=0)
-    lane = lax.broadcasted_iota(jnp.int32, (1, 128), 1)
-    for block in range(4):
-        valid = lane + 128 * (block % 2) < lengths_ref[block // 2]
-        tok_ref[block : block + 1, :] = jnp.where(valid, peaks[block : block + 1], 0.0)
     for step in range(8):
         store(step).wait()
+    scale_copy.wait()
+    tok_copy.wait()
 
 
 def swap(x, axis, bit):
@@ -234,8 +240,15 @@
                 jax.ShapeDtypeStruct((4, 128), jnp.float32),
             ),
             in_specs=[SMEM_SPEC, VMEM_SPEC, VMEM_SPEC],
-            out_specs=(ANY_SPEC, VMEM_SPEC, VMEM_SPEC),
-            scratch_shapes=[pltpu.VMEM((48, D), jnp.bfloat16), pltpu.SemaphoreType.DMA((8,))],
+            out_specs=(ANY_SPEC,) * 3,
+            scratch_shapes=[
+                pltpu.VMEM((48, D), jnp.bfloat16),
+                pltpu.VMEM((12, 128), jnp.float32),
+                pltpu.VMEM((4, 128), jnp.float32),
+                pltpu.SemaphoreType.DMA((8,)),
+                pltpu.SemaphoreType.DMA,
+                pltpu.SemaphoreType.DMA,
+            ],
             compiler_params=params(),
         )(lengths, blocks, pages)
     return served, scale.reshape(1536), tok.reshape(512)

time: 88.2 us -> 87.5 us (level)
  no operation moved by 1% of the time
where the time goes in v13:
time: 87.5 us; the launch traced here: 86 us
  blocking collectives  32.8 us (37%)
  starting transfers between devices  30.9 us (35%)
  waiting for transfers between devices  13.8 us (16%)
  Pallas kernels  7.52 us (9%)
    all_to_all x1, blocking collectives, body(): lax.all_to_all(copies, 'dp', 0, 0, axis_index_groups=kinds, tiled=True)  17.6 us
    all_to_all x1, starting transfers between devices, body(): pages = lax.all_to_all(packed, 'dp', 0, 0, tiled=True)  15.6 us
    ppermute x4, starting transfers between devices, swap(): return lax.ppermute(x, axis, [(i, i ^ bit) for i in range(size)])  15.3 us
    all_to_all x1, blocking collectives, body(): blocks = lax.all_to_all(page, 'mp', 0, 0, tiled=True)  15.2 us
    ppermute x4, waiting for transfers between devices, swap(): return lax.ppermute(x, axis, [(i, i ^ bit) for i in range(size)])  10.2 us
    all_to_all x1, waiting for transfers between devices, body(): pages = lax.all_to_all(packed, 'dp', 0, 0, tiled=True)  3.58 us
    pallas_call x1, Pallas kernels, body(): pl.pallas_call(pack_kernel, out_shape=(jax.ShapeDtypeStruct((64, 72, 128)...  2.81 us
    pallas_call x1, Pallas kernels, body(): pl.pallas_call(serve_kernel, out_shape=(jax.ShapeDtypeStruct((48, D), jnp...  1.78 us
  transfers between devices with their start and end apart: 5, of which 5 were waited for; matrix products, arithmetic and copies ran while one was open for 0% of the time, Pallas kernels for 2%

profile of v13, /device:TPU:1, one launch (start us, length us, event | category | flops | bytes accessed | tf_op | source)
XLA Modules:
  0.0 86.0 jit_solution(3228973397941674692)
XLA Ops:
  0.6 2.8 %weight_exchange.1 = (bf16[64,72,128]{2,1,0:T(8,128)(2,1)}, bf16[192,128]{1,0:T(8,128)(2,1)}) custom-call(bf16[192,3072]{1,0:T(8,128)(2,1)} %w_hbm.1), custom_call_target="tpu_custom_call" | custom-call | tf_op jit(solution)/shard_map/weight_exchange/pallas_call | solution.py:180
  3.5 0.0 copy-start
  3.5 0.0 copy-start.1
  3.5 15.6 %all-to-all-start = ((bf16[64,72,128]{2,1,0:T(8,128)(2,1)}), bf16[64,72,128]{2,1,0:T(8,128)(2,1)S(1)}, u32[]{:S(2)}, u32[]{:S(2)}) async-start(bf16[64,72,128]{2,1,0:T(8,128)(2,1)} %get-tuple-element.11), calls=%async_computation | async-start | bytes 2359296 | tf_op jit(solution)/shard_map/weight_exchange/all_to_all | solution.py:198
  19.0 0.0 copy-start.2
  19.1 0.0 copy-start.3
  19.1 0.0 copy-start.4
  19.1 0.0 copy-done
  19.1 0.0 copy-done.1
  19.1 0.5 token_moments.1
  19.6 3.1 %collective-permute-start = (f32[16,128]{1,0:T(8,128)S(1)}, f32[16,128]{1,0:T(8,128)S(1)}, u32[]{:S(2)}, u32[]{:S(2)}) collective-permute-start(f32[16,128]{1,0:T(8,128)S(1)} %token_moments.1), channel_id=1, source_target_pairs={{0,1},{1,0},{2,3},{3,2},{4,5},{5,4},{6,7},{7,6},{8,9},{9,8},{10,11... | collective-permute-start | bytes 24584 | tf_op jit(solution)/shard_map/token_moments/ppermute | solution.py:173
  22.7 1.6 %collective-permute-done = f32[16,128]{1,0:T(8,128)S(1)} collective-permute-done((f32[16,128]{1,0:T(8,128)S(1)}, f32[16,128]{1,0:T(8,128)S(1)}, u32[]{:S(2)}, u32[]{:S(2)}) %collective-permute-start) | collective-permute-done | bytes 8224 | tf_op jit(solution)/shard_map/token_moments/ppermute | solution.py:173
  24.3 0.1 maximum_select_fusion.2
  24.4 4.6 %collective-permute-start.1 = (f32[16,128]{1,0:T(8,128)S(1)}, f32[16,128]{1,0:T(8,128)S(1)}, u32[]{:S(2)}, u32[]{:S(2)}) collective-permute-start(f32[16,128]{1,0:T(8,128)S(1)} %maximum_select_fusion.2), channel_id=1, source_target_pairs={{0,2},{1,3},{2,0},{3,1},{4,6},{5,7},{6,4},{7,5},{8,10},{9,11},{10,... | collective-permute-start | bytes 24584 | tf_op jit(solution)/shard_map/token_moments/ppermute | solution.py:173
  29.0 1.5 %collective-permute-done.1 = f32[16,128]{1,0:T(8,128)S(1)} collective-permute-done((f32[16,128]{1,0:T(8,128)S(1)}, f32[16,128]{1,0:T(8,128)S(1)}, u32[]{:S(2)}, u32[]{:S(2)}) %collective-permute-start.1) | collective-permute-done | bytes 8224 | tf_op jit(solution)/shard_map/token_moments/ppermute | solution.py:173
  30.5 0.1 maximum_select_fusion.1
  30.6 4.7 %collective-permute-start.2 = (f32[16,128]{1,0:T(8,128)S(1)}, f32[16,128]{1,0:T(8,128)S(1)}, u32[]{:S(2)}, u32[]{:S(2)}) collective-permute-start(f32[16,128]{1,0:T(8,128)S(1)} %maximum_select_fusion.1), channel_id=1, source_target_pairs={{0,4},{1,5},{2,6},{3,7},{4,0},{5,1},{6,2},{7,3},{8,12},{9,13},{10,... | collective-permute-start | bytes 24584 | tf_op jit(solution)/shard_map/token_moments/ppermute | solution.py:173
  35.4 6.3 %collective-permute-done.2 = f32[16,128]{1,0:T(8,128)S(1)} collective-permute-done((f32[16,128]{1,0:T(8,128)S(1)}, f32[16,128]{1,0:T(8,128)S(1)}, u32[]{:S(2)}, u32[]{:S(2)}) %collective-permute-start.2) | collective-permute-done | bytes 8224 | tf_op jit(solution)/shard_map/token_moments/ppermute | solution.py:173
  41.7 0.1 maximum_select_fusion.sums_ref
  41.7 0.0 copy-done.2
  41.7 0.0 copy-done.3
  41.7 0.0 copy-done.4
  41.8 1.5 %channel_maxima.1 = f32[16,128]{1,0:T(8,128)S(1)} custom-call(s32[2]{0:T(128)S(1)} %copy-done.4, f32[16,128]{1,0:T(8,128)S(1)} %maximum_select_fusion.sums_ref, bf16[512,1536]{1,0:T(8,128)(2,1)S(1)} %copy-done, f32[12,128]{1,0:T(8,128)S(1)} %bitcast.4, f32[12,128]{1,0:T(8,128)S(1)} %bitcast.6), custom_call_target="tpu_custom_call" | custom-call | tf_op jit(solution)/shard_map/channel_maxima/pallas_call | solution.py:213
  43.2 2.8 %collective-permute-start.3 = (f32[16,128]{1,0:T(8,128)S(1)}, f32[16,128]{1,0:T(8,128)S(1)}, u32[]{:S(2)}, u32[]{:S(2)}) collective-permute-start(f32[16,128]{1,0:T(8,128)S(1)} %channel_maxima.1), channel_id=1, source_target_pairs={{0,8},{8,0},{16,24},{24,16},{32,40},{40,32},{48,56},{56,48},{64,72... | collective-permute-start | bytes 24584 | tf_op jit(solution)/shard_map/channel_maxima/ppermute | solution.py:173
  46.1 0.8 collective-permute-done.3
  46.9 3.6 %all-to-all-done.pages_ref = bf16[64,72,128]{2,1,0:T(8,128)(2,1)S(1)} async-done(((bf16[64,72,128]{2,1,0:T(8,128)(2,1)}), bf16[64,72,128]{2,1,0:T(8,128)(2,1)S(1)}, u32[]{:S(2)}, u32[]{:S(2)}) %all-to-all-start) | async-done | bytes 1179680 | tf_op jit(solution)/shard_map/weight_exchange/all_to_all | solution.py:198
  50.5 17.6 %all_to_all.15.maxima_ref = f32[32,16,128]{2,1,0:T(8,128)S(1)} all-to-all(f32[32,16,128]{2,1,0:T(8,128)S(1)} %broadcast_in_dim.2), channel_id=1, replica_groups={{0,16,32,48,64,80,96,112,128,144,160,176,192,208,224,240,256,272,288,30..., dimensions={0} | all-to-all | bytes 524288 | tf_op jit(solution)/shard_map/channel_maxima/all_to_all | solution.py:224
  68.1 0.9 %token_peaks.1 = f32[8,16,128]{2,1,0:T(8,128)S(1)} custom-call(f32[32,16,128]{2,1,0:T(8,128)S(1)} %all_to_all.15.maxima_ref, f32[16,128]{1,0:T(8,128)S(1)} %maximum_select_fusion.sums_ref, bf16[512,1536]{1,0:T(8,128)(2,1)S(1)} %copy-done, f32[12,128]{1,0:T(8,128)S(1)} %bitcast.5, f32[12,128]{1,0:T(8,128)S(1)} %bitcast.7), custom_call_target="tpu_custom_call" | custom-call | tf_op jit(solution)/shard_map/token_peaks/pallas_call | solution.py:226
  69.1 15.2 %all_to_all.16.blocks_ref = f32[8,16,128]{2,1,0:T(8,128)S(1)} all-to-all(f32[8,16,128]{2,1,0:T(8,128)S(1)} %token_peaks.1), channel_id=1, replica_groups=mesh['dp'=64,'mp'=8] {'mp'}, dimensions={0} | all-to-all | bytes 131072 | tf_op jit(solution)/shard_map/token_peaks/all_to_all | solution.py:233
  84.2 1.8 %smoothed_weight.1 = (bf16[48,12288]{1,0:T(8,128)(2,1)}, f32[12,128]{1,0:T(8,128)}, f32[4,128]{1,0:T(4,128)}) custom-call(s32[2]{0:T(128)S(1)} %copy-done.4, f32[8,16,128]{2,1,0:T(8,128)S(1)} %all_to_all.16.blocks_ref, bf16[64,72,128]{2,1,0:T(8,128)(2,1)S(1)} %all-to-all-done.pages_ref), custom_call_target="tpu_custom_call" | custom-call | tf_op jit(solution)/shard_map/smoothed_weight/pallas_call | solution.py:235
  (3 shorter events, 0.0 us)
Async XLA Ops:
  3.5 15.6 %copy-start = (bf16[512,1536]{1,0:T(8,128)(2,1)S(1)}, bf16[512,1536]{1,0:T(8,128)(2,1)}, u32[]{:S(2)}) copy-start(bf16[512,1536]{1,0:T(8,128)(2,1)} %acts_ref.5) | copy-start | bytes 4718596
  3.5 15.6 %copy-start.1 = (bf16[192,128]{1,0:T(8,128)(2,1)S(1)}, bf16[192,128]{1,0:T(8,128)(2,1)}, u32[]{:S(2)}) copy-start(bf16[192,128]{1,0:T(8,128)(2,1)} %get-tuple-element.10.peak_ref) | copy-start | bytes 147460
  3.5 47.0 %all-to-all-start = ((bf16[64,72,128]{2,1,0:T(8,128)(2,1)}), bf16[64,72,128]{2,1,0:T(8,128)(2,1)S(1)}, u32[]{:S(2)}, u32[]{:S(2)}) async-start(bf16[64,72,128]{2,1,0:T(8,128)(2,1)} %get-tuple-element.11), calls=%async_computation | async-start | bytes 2359296 | tf_op jit(solution)/shard_map/weight_exchange/all_to_all | solution.py:198
  19.0 22.7 %copy-start.2 = (f32[1536]{0:T(1024)S(1)}, f32[1536]{0:T(1024)}, u32[]{:S(2)}) copy-start(f32[1536]{0:T(1024)} %param.7) | copy-start | bytes 18436
  19.1 22.7 %copy-start.3 = (f32[1536]{0:T(1024)S(1)}, f32[1536]{0:T(1024)}, u32[]{:S(2)}) copy-start(f32[1536]{0:T(1024)} %param.8) | copy-start | bytes 18436
  19.1 22.7 %copy-start.4 = (s32[2]{0:T(128)S(1)}, s32[2]{0:T(128)}, u32[]{:S(2)}) copy-start(s32[2]{0:T(128)} %lengths_ref.3) | copy-start | bytes 28
  19.6 4.7 %collective-permute-start = (f32[16,128]{1,0:T(8,128)S(1)}, f32[16,128]{1,0:T(8,128)S(1)}, u32[]{:S(2)}, u32[]{:S(2)}) collective-permute-start(f32[16,128]{1,0:T(8,128)S(1)} %token_moments.1), channel_id=1, source_target_pairs={{0,1},{1,0},{2,3},{3,2},{4,5},{5,4},{6,7},{7,6},{8,9},{9,8},{10,11... | collective-permute-start | bytes 24584 | tf_op jit(solution)/shard_map/token_moments/ppermute | solution.py:173
  24.4 6.2 %collective-permute-start.1 = (f32[16,128]{1,0:T(8,128)S(1)}, f32[16,128]{1,0:T(8,128)S(1)}, u32[]{:S(2)}, u32[]{:S(2)}) collective-permute-start(f32[16,128]{1,0:T(8,128)S(1)} %maximum_select_fusion.2), channel_id=1, source_target_pairs={{0,2},{1,3},{2,0},{3,1},{4,6},{5,7},{6,4},{7,5},{8,10},{9,11},{10,... | collective-permute-start | bytes 24584 | tf_op jit(solution)/shard_map/token_moments/ppermute | solution.py:173
  30.6 11.1 %collective-permute-start.2 = (f32[16,128]{1,0:T(8,128)S(1)}, f32[16,128]{1,0:T(8,128)S(1)}, u32[]{:S(2)}, u32[]{:S(2)}) collective-permute-start(f32[16,128]{1,0:T(8,128)S(1)} %maximum_select_fusion.1), channel_id=1, source_target_pairs={{0,4},{1,5},{2,6},{3,7},{4,0},{5,1},{6,2},{7,3},{8,12},{9,13},{10,... | collective-permute-start | bytes 24584 | tf_op jit(solution)/shard_map/token_moments/ppermute | solution.py:173
  43.2 3.6 %collective-permute-start.3 = (f32[16,128]{1,0:T(8,128)S(1)}, f32[16,128]{1,0:T(8,128)S(1)}, u32[]{:S(2)}, u32[]{:S(2)}) collective-permute-start(f32[16,128]{1,0:T(8,128)S(1)} %channel_maxima.1), channel_id=1, source_target_pairs={{0,8},{8,0},{16,24},{24,16},{32,40},{40,32},{48,56},{56,48},{64,72... | collective-permute-start | bytes 24584 | tf_op jit(solution)/shard_map/channel_maxima/ppermute | solution.py:173
